TPU v7x, 512 devices: a whole 4x4x16 slice. The times are simulated.
512 devices in a mesh: section: 8 (over z_hi, core), peer: 64 (over y, z_lo, x).
Axes of the slice: x: 4, y: 4, z: 16 (z_hi: 4, z_lo: 4; z = z_hi * 4 + z_lo), core: 2. Of those that a mesh axis runs over, the one named last changes fastest.
Arguments:
- hidden_in: bfloat16 [8, 8192, 5120], P('section', 'peer'), may hold values from -6 to 6
- out_grad: bfloat16 [8, 8192, 5120], P('section', 'peer'), may hold values from -16 to 16
- gain: float32 [8, 5120], P('section'), may hold values from 0.5 to 1.5
- w_down: bfloat16 [8, 64, 5120], P('section'), may hold values from -0.078125 to 0.078125
- w_up: bfloat16 [8, 64, 5120], P('section'), may hold values from -0.75 to 0.75
- matching: int32 [8, 64], P('section'), may hold values from 0 to 63, each once within a row
Outputs:
- act_out: bfloat16 [8, 8192, 5120], P('section', 'peer')
- grad_down: float32 [8, 64, 5120], P('section', None, 'peer')
- grad_up: float32 [8, 64, 5120], P('section', None, 'peer')
- grad_gain: float32 [8, 5120], P('section', 'peer')
Inputs may be any that keep to these rules, and one draw needn't show every extreme that they name: Every row of matching is a permutation of the 64 peers.
All inputs are finite; a program needn't handle non-finite values.
Results may differ from a plain program's by a relative error of at most 0.0053.
Values may be sent and summed in bfloat16 or wider, within the bound.
No kernel may reach another device: no remote copies, remote signals or barrier semaphores. Data moves between devices by JAX's collectives and lax.ppermute only.
A program may use at most 64 MiB of HBM per device.

v0:
```python
import jax
import jax.numpy as jnp
from jax import lax
from jax.sharding import PartitionSpec as P


def passed_along(value, axis, steps):
    count = lax.axis_size(axis)
    pairs = [(source, (source + steps) % count) for source in range(count)]
    return lax.ppermute(value, axis, pairs)


def inverse_of(sources):
    counting = jnp.arange(sources.shape[0], dtype=jnp.int32)
    return jnp.zeros_like(sources).at[sources].set(counting)


def regroup(payload, sources):
    peer_count = sources.shape[0]
    spread = lax.all_to_all(payload, "peer", split_axis=0, concat_axis=0, tiled=True)
    blocks = spread.reshape(peer_count, payload.shape[0] // peer_count, payload.shape[1])
    picked = jnp.take(blocks, sources, axis=0).reshape(payload.shape)
    return lax.all_to_all(picked, "peer", split_axis=0, concat_axis=0, tiled=True)


def on_device(hidden_in, out_grad, gain, w_down, w_up, matching):
    tokens = hidden_in[0]
    held_grad = out_grad[0]
    gain_row = gain[0]
    down_rows = w_down[0]
    up_rows = w_up[0]
    match_row = matching[0]
    tokens_f = tokens.astype(jnp.float32)
    inv_rms = lax.rsqrt(jnp.mean(tokens_f * tokens_f, axis=-1, keepdims=True) + 1e-05)
    normed = (tokens_f * inv_rms * gain_row).astype(jnp.bfloat16)
    preact = jnp.dot(normed, down_rows.T, preferred_element_type=jnp.float32)
    active = jax.nn.silu(preact).astype(jnp.bfloat16)
    result = (tokens_f + jnp.dot(active, up_rows, preferred_element_type=jnp.float32)).astype(
        jnp.bfloat16
    )
    arrived = regroup(result, inverse_of(match_row))
    moved_out = passed_along(arrived, "section", 1)
    lowered = passed_along(held_grad, "section", -1)
    cotangent = regroup(lowered, match_row)
    up_grad = jnp.dot(active.T, cotangent, preferred_element_type=jnp.float32)
    act_grad = jnp.dot(cotangent, up_rows.T, preferred_element_type=jnp.float32)
    sigmoid_pre = jax.nn.sigmoid(preact)
    pre_grad = (act_grad * sigmoid_pre * (1.0 + preact * (1.0 - sigmoid_pre))).astype(jnp.bfloat16)
    down_grad = jnp.dot(pre_grad.T, normed, preferred_element_type=jnp.float32)
    normed_grad = jnp.dot(pre_grad, down_rows, preferred_element_type=jnp.float32)
    gain_grad = jnp.sum(normed_grad * tokens_f * inv_rms, axis=0, keepdims=True)
    summed_down, summed_up, summed_gain = lax.psum((down_grad, up_grad, gain_grad), "peer")
    slice_width = summed_down.shape[1] // lax.axis_size("peer")
    offset = lax.axis_index("peer") * slice_width
    summed_down = lax.dynamic_slice_in_dim(summed_down, offset, slice_width, 1)
    summed_up = lax.dynamic_slice_in_dim(summed_up, offset, slice_width, 1)
    summed_gain = lax.dynamic_slice_in_dim(summed_gain, offset, slice_width, 1)
    return (moved_out[None], summed_down[None], summed_up[None], summed_gain)


def solution(mesh):
    placed = (
        P("section", "peer", None),
        P("section", "peer", None),
        P("section", None),
        P("section", None, None),
        P("section", None, None),
        P("section", None),
    )
    return jax.shard_map(
        on_device,
        mesh=mesh,
        in_specs=placed,
        out_specs=(
            P("section", "peer", None),
            P("section", None, "peer"),
            P("section", None, "peer"),
            P("section", "peer"),
        ),
        check_vma=False,
    )
```

profile of v0, /device:TPU:128, one launch (start us, length us, event | category | flops | bytes accessed | tf_op | source)
XLA Modules:
  0.0 964.9 jit_solution(15583655212376485348)
XLA Ops:
  7.2 2.1 collective-permute-start.1
  9.2 57.6 %collective-permute-done.1 = bf16[128,5120]{1,0:T(8,128)(2,1)S(1)} collective-permute-done((bf16[128,5120]{1,0:T(8,128)(2,1)}, bf16[128,5120]{1,0:T(8,128)(2,1)S(1)}, u32[]{:S(2)}, u32[]{:S(2)}) %collective-permute-start.1) | collective-permute-done | bytes 1310752 | tf_op jit(solution)/shard_map/ppermute | solution.py:10
  66.9 1.3 all_to_all.28
  68.2 8.3 all-to-all-start.2
  77.6 0.7 fusion.11
  78.3 0.5 fusion.1
  78.9 1.4 all_to_all.24
  80.2 29.2 %all-to-all-done.2 = bf16[64,2,5120]{2,1,0:T(2,128)(2,1)} async-done(((bf16[64,2,5120]{2,1,0:T(2,128)(2,1)}), bf16[64,2,5120]{2,1,0:T(2,128)(2,1)}, u32[]{:S(2)}, u32[]{:S(2)}) %all-to-all-start.2) | async-done | bytes 1310752 | tf_op jit(solution)/shard_map/all_to_all | solution.py:20
  109.4 6.5 all-to-all-start
  115.9 5.5 gather_fusion.1
  121.4 3.6 broadcast_select_fusion
  125.1 26.4 %all-to-all-done = bf16[64,2,5120]{2,1,0:T(2,128)(2,1)S(1)} async-done(((bf16[64,2,5120]{2,1,0:T(2,128)(2,1)}), bf16[64,2,5120]{2,1,0:T(2,128)(2,1)S(1)}, u32[]{:S(2)}, u32[]{:S(2)}) %all-to-all-start) | async-done | bytes 1310752 | tf_op jit(solution)/shard_map/all_to_all | solution.py:20
  151.4 6.0 all-to-all-start.3
  157.4 1.0 scatter_custom_fusion
  158.4 4.2 gather_fusion
  162.6 3.6 broadcast_select_fusion.1
  166.2 26.3 %all-to-all-done.3 = bf16[64,2,5120]{2,1,0:T(2,128)(2,1)} async-done(((bf16[64,2,5120]{2,1,0:T(2,128)(2,1)}), bf16[64,2,5120]{2,1,0:T(2,128)(2,1)}, u32[]{:S(2)}, u32[]{:S(2)}) %all-to-all-start.3) | async-done | bytes 1310752 | tf_op jit(solution)/shard_map/all_to_all | solution.py:23
  192.6 5.5 all-to-all-start.1
  198.1 3.1 all_to_all.31
  201.2 0.6 fusion.20
  201.8 1.4 fusion.28
  203.3 1.6 fusion.13
  204.9 27.4 %all-to-all-done.1 = bf16[64,2,5120]{2,1,0:T(2,128)(2,1)} async-done(((bf16[64,2,5120]{2,1,0:T(2,128)(2,1)}), bf16[64,2,5120]{2,1,0:T(2,128)(2,1)}, u32[]{:S(2)}, u32[]{:S(2)}) %all-to-all-start.1) | async-done | bytes 1310752 | tf_op jit(solution)/shard_map/all_to_all | solution.py:23
  232.4 4.0 all_to_all.27
  236.3 1.9 collective-permute-start
  238.2 52.0 %collective-permute-done = bf16[128,5120]{1,0:T(8,128)(2,1)S(1)} collective-permute-done((bf16[128,5120]{1,0:T(8,128)(2,1)}, bf16[128,5120]{1,0:T(8,128)(2,1)S(1)}, u32[]{:S(2)}, u32[]{:S(2)}) %collective-permute-start) | collective-permute-done | bytes 1310752 | tf_op jit(solution)/shard_map/ppermute | solution.py:10
  290.2 1.7 fusion.9
  291.9 367.6 %psum.23 = f32[1,5120]{1,0:T(1,128)S(1)} all-reduce(f32[1,5120]{1,0:T(1,128)S(1)} %bitcast.55), channel_id=1, replica_groups=mesh['section'=8,'peer'=64] {'peer'}, use_global_device_ids=true, to_apply=%region_5.7 | all-reduce | flops 5120 | bytes 40960 | tf_op jit(solution)/shard_map/psum | solution.py:52
  659.5 0.6 constant_dynamic-slice_fusion
  660.1 295.3 %all-reduce.3.cloned.1.call-done = (f32[64,5120]{1,0:T(8,128)}, f32[64,5120]{1,0:T(8,128)}) async-done(((f32[64,5120]{1,0:T(8,128)}, f32[64,5120]{1,0:T(8,128)}), (f32[64,5120]{1,0:T(8,128)}, f32[64,5120]{1,0:T(8,128)})) %all-reduce.3.cloned.1.call-update) | async-done | bytes 2621456 | tf_op jit(solution)/shard_map/psum | solution.py:52
  955.4 1.6 dynamic-slice_bitcast_fusion
  957.0 1.1 copy.13
  (22 shorter events, 1.2 us)
Async XLA Ops:
  7.2 71.1 %copy-start = (bf16[1,64,5120]{2,1,0:T(8,128)(2,1)S(1)}, bf16[1,64,5120]{2,1,0:T(8,128)(2,1)}, u32[]{:S(2)}) copy-start(bf16[1,64,5120]{2,1,0:T(8,128)(2,1)} %param.12) | copy-start | bytes 1966084
  7.2 59.7 %collective-permute-start.1 = (bf16[128,5120]{1,0:T(8,128)(2,1)}, bf16[128,5120]{1,0:T(8,128)(2,1)S(1)}, u32[]{:S(2)}, u32[]{:S(2)}) collective-permute-start(bf16[128,5120]{1,0:T(8,128)(2,1)} %bitcast.56), channel_id=1, source_target_pairs={{0,448},{64,0},{128,64},{192,128},{256,192},{320,256},{384,320},{4... | collective-permute-start | bytes 3932168 | tf_op jit(solution)/shard_map/ppermute | solution.py:10
  68.2 8.3 copy-start.1
  68.2 41.2 %all-to-all-start.2 = ((bf16[64,2,5120]{2,1,0:T(2,128)(2,1)}), bf16[64,2,5120]{2,1,0:T(2,128)(2,1)}, u32[]{:S(2)}, u32[]{:S(2)}) async-start(bf16[64,2,5120]{2,1,0:T(2,128)(2,1)} %all_to_all.28), calls=%async_computation.2 | async-start | bytes 2621440 | tf_op jit(solution)/shard_map/all_to_all | solution.py:20
  76.5 0.7 copy-start.2
  76.5 1.1 copy-start.3
  80.2 35.7 %copy-start.4 = (s32[1,64]{1,0:T(1,128)S(1)}, s32[1,64]{1,0:T(1,128)}, u32[]{:S(2)}) copy-start(s32[1,64]{1,0:T(1,128)} %param.13) | copy-start | bytes 772
  109.4 42.0 %all-to-all-start = ((bf16[64,2,5120]{2,1,0:T(2,128)(2,1)}), bf16[64,2,5120]{2,1,0:T(2,128)(2,1)S(1)}, u32[]{:S(2)}, u32[]{:S(2)}) async-start(bf16[64,2,5120]{2,1,0:T(2,128)(2,1)} %all_to_all.24), calls=%async_computation | async-start | bytes 2621440 | tf_op jit(solution)/shard_map/all_to_all | solution.py:20
  151.4 41.1 %all-to-all-start.3 = ((bf16[64,2,5120]{2,1,0:T(2,128)(2,1)}), bf16[64,2,5120]{2,1,0:T(2,128)(2,1)}, u32[]{:S(2)}, u32[]{:S(2)}) async-start(bf16[64,2,5120]{2,1,0:T(2,128)(2,1)} %broadcast_select_fusion), calls=%async_computation.3 | async-start | bytes 2621440 | tf_op jit(solution)/shard_map/all_to_all | solution.py:23
  192.6 39.8 %all-to-all-start.1 = ((bf16[64,2,5120]{2,1,0:T(2,128)(2,1)}), bf16[64,2,5120]{2,1,0:T(2,128)(2,1)}, u32[]{:S(2)}, u32[]{:S(2)}) async-start(bf16[64,2,5120]{2,1,0:T(2,128)(2,1)} %broadcast_select_fusion.1), calls=%async_computation.1 | async-start | bytes 2621440 | tf_op jit(solution)/shard_map/all_to_all | solution.py:23
  198.1 757.3 %all-reduce.3.cloned.1.call-start = ((), (), s32[]{:S(2)}) async-start(), calls=%async_computation.4 | async-start | bytes 5242880 | tf_op jit(solution)/shard_map/psum | solution.py:52
  236.3 53.9 %collective-permute-start = (bf16[128,5120]{1,0:T(8,128)(2,1)}, bf16[128,5120]{1,0:T(8,128)(2,1)S(1)}, u32[]{:S(2)}, u32[]{:S(2)}) collective-permute-start(bf16[128,5120]{1,0:T(8,128)(2,1)} %all_to_all.27), channel_id=1, source_target_pairs={{0,64},{64,128},{128,192},{192,256},{256,320},{320,384},{384,448},... | collective-permute-start | bytes 3932168 | tf_op jit(solution)/shard_map/ppermute | solution.py:10
Sparse Core Ops, SparseCore 0:
  205.1 750.2 all-reduce.2
where the time goes:
time: 966 us; the launch traced here: 965 us
  waiting for transfers between devices  514 us (53%)
  blocking collectives  368 us (38%)
  starting transfers between devices  30.2 us (3%)
  local copies, waits for them, and re-layouts  24.4 us (3%)
  between operations  14.2 us (1%)
    psum x1, blocking collectives, on_device(): lax.psum((down_grad, up_grad, gain_grad), 'peer')  368 us
    psum x1, waiting for transfers between devices, on_device(): lax.psum((down_grad, up_grad, gain_grad), 'peer')  295 us
    ppermute x2, waiting for transfers between devices, passed_along(): return lax.ppermute(value, axis, pairs)  110 us
    all_to_all x2, waiting for transfers between devices, regroup(): lax.all_to_all(payload, 'peer', split_axis=0, concat_axis=0, tiled=True)  55.6 us
    all_to_all x2, waiting for transfers between devices, regroup(): lax.all_to_all(picked, 'peer', split_axis=0, concat_axis=0, tiled=True)  53.8 us
  transfers between devices with their start and end apart: 7, of which 7 were waited for; matrix products, arithmetic and copies ran while one was open for 3% of the time, Pallas kernels for 0%

commit v1 on v0

v1 whole, which is shorter than its diff:
```python
import jax
import jax.numpy as jnp
from jax import lax
from jax.experimental import pallas as pl
from jax.experimental.pallas import tpu as pltpu
from jax.sharding import PartitionSpec as P

NX, NY, NZ = 4, 4, 4
N_PEER = NX * NY * NZ
N_SECTION = 8
PLANES = [[y * 16 + z * 4 + x for y in range(NY) for x in range(NX)] for z in range(NZ)]
BF16, F32 = jnp.bfloat16, jnp.float32


def along(value, section_steps, z_steps=0):
    pairs = []
    for s in range(N_SECTION):
        for y in range(NY):
            for z in range(NZ):
                for x in range(NX):
                    source = s * N_PEER + y * 16 + z * 4 + x
                    target = ((s + section_steps) % N_SECTION) * N_PEER + y * 16 + ((z + z_steps) % NZ) * 4 + x
                    pairs.append((source, target))
    return lax.ppermute(value, ("section", "peer"), pairs)


def spread_kernel(match_ref, pieces_ref, out_ref):
    def step(p, carry):
        out_ref[match_ref[p]] = pieces_ref[p]
        return carry

    lax.fori_loop(0, N_PEER, step, 0)


def by_target(match_row, pieces):
    return pl.pallas_call(
        spread_kernel,
        out_shape=jax.ShapeDtypeStruct(pieces.shape, pieces.dtype),
        in_specs=[pl.BlockSpec(memory_space=pltpu.SMEM), pl.BlockSpec(memory_space=pltpu.VMEM)],
        out_specs=pl.BlockSpec(memory_space=pltpu.VMEM),
        name="by_target",
    )(match_row, pieces)


def meet_kernel(match_ref, before_ref, ahead_ref, behind_ref, out_ref):
    first = lax.broadcasted_iota(jnp.int32, (2, 128), 1) < 64

    def forward(p, carry):
        out_ref[before_ref[p]] = behind_ref[p]
        return carry

    def backward(p, carry):
        out_ref[p] = jnp.where(first, out_ref[p], ahead_ref[match_ref[p]])
        return carry

    lax.fori_loop(0, N_PEER, forward, 0)
    lax.fori_loop(0, N_PEER, backward, 0)


def meet(match_row, match_before, from_ahead, from_behind):
    return pl.pallas_call(
        meet_kernel,
        out_shape=jax.ShapeDtypeStruct(from_ahead.shape, from_ahead.dtype),
        in_specs=[pl.BlockSpec(memory_space=pltpu.SMEM)] * 2 + [pl.BlockSpec(memory_space=pltpu.VMEM)] * 2,
        out_specs=pl.BlockSpec(memory_space=pltpu.VMEM),
        name="meet",
    )(match_row, match_before, from_ahead, from_behind)


def exchange(value):
    return lax.all_to_all(value, "peer", split_axis=0, concat_axis=0, tiled=True)


def on_device(hidden_in, out_grad, gain, w_down, w_up, matching):
    tokens, held_grad, gain_row = hidden_in[0], out_grad[0], gain[0]
    down_rows, up_rows, match_row = w_down[0], w_up[0], matching[0]
    peer = lax.axis_index("peer")
    z_at = (peer // NX) % NZ

    up_before = along(up_rows, 1)
    match_before = along(match_row, 1)

    tokens_f = tokens.astype(F32)
    inv_rms = lax.rsqrt(jnp.mean(tokens_f * tokens_f, axis=-1, keepdims=True) + 1e-05)
    normed = (tokens_f * inv_rms * gain_row).astype(BF16)
    preact = jnp.dot(normed, down_rows.T, preferred_element_type=F32)
    active = jax.nn.silu(preact).astype(BF16)
    result = (tokens_f + jnp.dot(active, up_rows, preferred_element_type=F32)).astype(BF16)

    pieces = result.reshape(8, 16, 8, 640).transpose(0, 2, 1, 3).reshape(N_PEER, 16, 640)
    held = exchange(pieces)
    moved = along(by_target(match_row, held), 1)

    act_grad_held = jnp.dot(held_grad, up_before.T, preferred_element_type=F32)
    small = jnp.concatenate([active.astype(F32), act_grad_held], axis=1)
    small = exchange(small.reshape(N_PEER, 2, 128))
    small = meet(match_row, match_before, along(small, -1), along(small, 1))
    small = exchange(small).reshape(128, 128)
    active_before = small[:, :64].astype(BF16)
    act_grad = small[:, 64:]

    q = jax.nn.sigmoid(preact)
    pre_grad = (act_grad * q * (1.0 + preact * (1.0 - q))).astype(BF16)
    contract = (((0,), (0,)), ((), ()))
    down_part = lax.dot_general(normed, pre_grad, contract, preferred_element_type=F32)
    up_part = lax.dot_general(held_grad, active_before, contract, preferred_element_type=F32)
    part = jnp.concatenate([down_part, up_part], axis=1).astype(BF16)
    part = part.reshape(NY, NZ, NX, 80, 128).transpose(0, 2, 1, 3, 4).reshape(NY * NX, NZ * 80, 128)
    part = lax.all_to_all(part, "peer", split_axis=0, concat_axis=0, tiled=True, axis_index_groups=PLANES)
    plane_sum = jnp.sum(part.astype(F32), axis=0).reshape(NZ, 80, 128)
    total = lax.dynamic_index_in_dim(plane_sum, z_at, 0, keepdims=False)
    for k in range(1, NZ):
        chunk = lax.dynamic_index_in_dim(plane_sum, (z_at + k) % NZ, 0, keepdims=False)
        total = total + along(chunk, 0, k)
    grad_down = total[:, :64].T
    grad_up = along(total[:, 64:], -1).T
    own = lambda array: lax.dynamic_slice_in_dim(array, peer * 80, 80, array.ndim - 1)
    grad_gain = jnp.sum(own(down_rows).astype(F32) * grad_down, axis=0) / own(gain_row)

    landed = exchange(moved)
    act_out = landed.reshape(8, 8, 16, 640).transpose(0, 2, 1, 3).reshape(128, 5120)
    return act_out[None], grad_down[None], grad_up[None], grad_gain[None]


def solution(mesh):
    placed = (
        P("section", "peer", None),
        P("section", "peer", None),
        P("section", None),
        P("section", None, None),
        P("section", None, None),
        P("section", None),
    )
    return jax.shard_map(
        on_device,
        mesh=mesh,
        in_specs=placed,
        out_specs=(
            P("section", "peer", None),
            P("section", None, "peer"),
            P("section", None, "peer"),
            P("section", "peer"),
        ),
        check_vma=False,
    )
```

time: 966 us -> 251 us (0.26)
  the two profiles are of different devices: /device:TPU:128 before, /device:TPU:1 now
where the time goes in v1:
time: 251 us; the launch traced here: 250 us
  waiting for transfers between devices  92.4 us (37%)
  starting transfers between devices  65.7 us (26%)
  blocking collectives  54 us (22%)
  local copies, waits for them, and re-layouts  19.1 us (8%)
  other arithmetic  7.54 us (3%)
  matrix products  5.44 us (2%)
  Pallas kernels  5.13 us (2%)
    ppermute x9, waiting for transfers between devices, along(): return lax.ppermute(value, ('section', 'peer'), pairs)  64.2 us
    ppermute x9, starting transfers between devices, along(): return lax.ppermute(value, ('section', 'peer'), pairs)  48 us
    all_to_all x1, blocking collectives, exchange(): lax.all_to_all(value, 'peer', split_axis=0, concat_axis=0, tiled=True)  32.6 us
    all_to_all x3, waiting for transfers between devices, exchange(): lax.all_to_all(value, 'peer', split_axis=0, concat_axis=0, tiled=True)  28.2 us
    all_to_all x1, blocking collectives, on_device(): lax.all_to_all(part, 'peer', split_axis=0, concat_axis=0, tiled=True, axi...  21.5 us
    all_to_all x3, starting transfers between devices, exchange(): lax.all_to_all(value, 'peer', split_axis=0, concat_axis=0, tiled=True)  17.7 us
    concatenate x2, local copies, waits for them, and re-layouts, on_device(): part = jnp.concatenate([down_part, up_part], axis=1).astype(BF16)  5.19 us
  transfers between devices with their start and end apart: 12, of which 8 were waited for; matrix products, arithmetic and copies ran while one was open for 10% of the time, Pallas kernels for 0%

profile of v1, /device:TPU:1, one launch (start us, length us, event | category | flops | bytes accessed | tf_op | source)
XLA Modules:
  0.0 250.3 jit_solution(7667871647910417184)
XLA Ops:
  0.7 10.3 %collective-permute-start.2 = (bf16[64,5120]{1,0:T(8,128)(2,1)}, bf16[64,5120]{1,0:T(8,128)(2,1)S(1)}, u32[]{:S(2)}, u32[]{:S(2)}) collective-permute-start(bf16[64,5120]{1,0:T(8,128)(2,1)} %bitcast.98), channel_id=1, source_target_pairs={{0,64},{1,65},{2,66},{3,67},{4,68},{5,69},{6,70},{7,71},{8,72},{9,... | collective-permute-start | bytes 1966088 | tf_op jit(solution)/shard_map/ppermute | solution.py:24
  11.0 1.7 fusion.4
  12.7 1.8 fusion.26
  14.5 12.2 %collective-permute-done.2 = bf16[64,5120]{1,0:T(8,128)(2,1)S(1)} collective-permute-done((bf16[64,5120]{1,0:T(8,128)(2,1)}, bf16[64,5120]{1,0:T(8,128)(2,1)S(1)}, u32[]{:S(2)}, u32[]{:S(2)}) %collective-permute-start.2) | collective-permute-done | bytes 655392 | tf_op jit(solution)/shard_map/ppermute | solution.py:24
  27.3 32.6 %all_to_all.25 = f32[64,2,128]{2,1,0:T(2,128)S(1)} all-to-all(f32[64,2,128]{2,1,0:T(2,128)S(1)} %bitcast.103), channel_id=1, replica_groups=mesh['section'=8,'peer'=64] {'peer'}, dimensions={0} | all-to-all | bytes 131072 | tf_op jit(solution)/shard_map/all_to_all | solution.py:71
  59.9 6.0 %collective-permute-start.3 = (f32[64,2,128]{2,1,0:T(2,128)S(1)}, f32[64,2,128]{2,1,0:T(2,128)S(1)}, u32[]{:S(2)}, u32[]{:S(2)}) collective-permute-start(f32[64,2,128]{2,1,0:T(2,128)S(1)} %all_to_all.25), channel_id=1, source_target_pairs={{0,448},{1,449},{2,450},{3,451},{4,452},{5,453},{6,454},{7,455},{8... | collective-permute-start | bytes 196616 | tf_op jit(solution)/shard_map/ppermute | solution.py:24
  65.9 5.6 %collective-permute-start.4 = (f32[64,2,128]{2,1,0:T(2,128)S(1)}, f32[64,2,128]{2,1,0:T(2,128)S(1)}, u32[]{:S(2)}, u32[]{:S(2)}) collective-permute-start(f32[64,2,128]{2,1,0:T(2,128)S(1)} %all_to_all.25), channel_id=1, source_target_pairs={{0,64},{1,65},{2,66},{3,67},{4,68},{5,69},{6,70},{7,71},{8,72},{9,... | collective-permute-start | bytes 196616 | tf_op jit(solution)/shard_map/ppermute | solution.py:24
  71.5 2.4 collective-permute-start.1
  75.9 2.3 meet.1
  78.2 4.6 %all-to-all-start.3 = ((f32[64,2,128]{2,1,0:T(2,128)}), f32[64,2,128]{2,1,0:T(2,128)S(1)}, u32[]{:S(2)}, u32[]{:S(2)}) async-start(f32[64,2,128]{2,1,0:T(2,128)} %meet.1), calls=%async_computation.3 | async-start | bytes 131072 | tf_op jit(solution)/shard_map/all_to_all | solution.py:71
  84.8 7.1 %all-to-all-done.3 = f32[64,2,128]{2,1,0:T(2,128)S(1)} async-done(((f32[64,2,128]{2,1,0:T(2,128)}), f32[64,2,128]{2,1,0:T(2,128)S(1)}, u32[]{:S(2)}, u32[]{:S(2)}) %all-to-all-start.3) | async-done | bytes 65568 | tf_op jit(solution)/shard_map/all_to_all | solution.py:71
  91.8 5.6 %all-to-all-start = ((bf16[64,16,640]{2,1,0:T(8,128)(2,1)}), bf16[64,16,640]{2,1,0:T(8,128)(2,1)}, u32[]{:S(2)}, u32[]{:S(2)}) async-start(bf16[64,16,640]{2,1,0:T(8,128)(2,1)} %bitcast.94), calls=%async_computation | async-start | bytes 2621440 | tf_op jit(solution)/shard_map/all_to_all | solution.py:71
  99.0 1.8 copy.24
  101.3 2.3 concatenate.11
  103.6 2.9 %copy.27 = bf16[4,4,4,80,64]{3,4,2,1,0:T(8,128)(2,1)} copy(bf16[4,4,4,80,64]{3,2,1,0,4:T(4,128)(2,1)} %concatenate.11) | data formatting | bytes 1310720 | tf_op jit(solution)/shard_map/concatenate | solution.py:107
  106.5 2.2 convolution_convert_fusion.1
  108.6 21.1 %all-to-all-done.pieces_ref = bf16[64,16,640]{2,1,0:T(8,128)(2,1)} async-done(((bf16[64,16,640]{2,1,0:T(8,128)(2,1)}), bf16[64,16,640]{2,1,0:T(8,128)(2,1)}, u32[]{:S(2)}, u32[]{:S(2)}) %all-to-all-start) | async-done | bytes 1310752 | tf_op jit(solution)/shard_map/all_to_all | solution.py:71
  129.8 2.8 %by_target.1 = bf16[64,16,640]{2,1,0:T(8,128)(2,1)} custom-call(s32[64]{0:T(128)} %bitcast.108, bf16[64,16,640]{2,1,0:T(8,128)(2,1)} %all-to-all-done.pieces_ref), custom_call_target="tpu_custom_call" | custom-call | tf_op jit(solution)/shard_map/by_target/pallas_call | solution.py:36
  132.6 9.1 %collective-permute-start = (bf16[64,16,640]{2,1,0:T(8,128)(2,1)}, bf16[64,16,640]{2,1,0:T(8,128)(2,1)}, u32[]{:S(2)}, u32[]{:S(2)}) collective-permute-start(bf16[64,16,640]{2,1,0:T(8,128)(2,1)} %by_target.1), channel_id=1, source_target_pairs={{0,64},{1,65},{2,66},{3,67},{4,68},{5,69},{6,70},{7,71},{8,72},{9,... | collective-permute-start | bytes 3932168 | tf_op jit(solution)/shard_map/ppermute | solution.py:24
  141.7 2.2 maximum_bitcast_fusion
  143.9 2.2 copy.28
  146.1 21.5 %all_to_all.26 = bf16[16,320,128]{2,1,0:T(8,128)(2,1)} all-to-all(bf16[16,320,128]{2,1,0:T(8,128)(2,1)} %bitcast.97), channel_id=1, replica_groups={{0,1,2,3,16,17,18,19,32,33,34,35,48,49,50,51},{4,5,6,7,20,21,22,23,36,3..., dimensions={0} | all-to-all | bytes 2621440 | tf_op jit(solution)/shard_map/all_to_all | solution.py:109
  167.5 28.2 %collective-permute-done = bf16[64,16,640]{2,1,0:T(8,128)(2,1)} collective-permute-done((bf16[64,16,640]{2,1,0:T(8,128)(2,1)}, bf16[64,16,640]{2,1,0:T(8,128)(2,1)}, u32[]{:S(2)}, u32[]{:S(2)}) %collective-permute-start) | collective-permute-done | bytes 1310752 | tf_op jit(solution)/shard_map/ppermute | solution.py:24
  195.8 7.5 %all-to-all-start.1 = ((bf16[64,16,640]{2,1,0:T(8,128)(2,1)}), bf16[64,16,640]{2,1,0:T(8,128)(2,1)S(1)}, u32[]{:S(2)}, u32[]{:S(2)}) async-start(bf16[64,16,640]{2,1,0:T(8,128)(2,1)} %collective-permute-done), calls=%async_computation.1 | async-start | bytes 2621440 | tf_op jit(solution)/shard_map/all_to_all | solution.py:71
  204.9 2.9 %collective-permute-start.5 = (f32[80,128]{1,0:T(8,128)S(1)}, f32[80,128]{1,0:T(8,128)S(1)}, u32[]{:S(2)}, u32[]{:S(2)}) collective-permute-start(f32[80,128]{1,0:T(8,128)S(1)} %get-tuple-element.8), channel_id=1, source_target_pairs={{0,4},{1,5},{2,6},{3,7},{4,8},{5,9},{6,10},{7,11},{8,12},{9,13},{1... | collective-permute-start | bytes 122888 | tf_op jit(solution)/shard_map/ppermute | solution.py:24
  207.8 4.0 %collective-permute-start.6 = (f32[80,128]{1,0:T(8,128)S(1)}, f32[80,128]{1,0:T(8,128)S(1)}, u32[]{:S(2)}, u32[]{:S(2)}) collective-permute-start(f32[80,128]{1,0:T(8,128)S(1)} %get-tuple-element.10), channel_id=1, source_target_pairs={{0,8},{1,9},{2,10},{3,11},{4,12},{5,13},{6,14},{7,15},{8,0},{9,1},... | collective-permute-start | bytes 122888 | tf_op jit(solution)/shard_map/ppermute | solution.py:24
  211.8 3.1 %collective-permute-start.7 = (f32[80,128]{1,0:T(8,128)S(1)}, f32[80,128]{1,0:T(8,128)S(1)}, u32[]{:S(2)}, u32[]{:S(2)}) collective-permute-start(f32[80,128]{1,0:T(8,128)S(1)} %get-tuple-element.9), channel_id=1, source_target_pairs={{0,12},{1,13},{2,14},{3,15},{4,0},{5,1},{6,2},{7,3},{8,4},{9,5},{1... | collective-permute-start | bytes 122888 | tf_op jit(solution)/shard_map/ppermute | solution.py:24
  215.9 9.9 %collective-permute-done.5 = f32[80,128]{1,0:T(8,128)S(1)} collective-permute-done((f32[80,128]{1,0:T(8,128)S(1)}, f32[80,128]{1,0:T(8,128)S(1)}, u32[]{:S(2)}, u32[]{:S(2)}) %collective-permute-start.5) | collective-permute-done | bytes 40992 | tf_op jit(solution)/shard_map/ppermute | solution.py:24
  225.7 9.5 %collective-permute-done.6 = f32[80,128]{1,0:T(8,128)S(1)} collective-permute-done((f32[80,128]{1,0:T(8,128)S(1)}, f32[80,128]{1,0:T(8,128)S(1)}, u32[]{:S(2)}, u32[]{:S(2)}) %collective-permute-start.6) | collective-permute-done | bytes 40992 | tf_op jit(solution)/shard_map/ppermute | solution.py:24
  235.4 4.5 %collective-permute-start.8 = (f32[80,64]{1,0:T(8,128)S(1)}, f32[80,64]{1,0:T(8,128)S(1)}, u32[]{:S(2)}, u32[]{:S(2)}) collective-permute-start(f32[80,64]{1,0:T(8,128)S(1)} %get-tuple-element.11), channel_id=1, source_target_pairs={{0,448},{1,449},{2,450},{3,451},{4,452},{5,453},{6,454},{7,455},{8... | collective-permute-start | bytes 61448 | tf_op jit(solution)/shard_map/ppermute | solution.py:24
  241.3 3.8 %collective-permute-done.8 = f32[80,64]{1,0:T(8,128)S(1)} collective-permute-done((f32[80,64]{1,0:T(8,128)S(1)}, f32[80,64]{1,0:T(8,128)S(1)}, u32[]{:S(2)}, u32[]{:S(2)}) %collective-permute-start.8) | collective-permute-done | bytes 20512 | tf_op jit(solution)/shard_map/ppermute | solution.py:24
  247.1 3.2 %broadcast_in_dim_reshape.3 = bf16[1,128,5120]{2,1,0:T(8,128)(2,1)} reshape(bf16[8,16,8,640]{3,2,1,0:T(8,128)(2,1)} %copy.23) | data formatting | bytes 2621440 | tf_op jit(solution)/shard_map/broadcast_in_dim;reshape | solution.py:122
  (43 shorter events, 12.7 us)
Async XLA Ops:
  0.6 26.0 %copy-start = (bf16[1,128,5120]{2,1,0:T(8,128)(2,1)S(1)}, bf16[1,128,5120]{2,1,0:T(8,128)(2,1)}, u32[]{:S(2)}) copy-start(bf16[1,128,5120]{2,1,0:T(8,128)(2,1)} %param.7) | copy-start | bytes 3932164
  0.6 12.0 %copy-start.1 = (bf16[1,128,5120]{2,1,0:T(8,128)(2,1)S(1)}, bf16[1,128,5120]{2,1,0:T(8,128)(2,1)}, u32[]{:S(2)}) copy-start(bf16[1,128,5120]{2,1,0:T(8,128)(2,1)} %param.6) | copy-start | bytes 3932164
  0.7 26.0 %collective-permute-start.2 = (bf16[64,5120]{1,0:T(8,128)(2,1)}, bf16[64,5120]{1,0:T(8,128)(2,1)S(1)}, u32[]{:S(2)}, u32[]{:S(2)}) collective-permute-start(bf16[64,5120]{1,0:T(8,128)(2,1)} %bitcast.98), channel_id=1, source_target_pairs={{0,64},{1,65},{2,66},{3,67},{4,68},{5,69},{6,70},{7,71},{8,72},{9,... | collective-permute-start | bytes 1966088 | tf_op jit(solution)/shard_map/ppermute | solution.py:24
  14.4 57.1 %copy-start.6 = (s32[1,64]{1,0:T(1,128)S(1)}, s32[1,64]{1,0:T(1,128)}, u32[]{:S(2)}) copy-start(s32[1,64]{1,0:T(1,128)} %param.11) | copy-start | bytes 772
  14.5 68.3 %copy-start.2 = (bf16[1,64,5120]{2,1,0:T(8,128)(2,1)S(1)}, bf16[1,64,5120]{2,1,0:T(8,128)(2,1)}, u32[]{:S(2)}) copy-start(bf16[1,64,5120]{2,1,0:T(8,128)(2,1)} %param.10) | copy-start | bytes 1966084
  59.9 14.7 %collective-permute-start.3 = (f32[64,2,128]{2,1,0:T(2,128)S(1)}, f32[64,2,128]{2,1,0:T(2,128)S(1)}, u32[]{:S(2)}, u32[]{:S(2)}) collective-permute-start(f32[64,2,128]{2,1,0:T(2,128)S(1)} %all_to_all.25), channel_id=1, source_target_pairs={{0,448},{1,449},{2,450},{3,451},{4,452},{5,453},{6,454},{7,455},{8... | collective-permute-start | bytes 196616 | tf_op jit(solution)/shard_map/ppermute | solution.py:24
  65.9 8.7 %collective-permute-start.4 = (f32[64,2,128]{2,1,0:T(2,128)S(1)}, f32[64,2,128]{2,1,0:T(2,128)S(1)}, u32[]{:S(2)}, u32[]{:S(2)}) collective-permute-start(f32[64,2,128]{2,1,0:T(2,128)S(1)} %all_to_all.25), channel_id=1, source_target_pairs={{0,64},{1,65},{2,66},{3,67},{4,68},{5,69},{6,70},{7,71},{8,72},{9,... | collective-permute-start | bytes 196616 | tf_op jit(solution)/shard_map/ppermute | solution.py:24
  71.5 3.1 %collective-permute-start.1 = (s32[64]{0:T(128)S(1)}, s32[64]{0:T(128)S(1)}, u32[]{:S(2)}, u32[]{:S(2)}) collective-permute-start(s32[64]{0:T(128)S(1)} %bitcast.109), channel_id=1, source_target_pairs={{0,64},{1,65},{2,66},{3,67},{4,68},{5,69},{6,70},{7,71},{8,72},{9,... | collective-permute-start | bytes 776 | tf_op jit(solution)/shard_map/ppermute | solution.py:24
  74.6 0.5 copy-start.7
  74.6 0.6 copy-start.3
  75.3 0.6 copy-start.4
  78.2 13.6 %all-to-all-start.3 = ((f32[64,2,128]{2,1,0:T(2,128)}), f32[64,2,128]{2,1,0:T(2,128)S(1)}, u32[]{:S(2)}, u32[]{:S(2)}) async-start(f32[64,2,128]{2,1,0:T(2,128)} %meet.1), calls=%async_computation.3 | async-start | bytes 131072 | tf_op jit(solution)/shard_map/all_to_all | solution.py:71
  91.8 5.6 %copy-start.5 = (f32[1,5120]{1,0:T(1,128)S(1)}, f32[1,5120]{1,0:T(1,128)}, u32[]{:S(2)}) copy-start(f32[1,5120]{1,0:T(1,128)} %param.8) | copy-start | bytes 61444
  91.8 37.9 %all-to-all-start = ((bf16[64,16,640]{2,1,0:T(8,128)(2,1)}), bf16[64,16,640]{2,1,0:T(8,128)(2,1)}, u32[]{:S(2)}, u32[]{:S(2)}) async-start(bf16[64,16,640]{2,1,0:T(8,128)(2,1)} %bitcast.94), calls=%async_computation | async-start | bytes 2621440 | tf_op jit(solution)/shard_map/all_to_all | solution.py:71
  132.6 63.2 %collective-permute-start = (bf16[64,16,640]{2,1,0:T(8,128)(2,1)}, bf16[64,16,640]{2,1,0:T(8,128)(2,1)}, u32[]{:S(2)}, u32[]{:S(2)}) collective-permute-start(bf16[64,16,640]{2,1,0:T(8,128)(2,1)} %by_target.1), channel_id=1, source_target_pairs={{0,64},{1,65},{2,66},{3,67},{4,68},{5,69},{6,70},{7,71},{8,72},{9,... | collective-permute-start | bytes 3932168 | tf_op jit(solution)/shard_map/ppermute | solution.py:24
  195.8 49.9 %all-to-all-start.1 = ((bf16[64,16,640]{2,1,0:T(8,128)(2,1)}), bf16[64,16,640]{2,1,0:T(8,128)(2,1)S(1)}, u32[]{:S(2)}, u32[]{:S(2)}) async-start(bf16[64,16,640]{2,1,0:T(8,128)(2,1)} %collective-permute-done), calls=%async_computation.1 | async-start | bytes 2621440 | tf_op jit(solution)/shard_map/all_to_all | solution.py:71
  204.9 20.8 %collective-permute-start.5 = (f32[80,128]{1,0:T(8,128)S(1)}, f32[80,128]{1,0:T(8,128)S(1)}, u32[]{:S(2)}, u32[]{:S(2)}) collective-permute-start(f32[80,128]{1,0:T(8,128)S(1)} %get-tuple-element.8), channel_id=1, source_target_pairs={{0,4},{1,5},{2,6},{3,7},{4,8},{5,9},{6,10},{7,11},{8,12},{9,13},{1... | collective-permute-start | bytes 122888 | tf_op jit(solution)/shard_map/ppermute | solution.py:24
  207.8 27.4 %collective-permute-start.6 = (f32[80,128]{1,0:T(8,128)S(1)}, f32[80,128]{1,0:T(8,128)S(1)}, u32[]{:S(2)}, u32[]{:S(2)}) collective-permute-start(f32[80,128]{1,0:T(8,128)S(1)} %get-tuple-element.10), channel_id=1, source_target_pairs={{0,8},{1,9},{2,10},{3,11},{4,12},{5,13},{6,14},{7,15},{8,0},{9,1},... | collective-permute-start | bytes 122888 | tf_op jit(solution)/shard_map/ppermute | solution.py:24
  211.8 23.4 %collective-permute-start.7 = (f32[80,128]{1,0:T(8,128)S(1)}, f32[80,128]{1,0:T(8,128)S(1)}, u32[]{:S(2)}, u32[]{:S(2)}) collective-permute-start(f32[80,128]{1,0:T(8,128)S(1)} %get-tuple-element.9), channel_id=1, source_target_pairs={{0,12},{1,13},{2,14},{3,15},{4,0},{5,1},{6,2},{7,3},{8,4},{9,5},{1... | collective-permute-start | bytes 122888 | tf_op jit(solution)/shard_map/ppermute | solution.py:24
  235.4 9.7 %collective-permute-start.8 = (f32[80,64]{1,0:T(8,128)S(1)}, f32[80,64]{1,0:T(8,128)S(1)}, u32[]{:S(2)}, u32[]{:S(2)}) collective-permute-start(f32[80,64]{1,0:T(8,128)S(1)} %get-tuple-element.11), channel_id=1, source_target_pairs={{0,448},{1,449},{2,450},{3,451},{4,452},{5,453},{6,454},{7,455},{8... | collective-permute-start | bytes 61448 | tf_op jit(solution)/shard_map/ppermute | solution.py:24

commit v2 on v0

v2 whole, which is shorter than its diff:
```python
import jax
import jax.numpy as jnp
from jax import lax
from jax.experimental import pallas as pl
from jax.experimental.pallas import tpu as pltpu
from jax.sharding import PartitionSpec as P

NX, NY, NZ = 4, 4, 4
N_PEER = NX * NY * NZ
N_SECTION = 8
PLANE = NX * NY
D = 5120
LATENT = 64
ROWS = 128
HALF = D // 2
WIDE = HALF // NZ
OWN = D // N_PEER
PLANES = [[y * 16 + z * 4 + x for y in range(NY) for x in range(NX)] for z in range(NZ)]
BF16, F32 = jnp.bfloat16, jnp.float32
SMEM = pl.BlockSpec(memory_space=pltpu.SMEM)
VMEM = pl.BlockSpec(memory_space=pltpu.VMEM)
ANY = pl.BlockSpec(memory_space=pl.ANY)
LAST = (((1,), (1,)), ((), ()))


def along(value, section_steps, z_steps=0, flip_x=0):
    pairs = []
    for s in range(N_SECTION):
        for y in range(NY):
            for z in range(NZ):
                for x in range(NX):
                    source = s * N_PEER + y * 16 + z * 4 + x
                    target = ((s + section_steps) % N_SECTION) * N_PEER + y * 16 + ((z + z_steps) % NZ) * 4 + (x ^ flip_x)
                    pairs.append((source, target))
    return lax.ppermute(value, ("section", "peer"), pairs)


def in_plane(value):
    return lax.all_to_all(value, "peer", split_axis=0, concat_axis=0, tiled=True, axis_index_groups=PLANES)


def in_cube(value):
    return lax.all_to_all(value, "peer", split_axis=0, concat_axis=0, tiled=True)


def shape(dims, kind=BF16):
    return jax.ShapeDtypeStruct(dims, kind)


def sigmoid(value):
    return 1.0 / (1.0 + jnp.exp(-value))


def turned(at, steps):
    return lax.rem(at + steps, NZ)


def columns_of(group, start=0):
    return pl.ds(pl.multiple_of(start + group * WIDE, 128), WIDE)


def forward_kernel(z_ref, tokens_ref, gain_ref, down_ref, up_ref, normed_ref, preact_ref, active_ref, b_ref, *a_refs):
    z = z_ref[0]
    chunks = [slice(c * WIDE, (c + 1) * WIDE) for c in range(D // WIDE)]
    squares = jnp.zeros((ROWS, 1), F32)
    for cols in chunks:
        t = tokens_ref[:, cols].astype(F32)
        squares += jnp.sum(t * t, axis=1, keepdims=True)
    inv_rms = lax.rsqrt(squares / D + 1e-05)
    preact = jnp.zeros((ROWS, LATENT), F32)
    for cols in chunks:
        n = (tokens_ref[:, cols].astype(F32) * inv_rms * gain_ref[:, cols]).astype(BF16)
        normed_ref[:, cols] = n
        preact += lax.dot_general(n, down_ref[:, cols], LAST, preferred_element_type=F32)
    preact_ref[...] = preact
    active = (preact * sigmoid(preact)).astype(BF16)
    active_ref[...] = active.astype(F32)

    def result(cols):
        up = jnp.dot(active, up_ref[:, cols], preferred_element_type=F32)
        return (tokens_ref[:, cols].astype(F32) + up).astype(BF16)

    for k in range(NZ):
        a_refs[k][...] = result(columns_of(turned(z, k)))
    for c in range(NZ):
        b_ref[:, c * WIDE : (c + 1) * WIDE] = result(slice(HALF + c * WIDE, HALF + (c + 1) * WIDE))


def forward(z_at, tokens, gain_row, down_rows, up_rows):
    return pl.pallas_call(
        forward_kernel,
        out_shape=(
            shape((ROWS, D)),
            shape((ROWS, LATENT), F32),
            shape((ROWS, LATENT), F32),
            shape((ROWS, HALF)),
            *[shape((ROWS, WIDE))] * NZ,
        ),
        in_specs=[SMEM] + [VMEM] * 4,
        out_specs=[VMEM] * (4 + NZ),
        name="forward",
    )(z_at, tokens, gain_row, down_rows, up_rows)


def small_kernel(half_ref, active_ref, grad_ref, own_ref, other_ref, after_ref, out_ref, up_ref):
    half = half_ref[0]
    up_ref[pl.ds(pl.multiple_of(half * 32, 32), 32), :] = own_ref[...]
    up_ref[pl.ds(pl.multiple_of((1 - half) * 32, 32), 32), :] = other_ref[...]
    out_ref[:, :LATENT] = active_ref[...]
    out_ref[:, LATENT:] = lax.dot_general(grad_ref[...], up_ref[...], LAST, preferred_element_type=F32)


def small_payload(half, active, held_grad, own_up, other_up, after):
    return pl.pallas_call(
        small_kernel,
        out_shape=shape((ROWS, 2 * LATENT), F32),
        in_specs=[SMEM] + [VMEM] * 4 + [ANY],
        out_specs=VMEM,
        scratch_shapes=[pltpu.VMEM((LATENT, D), BF16)],
        name="small_payload",
    )(half, active, held_grad, own_up, other_up, after)


def meet_kernel(match_ref, before_ref, ahead_ref, behind_ref, after_ref, out_ref):
    first = lax.broadcasted_iota(jnp.int32, (2, 128), 1) < LATENT
    for p in range(N_PEER):
        out_ref[before_ref[p]] = behind_ref[p]
    for p in range(N_PEER):
        out_ref[p] = jnp.where(first, out_ref[p], ahead_ref[match_ref[p]])


def meet(match_row, match_before, from_ahead, from_behind, after):
    return pl.pallas_call(
        meet_kernel,
        out_shape=shape(from_ahead.shape, F32),
        in_specs=[SMEM] * 2 + [VMEM] * 2 + [ANY],
        out_specs=VMEM,
        name="meet",
    )(match_row, match_before, from_ahead, from_behind, after)


def grads_kernel(small_ref, preact_ref, normed_ref, grad_ref, after_ref, out_ref):
    preact = preact_ref[...]
    q = sigmoid(preact)
    pre_grad = small_ref[:, LATENT:] * q * (1.0 + preact * (1.0 - q))
    none = jnp.zeros((ROWS, LATENT), F32)
    down = jnp.concatenate([pre_grad, none], axis=1).T.astype(BF16)
    up = jnp.concatenate([none, small_ref[:, :LATENT]], axis=1).T.astype(BF16)
    for j in range(D // WIDE):
        cols = slice(j * WIDE, (j + 1) * WIDE)
        part = jnp.dot(down, normed_ref[:, cols], preferred_element_type=F32)
        part += jnp.dot(up, grad_ref[:, cols], preferred_element_type=F32)
        part = part.T.astype(BF16)
        for i in range(WIDE // OWN):
            p = j * (WIDE // OWN) + i
            y, z, x = p // 16, (p // 4) % 4, p % 4
            out_ref[y * NX + x, z * OWN : (z + 1) * OWN, :] = part[i * OWN : (i + 1) * OWN]


def grads(small, preact, normed, held_grad, after):
    return pl.pallas_call(
        grads_kernel,
        out_shape=shape((PLANE, NZ * OWN, 2 * LATENT)),
        in_specs=[VMEM] * 4 + [ANY],
        out_specs=VMEM,
        name="grads",
    )(small, preact, normed, held_grad, after)


def beside_kernel(r0, r1, r2, r3, after_ref, out_ref):
    for k, ref in enumerate((r0, r1, r2, r3)):
        out_ref[:, :, k * WIDE : (k + 1) * WIDE] = ref[...]


def beside(parts, after):
    return pl.pallas_call(
        beside_kernel,
        out_shape=shape((PLANE, 8, HALF)),
        in_specs=[VMEM] * NZ + [ANY],
        out_specs=VMEM,
        name="beside",
    )(*parts, after)


def route_a_kernel(z_ref, before_ref, held_ref, o0, o1, o2, o3, sorted_ref):
    z = z_ref[0]
    for xy in range(PLANE):
        for k in range(NZ):
            source = (xy // NX) * 16 + turned(z, NZ - k) * 4 + xy % NX
            q = before_ref[source]
            place = (q // 16) * NX + lax.rem(q, NX)
            planes_on = turned(lax.rem(q // 4, NZ) + NZ, 0 - z)
            sorted_ref[planes_on, place] = held_ref[xy, :, k * WIDE : (k + 1) * WIDE]
    for k, out in enumerate((o0, o1, o2, o3)):
        out[...] = sorted_ref[k]


def route_a(z_at, match_before, held):
    return pl.pallas_call(
        route_a_kernel,
        out_shape=[shape((PLANE, 8, WIDE))] * NZ,
        in_specs=[SMEM] * 2 + [VMEM],
        out_specs=[VMEM] * NZ,
        scratch_shapes=[pltpu.VMEM((NZ, PLANE, 8, WIDE), BF16)],
        name="route_a",
    )(z_at, match_before, held)


def route_b_kernel(z_ref, before_ref, r0, r1, r2, r3, after_ref, out_ref, sorted_ref):
    z = z_ref[0]
    for k, ref in enumerate((r0, r1, r2, r3)):
        for xy in range(PLANE):
            source = (xy // NX) * 16 + turned(z, NZ - k) * 4 + xy % NX
            q = before_ref[source]
            place = (q // 16) * NX + lax.rem(q, NX)
            planes_on = turned(lax.rem(q // 4, NZ) + NZ, 0 - z)
            sorted_ref[planes_on, place] = ref[xy]
    for k in range(NZ):
        out_ref[:, :, k * WIDE : (k + 1) * WIDE] = sorted_ref[k]


def route_b(z_at, match_before, parts, after):
    return pl.pallas_call(
        route_b_kernel,
        out_shape=shape((PLANE, 8, HALF)),
        in_specs=[SMEM] * 2 + [VMEM] * NZ + [ANY],
        out_specs=VMEM,
        scratch_shapes=[pltpu.VMEM((NZ, PLANE, 8, WIDE), BF16)],
        name="route_b",
    )(z_at, match_before, *parts, after)


def assemble_kernel(z_ref, a_ref, b0_ref, b1_ref, b2_ref, b3_ref, out_ref):
    z = z_ref[0]
    for k, ref in enumerate((b0_ref, b1_ref, b2_ref, b3_ref)):
        group = turned(z, NZ - k)
        out_ref[:, columns_of(group)] = a_ref[:, k * WIDE : (k + 1) * WIDE]
        out_ref[:, columns_of(group, HALF)] = ref[:, :WIDE]


def assemble(z_at, landed_a, landed_b):
    return pl.pallas_call(
        assemble_kernel,
        out_shape=shape((ROWS, D)),
        in_specs=[SMEM] + [VMEM] * (1 + NZ),
        out_specs=VMEM,
        name="assemble",
    )(z_at, landed_a, *landed_b)


def on_device(hidden_in, out_grad, gain, w_down, w_up, matching):
    tokens, held_grad = hidden_in[0], out_grad[0]
    down_rows, up_rows, match_row = w_down[0], w_up[0], matching[0]
    peer = lax.axis_index("peer")
    z = (peer // NX) % NZ
    z_at = z.reshape(1)
    half = peer % 2

    own_up = along(lax.dynamic_slice_in_dim(up_rows, half * 32, 32, 0), 1)
    match_before = along(match_row, 1)
    normed, preact, active, half_b, *groups_a = forward(z_at, tokens, gain, down_rows, up_rows)

    a_parts = [along(part.reshape(PLANE, 8, WIDE), 1, k) for k, part in enumerate(groups_a)]
    b_spread = in_plane(half_b.reshape(PLANE, 8, HALF))
    other_up = along(own_up, 0, 0, 1)

    small = small_payload(half.reshape(1), active, held_grad, own_up, other_up, b_spread)
    small = in_cube(small.reshape(N_PEER, 2, 128))

    b_parts = [
        along(lax.dynamic_slice_in_dim(b_spread, ((z + k) % NZ) * WIDE, WIDE, 2), 1, k) for k in range(NZ)
    ]

    a_spread = in_plane(beside(a_parts, small))
    a_sorted = route_a(z_at, match_before, a_spread)

    small = meet(match_row, match_before, along(small, -1), along(small, 1), a_spread)
    small = in_cube(small).reshape(ROWS, 2 * LATENT)

    b_sorted = in_plane(route_b(z_at, match_before, b_parts, small))

    part = in_plane(grads(small, preact, normed, held_grad, b_sorted))
    plane_sum = jnp.sum(part.astype(F32), axis=0).reshape(NZ, OWN, 2 * LATENT)
    total = lax.dynamic_index_in_dim(plane_sum, z, 0, keepdims=False)
    for k in range(1, NZ):
        chunk = lax.dynamic_index_in_dim(plane_sum, (z + k) % NZ, 0, keepdims=False)
        total = total + along(chunk, 0, k)
    grad_down = total[:, :LATENT].T
    grad_up = along(total[:, LATENT:], -1).T
    own = lambda array: lax.dynamic_slice_in_dim(array, peer * OWN, OWN, 1)
    grad_gain = jnp.sum(own(down_rows).astype(F32) * grad_down, axis=0, keepdims=True) / own(gain)

    a_landed = [a_sorted[0]] + [along(a_sorted[k], 0, k) for k in range(1, NZ)]
    b_landed = [b_sorted] + [along(b_sorted[:, :, k * WIDE : (k + 1) * WIDE], 0, k) for k in range(1, NZ)]
    a_last = in_plane(beside(a_landed, part))
    act_out = assemble(z_at, a_last.reshape(ROWS, HALF), [b.reshape(ROWS, -1) for b in b_landed])
    return act_out[None], grad_down[None], grad_up[None], grad_gain


def solution(mesh):
    placed = (
        P("section", "peer", None),
        P("section", "peer", None),
        P("section", None),
        P("section", None, None),
        P("section", None, None),
        P("section", None),
    )
    return jax.shard_map(
        on_device,
        mesh=mesh,
        in_specs=placed,
        out_specs=(
            P("section", "peer", None),
            P("section", None, "peer"),
            P("section", None, "peer"),
            P("section", "peer"),
        ),
        check_vma=False,
    )
```

time: 966 us -> 268 us (0.28)
  the two profiles are of different devices: /device:TPU:128 before, /device:TPU:1 now
where the time goes in v2:
time: 268 us; the launch traced here: 265 us
  starting transfers between devices  160 us (60%)
  waiting for transfers between devices  51.7 us (19%)
  Pallas kernels  24.9 us (9%)
  blocking collectives  16.4 us (6%)
  local copies, waits for them, and re-layouts  8.84 us (3%)
    ppermute x23, starting transfers between devices, along(): return lax.ppermute(value, ('section', 'peer'), pairs)  121 us
    ppermute x23, waiting for transfers between devices, along(): return lax.ppermute(value, ('section', 'peer'), pairs)  42.7 us
    all_to_all x4, starting transfers between devices, in_plane(): lax.all_to_all(value, 'peer', split_axis=0, concat_axis=0, tiled=True, ax...  21.7 us
    all_to_all x2, starting transfers between devices, in_cube(): lax.all_to_all(value, 'peer', split_axis=0, concat_axis=0, tiled=True)  17.6 us
    all_to_all x1, blocking collectives, in_plane(): lax.all_to_all(value, 'peer', split_axis=0, concat_axis=0, tiled=True, ax...  16.4 us
    all_to_all x4, waiting for transfers between devices, in_plane(): lax.all_to_all(value, 'peer', split_axis=0, concat_axis=0, tiled=True, ax...  8.99 us
    unnamed x69, local copies, waits for them, and re-layouts  6.73 us
  transfers between devices with their start and end apart: 29, of which 11 were waited for; matrix products, arithmetic and copies ran while one was open for 2% of the time, Pallas kernels for 3%

profile of v2, /device:TPU:1, one launch (start us, length us, event | category | flops | bytes accessed | tf_op | source)
XLA Modules:
  0.0 265.2 jit_solution(2962856478562832554)
XLA Ops:
  1.6 10.2 %collective-permute-start.5 = (bf16[32,5120]{1,0:T(8,128)(2,1)S(1)}, bf16[32,5120]{1,0:T(8,128)(2,1)S(1)}, u32[]{:S(2)}, u32[]{:S(2)}) collective-permute-start(bf16[32,5120]{1,0:T(8,128)(2,1)S(1)} %dynamic-slice_bitcast_fusion), channel_id=1, source_target_pairs={{0,64},{1,65},{2,66},{3,67},{4,68},{5,69},{6,70},{7,71},{8,72},{9,... | collective-permute-start | bytes 983048 | tf_op jit(solution)/shard_map/ppermute | solution.py:35
  11.9 4.1 %forward.1 = (bf16[128,5120]{1,0:T(8,128)(2,1)}, f32[128,64]{1,0:T(8,128)}, f32[128,64]{1,0:T(8,128)}, bf16[128,2560]{1,0:T(8,128)(2,1)}, bf16[128,640]{1,0:T(8,...) custom-call(s32[1]{0:T(128)} %bitcast.z_ref, bf16[128,5120]{1,0:T(8,128)(2,1)} %bitcast.54, ...), custom_call_target="tpu_custom_call" | custom-call | tf_op jit(solution)/shard_map/forward/pallas_call | solution.py:90
  16.0 6.8 %all-to-all-start = ((bf16[16,8,2560]{2,1,0:T(8,128)(2,1)}), bf16[16,8,2560]{2,1,0:T(8,128)(2,1)S(1)}, u32[]{:S(2)}, u32[]{:S(2)}) async-start(bf16[16,8,2560]{2,1,0:T(8,128)(2,1)} %bitcast.56), calls=%async_computation | async-start | bytes 1310720 | tf_op jit(solution)/shard_map/all_to_all | solution.py:39
  22.8 3.3 %collective-permute-start.6 = (bf16[32,5120]{1,0:T(8,128)(2,1)S(1)}, bf16[32,5120]{1,0:T(8,128)(2,1)S(1)}, u32[]{:S(2)}, u32[]{:S(2)}) collective-permute-start(bf16[32,5120]{1,0:T(8,128)(2,1)S(1)} %collective-permute-done.5.own_ref), channel_id=1, source_target_pairs={{0,1},{1,0},{2,3},{3,2},{4,5},{5,4},{6,7},{7,6},{8,9},{9,8},{10,11... | collective-permute-start | bytes 983048 | tf_op jit(solution)/shard_map/ppermute | solution.py:35
  26.0 9.0 %all-to-all-done.after_ref = bf16[16,8,2560]{2,1,0:T(8,128)(2,1)S(1)} async-done(((bf16[16,8,2560]{2,1,0:T(8,128)(2,1)}), bf16[16,8,2560]{2,1,0:T(8,128)(2,1)S(1)}, u32[]{:S(2)}, u32[]{:S(2)}) %all-to-all-start) | async-done | bytes 655392 | tf_op jit(solution)/shard_map/all_to_all | solution.py:39
  39.4 9.2 %all-to-all-start.1 = ((f32[64,2,128]{2,1,0:T(2,128)}), f32[64,2,128]{2,1,0:T(2,128)S(1)}, u32[]{:S(2)}, u32[]{:S(2)}) async-start(f32[64,2,128]{2,1,0:T(2,128)} %bitcast.61), calls=%async_computation.1 | async-start | bytes 131072 | tf_op jit(solution)/shard_map/all_to_all | solution.py:43
  48.6 10.9 %collective-permute-start.2 = (bf16[16,8,640]{2,1,0:T(8,128)(2,1)S(1)}, bf16[16,8,640]{2,1,0:T(8,128)(2,1)S(1)}, u32[]{:S(2)}, u32[]{:S(2)}) collective-permute-start(bf16[16,8,640]{2,1,0:T(8,128)(2,1)S(1)} %bitcast.71), channel_id=1, source_target_pairs={{0,68},{1,69},{2,70},{3,71},{4,72},{5,73},{6,74},{7,75},{8,76},{9,... | collective-permute-start | bytes 491528 | tf_op jit(solution)/shard_map/ppermute | solution.py:35
  61.4 7.7 %collective-permute-start.3 = (bf16[16,8,640]{2,1,0:T(8,128)(2,1)S(1)}, bf16[16,8,640]{2,1,0:T(8,128)(2,1)S(1)}, u32[]{:S(2)}, u32[]{:S(2)}) collective-permute-start(bf16[16,8,640]{2,1,0:T(8,128)(2,1)S(1)} %bitcast.69), channel_id=1, source_target_pairs={{0,72},{1,73},{2,74},{3,75},{4,76},{5,77},{6,78},{7,79},{8,64},{9,... | collective-permute-start | bytes 491528 | tf_op jit(solution)/shard_map/ppermute | solution.py:35
  72.2 3.0 %collective-permute-done.1.r0 = bf16[16,8,640]{2,1,0:T(8,128)(2,1)S(1)} collective-permute-done((bf16[16,8,640]{2,1,0:T(8,128)(2,1)S(1)}, bf16[16,8,640]{2,1,0:T(8,128)(2,1)S(1)}, u32[]{:S(2)}, u32[]{:S(2)}) %collective-permute-start.1) | collective-permute-done | bytes 163872 | tf_op jit(solution)/shard_map/ppermute | solution.py:35
  75.2 11.3 %collective-permute-done.3.r2 = bf16[16,8,640]{2,1,0:T(8,128)(2,1)S(1)} collective-permute-done((bf16[16,8,640]{2,1,0:T(8,128)(2,1)S(1)}, bf16[16,8,640]{2,1,0:T(8,128)(2,1)S(1)}, u32[]{:S(2)}, u32[]{:S(2)}) %collective-permute-start.3) | collective-permute-done | bytes 163872 | tf_op jit(solution)/shard_map/ppermute | solution.py:35
  86.5 4.7 %collective-permute-done.4.r3 = bf16[16,8,640]{2,1,0:T(8,128)(2,1)S(1)} collective-permute-done((bf16[16,8,640]{2,1,0:T(8,128)(2,1)S(1)}, bf16[16,8,640]{2,1,0:T(8,128)(2,1)S(1)}, u32[]{:S(2)}, u32[]{:S(2)}) %collective-permute-start.4) | collective-permute-done | bytes 163872 | tf_op jit(solution)/shard_map/ppermute | solution.py:35
  94.5 6.7 %all-to-all-start.2 = ((bf16[16,8,2560]{2,1,0:T(8,128)(2,1)}), bf16[16,8,2560]{2,1,0:T(8,128)(2,1)S(1)}, u32[]{:S(2)}, u32[]{:S(2)}) async-start(bf16[16,8,2560]{2,1,0:T(8,128)(2,1)} %beside.2), calls=%async_computation.2 | async-start | bytes 1310720 | tf_op jit(solution)/shard_map/all_to_all | solution.py:39
  101.3 10.8 %collective-permute-start.11 = (f32[64,2,128]{2,1,0:T(2,128)S(1)}, f32[64,2,128]{2,1,0:T(2,128)S(1)}, u32[]{:S(2)}, u32[]{:S(2)}) collective-permute-start(f32[64,2,128]{2,1,0:T(2,128)S(1)} %copy-done.10), channel_id=1, source_target_pairs={{0,64},{1,65},{2,66},{3,67},{4,68},{5,69},{6,70},{7,71},{8,72},{9,... | collective-permute-start | bytes 196616 | tf_op jit(solution)/shard_map/ppermute | solution.py:35
  114.0 7.5 %collective-permute-start = (s32[64]{0:T(128)S(1)}, s32[64]{0:T(128)S(1)}, u32[]{:S(2)}, u32[]{:S(2)}) collective-permute-start(s32[64]{0:T(128)S(1)} %bitcast.67), channel_id=1, source_target_pairs={{0,64},{1,65},{2,66},{3,67},{4,68},{5,69},{6,70},{7,71},{8,72},{9,... | collective-permute-start | bytes 776 | tf_op jit(solution)/shard_map/ppermute | solution.py:35
  125.4 8.4 %all-to-all-start.3 = ((f32[64,2,128]{2,1,0:T(2,128)}), f32[64,2,128]{2,1,0:T(2,128)S(1)}, u32[]{:S(2)}, u32[]{:S(2)}) async-start(f32[64,2,128]{2,1,0:T(2,128)} %meet.1), calls=%async_computation.3 | async-start | bytes 131072 | tf_op jit(solution)/shard_map/all_to_all | solution.py:43
  133.8 11.2 %collective-permute-start.15 = (bf16[16,8,640]{2,1,0:T(8,128)(2,1)S(1)}, bf16[16,8,640]{2,1,0:T(8,128)(2,1)S(1)}, u32[]{:S(2)}, u32[]{:S(2)}) collective-permute-start(bf16[16,8,640]{2,1,0:T(8,128)(2,1)S(1)} %get-tuple-element.35), channel_id=1, source_target_pairs={{0,76},{1,77},{2,78},{3,79},{4,64},{5,65},{6,66},{7,67},{8,68},{9,... | collective-permute-start | bytes 491528 | tf_op jit(solution)/shard_map/ppermute | solution.py:35
  146.9 4.8 %collective-permute-start.13 = (bf16[16,8,640]{2,1,0:T(8,128)(2,1)S(1)}, bf16[16,8,640]{2,1,0:T(8,128)(2,1)S(1)}, u32[]{:S(2)}, u32[]{:S(2)}) collective-permute-start(bf16[16,8,640]{2,1,0:T(8,128)(2,1)S(1)} %get-tuple-element.37), channel_id=1, source_target_pairs={{0,68},{1,69},{2,70},{3,71},{4,72},{5,73},{6,74},{7,75},{8,76},{9,... | collective-permute-start | bytes 491528 | tf_op jit(solution)/shard_map/ppermute | solution.py:35
  155.9 7.3 %collective-permute-done.14.r2 = bf16[16,8,640]{2,1,0:T(8,128)(2,1)S(1)} collective-permute-done((bf16[16,8,640]{2,1,0:T(8,128)(2,1)S(1)}, bf16[16,8,640]{2,1,0:T(8,128)(2,1)S(1)}, u32[]{:S(2)}, u32[]{:S(2)}) %collective-permute-start.14) | collective-permute-done | bytes 163872 | tf_op jit(solution)/shard_map/ppermute | solution.py:35
  163.3 3.5 %collective-permute-done.13.r1 = bf16[16,8,640]{2,1,0:T(8,128)(2,1)S(1)} collective-permute-done((bf16[16,8,640]{2,1,0:T(8,128)(2,1)S(1)}, bf16[16,8,640]{2,1,0:T(8,128)(2,1)S(1)}, u32[]{:S(2)}, u32[]{:S(2)}) %collective-permute-start.13) | collective-permute-done | bytes 163872 | tf_op jit(solution)/shard_map/ppermute | solution.py:35
  166.7 4.8 %collective-permute-done.12.r0 = bf16[16,8,640]{2,1,0:T(8,128)(2,1)S(1)} collective-permute-done((bf16[16,8,640]{2,1,0:T(8,128)(2,1)S(1)}, bf16[16,8,640]{2,1,0:T(8,128)(2,1)S(1)}, u32[]{:S(2)}, u32[]{:S(2)}) %collective-permute-start.12) | collective-permute-done | bytes 163872 | tf_op jit(solution)/shard_map/ppermute | solution.py:35
  175.2 16.4 %all_to_all.35.after_ref = bf16[16,8,2560]{2,1,0:T(8,128)(2,1)} all-to-all(bf16[16,8,2560]{2,1,0:T(8,128)(2,1)} %route_b.1), channel_id=1, replica_groups={{0,1,2,3,16,17,18,19,32,33,34,35,48,49,50,51},{4,5,6,7,20,21,22,23,36,3..., dimensions={0} | all-to-all | bytes 1310720 | tf_op jit(solution)/shard_map/all_to_all | solution.py:39
  191.5 4.0 %grads.1 = bf16[16,320,128]{2,1,0:T(8,128)(2,1)} custom-call(f32[128,128]{1,0:T(8,128)} %bitcast.60, f32[128,64]{1,0:T(8,128)} %get-tuple-element.26.preact_ref, bf16[128,5120]{1,0:T(8,128)(2,1)} %get-tuple-element.27.normed_ref, bf16[128,5120]{1,0:T(8,128)(2,1)} %bitcast.50, bf16[16,8,2560]{2,1,0:T(8,128)(2,1)} %all_to_all.35.after_ref), custom_call_target="tpu_custom_call" | custom-call | tf_op jit(solution)/shard_map/grads/pallas_call | solution.py:161
  195.5 3.7 %all-to-all-start.5 = ((bf16[16,320,128]{2,1,0:T(8,128)(2,1)}), bf16[16,320,128]{2,1,0:T(8,128)(2,1)S(1)}, u32[]{:S(2)}, u32[]{:S(2)}) async-start(bf16[16,320,128]{2,1,0:T(8,128)(2,1)} %grads.1), calls=%async_computation.5 | async-start | bytes 2621440 | tf_op jit(solution)/shard_map/all_to_all | solution.py:39
  203.1 8.0 %collective-permute-start.7 = (bf16[16,8,640]{2,1,0:T(8,128)(2,1)}, bf16[16,8,640]{2,1,0:T(8,128)(2,1)S(1)}, u32[]{:S(2)}, u32[]{:S(2)}) collective-permute-start(bf16[16,8,640]{2,1,0:T(8,128)(2,1)} %get-tuple-element.23), channel_id=1, source_target_pairs={{0,4},{1,5},{2,6},{3,7},{4,8},{5,9},{6,10},{7,11},{8,12},{9,13},{1... | collective-permute-start | bytes 491528 | tf_op jit(solution)/shard_map/ppermute | solution.py:35
  213.4 4.3 %collective-permute-start.9 = (bf16[16,8,640]{2,1,0:T(8,128)(2,1)}, bf16[16,8,640]{2,1,0:T(8,128)(2,1)S(1)}, u32[]{:S(2)}, u32[]{:S(2)}) collective-permute-start(bf16[16,8,640]{2,1,0:T(8,128)(2,1)} %get-tuple-element.25), channel_id=1, source_target_pairs={{0,12},{1,13},{2,14},{3,15},{4,0},{5,1},{6,2},{7,3},{8,4},{9,5},{1... | collective-permute-start | bytes 491528 | tf_op jit(solution)/shard_map/ppermute | solution.py:35
  217.9 6.2 %collective-permute-start.19 = (f32[80,128]{1,0:T(8,128)S(1)}, f32[80,128]{1,0:T(8,128)S(1)}, u32[]{:S(2)}, u32[]{:S(2)}) collective-permute-start(f32[80,128]{1,0:T(8,128)S(1)} %get-tuple-element.39), channel_id=1, source_target_pairs={{0,4},{1,5},{2,6},{3,7},{4,8},{5,9},{6,10},{7,11},{8,12},{9,13},{1... | collective-permute-start | bytes 122888 | tf_op jit(solution)/shard_map/ppermute | solution.py:35
  226.1 4.3 %collective-permute-start.20 = (f32[80,128]{1,0:T(8,128)S(1)}, f32[80,128]{1,0:T(8,128)S(1)}, u32[]{:S(2)}, u32[]{:S(2)}) collective-permute-start(f32[80,128]{1,0:T(8,128)S(1)} %get-tuple-element.41), channel_id=1, source_target_pairs={{0,8},{1,9},{2,10},{3,11},{4,12},{5,13},{6,14},{7,15},{8,0},{9,1},... | collective-permute-start | bytes 122888 | tf_op jit(solution)/shard_map/ppermute | solution.py:35
  230.5 3.0 %collective-permute-start.18 = (bf16[16,8,640]{2,1,0:T(8,128)(2,1)S(1)}, bf16[16,8,640]{2,1,0:T(8,128)(2,1)S(1)}, u32[]{:S(2)}, u32[]{:S(2)}) collective-permute-start(bf16[16,8,640]{2,1,0:T(8,128)(2,1)S(1)} %get-tuple-element.32), channel_id=1, source_target_pairs={{0,12},{1,13},{2,14},{3,15},{4,0},{5,1},{6,2},{7,3},{8,4},{9,5},{1... | collective-permute-start | bytes 491528 | tf_op jit(solution)/shard_map/ppermute | solution.py:35
  237.6 4.5 %all-to-all-start.6 = ((bf16[16,8,2560]{2,1,0:T(8,128)(2,1)}), bf16[16,8,2560]{2,1,0:T(8,128)(2,1)S(1)}, u32[]{:S(2)}, u32[]{:S(2)}) async-start(bf16[16,8,2560]{2,1,0:T(8,128)(2,1)} %beside.3), calls=%async_computation.6 | async-start | bytes 1310720 | tf_op jit(solution)/shard_map/all_to_all | solution.py:39
  242.2 3.1 %collective-permute-start.16 = (bf16[16,8,640]{2,1,0:T(8,128)(2,1)S(1)}, bf16[16,8,640]{2,1,0:T(8,128)(2,1)S(1)}, u32[]{:S(2)}, u32[]{:S(2)}) collective-permute-start(bf16[16,8,640]{2,1,0:T(8,128)(2,1)S(1)} %get-tuple-element.34), channel_id=1, source_target_pairs={{0,4},{1,5},{2,6},{3,7},{4,8},{5,9},{6,10},{7,11},{8,12},{9,13},{1... | collective-permute-start | bytes 491528 | tf_op jit(solution)/shard_map/ppermute | solution.py:35
  245.4 8.1 %collective-permute-start.22 = (f32[80,64]{1,0:T(8,128)S(1)}, f32[80,64]{1,0:T(8,128)S(1)}, u32[]{:S(2)}, u32[]{:S(2)}) collective-permute-start(f32[80,64]{1,0:T(8,128)S(1)} %get-tuple-element.42), channel_id=1, source_target_pairs={{0,448},{1,449},{2,450},{3,451},{4,452},{5,453},{6,454},{7,455},{8... | collective-permute-start | bytes 61448 | tf_op jit(solution)/shard_map/ppermute | solution.py:35
  255.6 5.3 %collective-permute-done.22 = f32[80,64]{1,0:T(8,128)S(1)} collective-permute-done((f32[80,64]{1,0:T(8,128)S(1)}, f32[80,64]{1,0:T(8,128)S(1)}, u32[]{:S(2)}, u32[]{:S(2)}) %collective-permute-start.22) | collective-permute-done | bytes 20512 | tf_op jit(solution)/shard_map/ppermute | solution.py:35
  (115 shorter events, 47.8 us)
Async XLA Ops:
  1.6 21.1 %collective-permute-start.5 = (bf16[32,5120]{1,0:T(8,128)(2,1)S(1)}, bf16[32,5120]{1,0:T(8,128)(2,1)S(1)}, u32[]{:S(2)}, u32[]{:S(2)}) collective-permute-start(bf16[32,5120]{1,0:T(8,128)(2,1)S(1)} %dynamic-slice_bitcast_fusion), channel_id=1, source_target_pairs={{0,64},{1,65},{2,66},{3,67},{4,68},{5,69},{6,70},{7,71},{8,72},{9,... | collective-permute-start | bytes 983048 | tf_op jit(solution)/shard_map/ppermute | solution.py:35
  16.0 19.0 %all-to-all-start = ((bf16[16,8,2560]{2,1,0:T(8,128)(2,1)}), bf16[16,8,2560]{2,1,0:T(8,128)(2,1)S(1)}, u32[]{:S(2)}, u32[]{:S(2)}) async-start(bf16[16,8,2560]{2,1,0:T(8,128)(2,1)} %bitcast.56), calls=%async_computation | async-start | bytes 1310720 | tf_op jit(solution)/shard_map/all_to_all | solution.py:39
  22.8 13.0 %collective-permute-start.6 = (bf16[32,5120]{1,0:T(8,128)(2,1)S(1)}, bf16[32,5120]{1,0:T(8,128)(2,1)S(1)}, u32[]{:S(2)}, u32[]{:S(2)}) collective-permute-start(bf16[32,5120]{1,0:T(8,128)(2,1)S(1)} %collective-permute-done.5.own_ref), channel_id=1, source_target_pairs={{0,1},{1,0},{2,3},{3,2},{4,5},{5,4},{6,7},{7,6},{8,9},{9,8},{10,11... | collective-permute-start | bytes 983048 | tf_op jit(solution)/shard_map/ppermute | solution.py:35
  36.6 32.6 %copy-start.29 = (bf16[128,640]{1,0:T(8,128)(2,1)S(1)}, bf16[128,640]{1,0:T(8,128)(2,1)}, u32[]{:S(2)}) copy-start(bf16[128,640]{1,0:T(8,128)(2,1)} %get-tuple-element.19) | copy-start | bytes 491524
  39.4 51.8 %all-to-all-start.1 = ((f32[64,2,128]{2,1,0:T(2,128)}), f32[64,2,128]{2,1,0:T(2,128)S(1)}, u32[]{:S(2)}, u32[]{:S(2)}) async-start(f32[64,2,128]{2,1,0:T(2,128)} %bitcast.61), calls=%async_computation.1 | async-start | bytes 131072 | tf_op jit(solution)/shard_map/all_to_all | solution.py:43
  48.6 23.6 %collective-permute-start.2 = (bf16[16,8,640]{2,1,0:T(8,128)(2,1)S(1)}, bf16[16,8,640]{2,1,0:T(8,128)(2,1)S(1)}, u32[]{:S(2)}, u32[]{:S(2)}) collective-permute-start(bf16[16,8,640]{2,1,0:T(8,128)(2,1)S(1)} %bitcast.71), channel_id=1, source_target_pairs={{0,68},{1,69},{2,70},{3,71},{4,72},{5,73},{6,74},{7,75},{8,76},{9,... | collective-permute-start | bytes 491528 | tf_op jit(solution)/shard_map/ppermute | solution.py:35
  59.5 15.7 %collective-permute-start.1 = (bf16[16,8,640]{2,1,0:T(8,128)(2,1)S(1)}, bf16[16,8,640]{2,1,0:T(8,128)(2,1)S(1)}, u32[]{:S(2)}, u32[]{:S(2)}) collective-permute-start(bf16[16,8,640]{2,1,0:T(8,128)(2,1)S(1)} %bitcast.70), channel_id=1, source_target_pairs={{0,64},{1,65},{2,66},{3,67},{4,68},{5,69},{6,70},{7,71},{8,72},{9,... | collective-permute-start | bytes 491528 | tf_op jit(solution)/shard_map/ppermute | solution.py:35
  61.4 25.1 %collective-permute-start.3 = (bf16[16,8,640]{2,1,0:T(8,128)(2,1)S(1)}, bf16[16,8,640]{2,1,0:T(8,128)(2,1)S(1)}, u32[]{:S(2)}, u32[]{:S(2)}) collective-permute-start(bf16[16,8,640]{2,1,0:T(8,128)(2,1)S(1)} %bitcast.69), channel_id=1, source_target_pairs={{0,72},{1,73},{2,74},{3,75},{4,76},{5,77},{6,78},{7,79},{8,64},{9,... | collective-permute-start | bytes 491528 | tf_op jit(solution)/shard_map/ppermute | solution.py:35
  69.2 44.8 %copy-start.28 = (s32[1,64]{1,0:T(1,128)S(1)}, s32[1,64]{1,0:T(1,128)}, u32[]{:S(2)}) copy-start(s32[1,64]{1,0:T(1,128)} %param.11) | copy-start | bytes 772
  69.2 22.0 %collective-permute-start.4 = (bf16[16,8,640]{2,1,0:T(8,128)(2,1)S(1)}, bf16[16,8,640]{2,1,0:T(8,128)(2,1)S(1)}, u32[]{:S(2)}, u32[]{:S(2)}) collective-permute-start(bf16[16,8,640]{2,1,0:T(8,128)(2,1)S(1)} %bitcast.68), channel_id=1, source_target_pairs={{0,76},{1,77},{2,78},{3,79},{4,64},{5,65},{6,66},{7,67},{8,68},{9,... | collective-permute-start | bytes 491528 | tf_op jit(solution)/shard_map/ppermute | solution.py:35
  94.5 39.2 %copy-start.4 = (bf16[16,8,2560]{2,1,0:T(8,128)(2,1)S(1)}, bf16[16,8,2560]{2,1,0:T(8,128)(2,1)}, u32[]{:S(2)}) copy-start(bf16[16,8,2560]{2,1,0:T(8,128)(2,1)} %copy-done.3) | copy-start | bytes 1966084
  94.5 27.7 %all-to-all-start.2 = ((bf16[16,8,2560]{2,1,0:T(8,128)(2,1)}), bf16[16,8,2560]{2,1,0:T(8,128)(2,1)S(1)}, u32[]{:S(2)}, u32[]{:S(2)}) async-start(bf16[16,8,2560]{2,1,0:T(8,128)(2,1)} %beside.2), calls=%async_computation.2 | async-start | bytes 1310720 | tf_op jit(solution)/shard_map/all_to_all | solution.py:39
  101.3 21.0 %collective-permute-start.11 = (f32[64,2,128]{2,1,0:T(2,128)S(1)}, f32[64,2,128]{2,1,0:T(2,128)S(1)}, u32[]{:S(2)}, u32[]{:S(2)}) collective-permute-start(f32[64,2,128]{2,1,0:T(2,128)S(1)} %copy-done.10), channel_id=1, source_target_pairs={{0,64},{1,65},{2,66},{3,67},{4,68},{5,69},{6,70},{7,71},{8,72},{9,... | collective-permute-start | bytes 196616 | tf_op jit(solution)/shard_map/ppermute | solution.py:35
  112.0 10.2 %collective-permute-start.10 = (f32[64,2,128]{2,1,0:T(2,128)S(1)}, f32[64,2,128]{2,1,0:T(2,128)S(1)}, u32[]{:S(2)}, u32[]{:S(2)}) collective-permute-start(f32[64,2,128]{2,1,0:T(2,128)S(1)} %copy-done.10), channel_id=1, source_target_pairs={{0,448},{1,449},{2,450},{3,451},{4,452},{5,453},{6,454},{7,455},{8... | collective-permute-start | bytes 196616 | tf_op jit(solution)/shard_map/ppermute | solution.py:35
  114.0 8.3 %collective-permute-start = (s32[64]{0:T(128)S(1)}, s32[64]{0:T(128)S(1)}, u32[]{:S(2)}, u32[]{:S(2)}) collective-permute-start(s32[64]{0:T(128)S(1)} %bitcast.67), channel_id=1, source_target_pairs={{0,64},{1,65},{2,66},{3,67},{4,68},{5,69},{6,70},{7,71},{8,72},{9,... | collective-permute-start | bytes 776 | tf_op jit(solution)/shard_map/ppermute | solution.py:35
  125.4 46.2 %all-to-all-start.3 = ((f32[64,2,128]{2,1,0:T(2,128)}), f32[64,2,128]{2,1,0:T(2,128)S(1)}, u32[]{:S(2)}, u32[]{:S(2)}) async-start(f32[64,2,128]{2,1,0:T(2,128)} %meet.1), calls=%async_computation.3 | async-start | bytes 131072 | tf_op jit(solution)/shard_map/all_to_all | solution.py:43
  133.8 22.1 %collective-permute-start.15 = (bf16[16,8,640]{2,1,0:T(8,128)(2,1)S(1)}, bf16[16,8,640]{2,1,0:T(8,128)(2,1)S(1)}, u32[]{:S(2)}, u32[]{:S(2)}) collective-permute-start(bf16[16,8,640]{2,1,0:T(8,128)(2,1)S(1)} %get-tuple-element.35), channel_id=1, source_target_pairs={{0,76},{1,77},{2,78},{3,79},{4,64},{5,65},{6,66},{7,67},{8,68},{9,... | collective-permute-start | bytes 491528 | tf_op jit(solution)/shard_map/ppermute | solution.py:35
  145.0 18.3 %collective-permute-start.14 = (bf16[16,8,640]{2,1,0:T(8,128)(2,1)S(1)}, bf16[16,8,640]{2,1,0:T(8,128)(2,1)S(1)}, u32[]{:S(2)}, u32[]{:S(2)}) collective-permute-start(bf16[16,8,640]{2,1,0:T(8,128)(2,1)S(1)} %get-tuple-element.36), channel_id=1, source_target_pairs={{0,72},{1,73},{2,74},{3,75},{4,76},{5,77},{6,78},{7,79},{8,64},{9,... | collective-permute-start | bytes 491528 | tf_op jit(solution)/shard_map/ppermute | solution.py:35
  146.9 19.8 %collective-permute-start.13 = (bf16[16,8,640]{2,1,0:T(8,128)(2,1)S(1)}, bf16[16,8,640]{2,1,0:T(8,128)(2,1)S(1)}, u32[]{:S(2)}, u32[]{:S(2)}) collective-permute-start(bf16[16,8,640]{2,1,0:T(8,128)(2,1)S(1)} %get-tuple-element.37), channel_id=1, source_target_pairs={{0,68},{1,69},{2,70},{3,71},{4,72},{5,73},{6,74},{7,75},{8,76},{9,... | collective-permute-start | bytes 491528 | tf_op jit(solution)/shard_map/ppermute | solution.py:35
  151.7 19.8 %collective-permute-start.12 = (bf16[16,8,640]{2,1,0:T(8,128)(2,1)S(1)}, bf16[16,8,640]{2,1,0:T(8,128)(2,1)S(1)}, u32[]{:S(2)}, u32[]{:S(2)}) collective-permute-start(bf16[16,8,640]{2,1,0:T(8,128)(2,1)S(1)} %get-tuple-element.38), channel_id=1, source_target_pairs={{0,64},{1,65},{2,66},{3,67},{4,68},{5,69},{6,70},{7,71},{8,72},{9,... | collective-permute-start | bytes 491528 | tf_op jit(solution)/shard_map/ppermute | solution.py:35
  195.5 22.1 %all-to-all-start.5 = ((bf16[16,320,128]{2,1,0:T(8,128)(2,1)}), bf16[16,320,128]{2,1,0:T(8,128)(2,1)S(1)}, u32[]{:S(2)}, u32[]{:S(2)}) async-start(bf16[16,320,128]{2,1,0:T(8,128)(2,1)} %grads.1), calls=%async_computation.5 | async-start | bytes 2621440 | tf_op jit(solution)/shard_map/all_to_all | solution.py:39
  203.1 23.0 %collective-permute-start.7 = (bf16[16,8,640]{2,1,0:T(8,128)(2,1)}, bf16[16,8,640]{2,1,0:T(8,128)(2,1)S(1)}, u32[]{:S(2)}, u32[]{:S(2)}) collective-permute-start(bf16[16,8,640]{2,1,0:T(8,128)(2,1)} %get-tuple-element.23), channel_id=1, source_target_pairs={{0,4},{1,5},{2,6},{3,7},{4,8},{5,9},{6,10},{7,11},{8,12},{9,13},{1... | collective-permute-start | bytes 491528 | tf_op jit(solution)/shard_map/ppermute | solution.py:35
  211.1 19.4 %collective-permute-start.8 = (bf16[16,8,640]{2,1,0:T(8,128)(2,1)}, bf16[16,8,640]{2,1,0:T(8,128)(2,1)S(1)}, u32[]{:S(2)}, u32[]{:S(2)}) collective-permute-start(bf16[16,8,640]{2,1,0:T(8,128)(2,1)} %get-tuple-element.24), channel_id=1, source_target_pairs={{0,8},{1,9},{2,10},{3,11},{4,12},{5,13},{6,14},{7,15},{8,0},{9,1},... | collective-permute-start | bytes 491528 | tf_op jit(solution)/shard_map/ppermute | solution.py:35
  213.4 20.2 %collective-permute-start.9 = (bf16[16,8,640]{2,1,0:T(8,128)(2,1)}, bf16[16,8,640]{2,1,0:T(8,128)(2,1)S(1)}, u32[]{:S(2)}, u32[]{:S(2)}) collective-permute-start(bf16[16,8,640]{2,1,0:T(8,128)(2,1)} %get-tuple-element.25), channel_id=1, source_target_pairs={{0,12},{1,13},{2,14},{3,15},{4,0},{5,1},{6,2},{7,3},{8,4},{9,5},{1... | collective-permute-start | bytes 491528 | tf_op jit(solution)/shard_map/ppermute | solution.py:35
  217.9 24.3 %collective-permute-start.19 = (f32[80,128]{1,0:T(8,128)S(1)}, f32[80,128]{1,0:T(8,128)S(1)}, u32[]{:S(2)}, u32[]{:S(2)}) collective-permute-start(f32[80,128]{1,0:T(8,128)S(1)} %get-tuple-element.39), channel_id=1, source_target_pairs={{0,4},{1,5},{2,6},{3,7},{4,8},{5,9},{6,10},{7,11},{8,12},{9,13},{1... | collective-permute-start | bytes 122888 | tf_op jit(solution)/shard_map/ppermute | solution.py:35
  224.1 21.2 %collective-permute-start.21 = (f32[80,128]{1,0:T(8,128)S(1)}, f32[80,128]{1,0:T(8,128)S(1)}, u32[]{:S(2)}, u32[]{:S(2)}) collective-permute-start(f32[80,128]{1,0:T(8,128)S(1)} %get-tuple-element.40), channel_id=1, source_target_pairs={{0,12},{1,13},{2,14},{3,15},{4,0},{5,1},{6,2},{7,3},{8,4},{9,5},{1... | collective-permute-start | bytes 122888 | tf_op jit(solution)/shard_map/ppermute | solution.py:35
  226.1 19.3 %collective-permute-start.20 = (f32[80,128]{1,0:T(8,128)S(1)}, f32[80,128]{1,0:T(8,128)S(1)}, u32[]{:S(2)}, u32[]{:S(2)}) collective-permute-start(f32[80,128]{1,0:T(8,128)S(1)} %get-tuple-element.41), channel_id=1, source_target_pairs={{0,8},{1,9},{2,10},{3,11},{4,12},{5,13},{6,14},{7,15},{8,0},{9,1},... | collective-permute-start | bytes 122888 | tf_op jit(solution)/shard_map/ppermute | solution.py:35
  230.5 31.1 %collective-permute-start.18 = (bf16[16,8,640]{2,1,0:T(8,128)(2,1)S(1)}, bf16[16,8,640]{2,1,0:T(8,128)(2,1)S(1)}, u32[]{:S(2)}, u32[]{:S(2)}) collective-permute-start(bf16[16,8,640]{2,1,0:T(8,128)(2,1)S(1)} %get-tuple-element.32), channel_id=1, source_target_pairs={{0,12},{1,13},{2,14},{3,15},{4,0},{5,1},{6,2},{7,3},{8,4},{9,5},{1... | collective-permute-start | bytes 491528 | tf_op jit(solution)/shard_map/ppermute | solution.py:35
  233.5 28.0 %collective-permute-start.17 = (bf16[16,8,640]{2,1,0:T(8,128)(2,1)S(1)}, bf16[16,8,640]{2,1,0:T(8,128)(2,1)S(1)}, u32[]{:S(2)}, u32[]{:S(2)}) collective-permute-start(bf16[16,8,640]{2,1,0:T(8,128)(2,1)S(1)} %get-tuple-element.33), channel_id=1, source_target_pairs={{0,8},{1,9},{2,10},{3,11},{4,12},{5,13},{6,14},{7,15},{8,0},{9,1},... | collective-permute-start | bytes 491528 | tf_op jit(solution)/shard_map/ppermute | solution.py:35
  237.6 24.0 %all-to-all-start.6 = ((bf16[16,8,2560]{2,1,0:T(8,128)(2,1)}), bf16[16,8,2560]{2,1,0:T(8,128)(2,1)S(1)}, u32[]{:S(2)}, u32[]{:S(2)}) async-start(bf16[16,8,2560]{2,1,0:T(8,128)(2,1)} %beside.3), calls=%async_computation.6 | async-start | bytes 1310720 | tf_op jit(solution)/shard_map/all_to_all | solution.py:39
  242.2 19.4 %collective-permute-start.16 = (bf16[16,8,640]{2,1,0:T(8,128)(2,1)S(1)}, bf16[16,8,640]{2,1,0:T(8,128)(2,1)S(1)}, u32[]{:S(2)}, u32[]{:S(2)}) collective-permute-start(bf16[16,8,640]{2,1,0:T(8,128)(2,1)S(1)} %get-tuple-element.34), channel_id=1, source_target_pairs={{0,4},{1,5},{2,6},{3,7},{4,8},{5,9},{6,10},{7,11},{8,12},{9,13},{1... | collective-permute-start | bytes 491528 | tf_op jit(solution)/shard_map/ppermute | solution.py:35
  245.4 15.5 %collective-permute-start.22 = (f32[80,64]{1,0:T(8,128)S(1)}, f32[80,64]{1,0:T(8,128)S(1)}, u32[]{:S(2)}, u32[]{:S(2)}) collective-permute-start(f32[80,64]{1,0:T(8,128)S(1)} %get-tuple-element.42), channel_id=1, source_target_pairs={{0,448},{1,449},{2,450},{3,451},{4,452},{5,453},{6,454},{7,455},{8... | collective-permute-start | bytes 61448 | tf_op jit(solution)/shard_map/ppermute | solution.py:35
  (30 other events, 218.6 us)

commit v3 on v0

v3 whole, which is shorter than its diff:
```python
import jax
import jax.numpy as jnp
from jax import lax
from jax.experimental import pallas as pl
from jax.experimental.pallas import tpu as pltpu
from jax.sharding import PartitionSpec as P

NX, NY, NZ = 4, 4, 4
N_PEER = NX * NY * NZ
N_SECTION = 8
PLANE = NX * NY
D = 5120
LATENT = 64
ROWS = 128
WIDE = 640
HALF = D // 2
OWN = D // N_PEER
PLANES = [[y * 16 + z * 4 + x for y in range(NY) for x in range(NX)] for z in range(NZ)]
BF16, F32 = jnp.bfloat16, jnp.float32
SMEM = pl.BlockSpec(memory_space=pltpu.SMEM)
VMEM = pl.BlockSpec(memory_space=pltpu.VMEM)
ROOM = pltpu.CompilerParams(vmem_limit_bytes=16 * 1024 * 1024)
LAST = (((1,), (1,)), ((), ()))


def along(value, section_steps, z_steps=0):
    pairs = []
    for s in range(N_SECTION):
        for y in range(NY):
            for z in range(NZ):
                for x in range(NX):
                    source = s * N_PEER + y * 16 + z * 4 + x
                    target = ((s + section_steps) % N_SECTION) * N_PEER + y * 16 + ((z + z_steps) % NZ) * 4 + x
                    pairs.append((source, target))
    return lax.ppermute(value, ("section", "peer"), pairs)


def in_plane(value):
    return lax.all_to_all(value, "peer", split_axis=0, concat_axis=0, tiled=True, axis_index_groups=PLANES)


def in_cube(value):
    return lax.all_to_all(value, "peer", split_axis=0, concat_axis=0, tiled=True)


def shape(dims, kind=BF16):
    return jax.ShapeDtypeStruct(dims, kind)


def sigmoid(value):
    return 1.0 / (1.0 + jnp.exp(-value))


def pack_kernel(rows_ref, gain_ref, match_ref, out_ref):
    gain = gain_ref[...]
    high = gain.astype(BF16).astype(F32)
    middle = (gain - high).astype(BF16).astype(F32)
    row = lax.broadcasted_iota(jnp.int32, (8, D), 0)
    rest = jnp.zeros((8, D), F32)
    for at, value in enumerate((high, middle, gain - high - middle, match_ref[...])):
        rest = jnp.where(row == at, value, rest)
    out_ref[...] = jnp.concatenate([rows_ref[...].astype(F32), rest], axis=0).astype(BF16)


def pack(rows, gain_row, match_row):
    return pl.pallas_call(
        pack_kernel,
        out_shape=shape((16, D)),
        in_specs=[VMEM] * 3,
        out_specs=VMEM,
        compiler_params=ROOM,
        name="pack",
    )(rows, gain_row, match_row)


def act_grad_kernel(grad_ref, both_ref, out_ref):
    out_ref[...] = lax.dot_general(grad_ref[...], both_ref[:, HALF:], LAST, preferred_element_type=F32)


def act_grad_of(held_grad, both):
    return pl.pallas_call(
        act_grad_kernel,
        out_shape=shape((ROWS, 2 * LATENT), F32),
        in_specs=[VMEM] * 2,
        out_specs=VMEM,
        compiler_params=ROOM,
        name="act_grad",
    )(held_grad, both)


def adapter_kernel(landed_ref, both_ref, packed_ref, grad_ref, act_grad_ref, out_ref, part_ref, normed_ref):
    def tokens(z, at):
        pieces = [landed_ref[y * 16 + z * 4 + x, :, at : at + WIDE].astype(F32) for y in range(NY) for x in range(NX)]
        return jnp.concatenate(pieces, axis=0)

    def weights(cols):
        return both_ref[:, HALF + cols.start : HALF + cols.stop]

    chunks = [(z, h * WIDE, slice(h * HALF + z * WIDE, h * HALF + (z + 1) * WIDE)) for h in range(2) for z in range(NZ)]
    squares = jnp.zeros((ROWS, 1), F32)
    for z, at, cols in chunks:
        t = tokens(z, at)
        squares += jnp.sum(t * t, axis=1, keepdims=True)
    inv_rms = lax.rsqrt(squares / D + 1e-05)
    product = jnp.zeros((ROWS, 2 * LATENT), F32)
    for z, at, cols in chunks:
        gain = jnp.sum(packed_ref[:, cols].astype(F32)[8:11], axis=0, keepdims=True)
        n = (tokens(z, at) * inv_rms * gain).astype(BF16)
        normed_ref[:, cols] = n
        product += lax.dot_general(n, weights(cols), LAST, preferred_element_type=F32)
    lane = lax.broadcasted_iota(jnp.int32, (ROWS, 2 * LATENT), 1)
    is_up = lax.rem(lane, 8) < 4
    preact = jnp.where(is_up, 0.0, product)
    q = sigmoid(preact)
    active = pltpu.roll(preact * q, 2 * LATENT - 4, 1)
    active = jnp.where(is_up, active, 0.0).astype(BF16)
    for z, at, cols in chunks:
        up = jnp.dot(active, weights(cols), preferred_element_type=F32)
        t = (tokens(z, at) + up)
        for g in range(PLANE):
            out_ref[g, :, cols] = t[g * 8 : (g + 1) * 8].astype(BF16)
    act_grad = pltpu.roll(act_grad_ref[...], 4, 1)
    pre_grad = jnp.where(is_up, 0.0, act_grad * q * (1.0 + preact * (1.0 - q)))
    down = pre_grad.T.astype(BF16)
    up = active.astype(F32).T.astype(BF16)
    for j in range(D // WIDE):
        cols = slice(j * WIDE, (j + 1) * WIDE)
        part = jnp.dot(down, normed_ref[:, cols], preferred_element_type=F32)
        part += jnp.dot(up, grad_ref[:, cols], preferred_element_type=F32)
        part = part.T.astype(BF16)
        for i in range(WIDE // OWN):
            p = j * (WIDE // OWN) + i
            y, z, x = p // 16, (p // 4) % 4, p % 4
            part_ref[y * NX + x, z * OWN : (z + 1) * OWN, :] = part[i * OWN : (i + 1) * OWN]


def adapter(landed, both, packed, held_grad, act_grad):
    return pl.pallas_call(
        adapter_kernel,
        out_shape=(shape((PLANE, 8, D)), shape((PLANE, NZ * OWN, 2 * LATENT))),
        in_specs=[VMEM] * 5,
        out_specs=[VMEM] * 2,
        scratch_shapes=[pltpu.VMEM((ROWS, D), BF16)],
        compiler_params=ROOM,
        name="adapter",
    )(landed, both, packed, held_grad, act_grad)


def turn_kernel(z_ref, a0, a1, a2, a3, spread_ref, packed_ref, a_ref, b0, b1, b2, b3):
    z = z_ref[0]
    for k, (part, out) in enumerate(zip((a0, a1, a2, a3), (b0, b1, b2, b3))):
        a_ref[:, :, k * WIDE : (k + 1) * WIDE] = part[...]
        at = pl.multiple_of(lax.rem(z + k, NZ) * WIDE, 128)
        out[...] = spread_ref[:, :, pl.ds(at, WIDE)]
    rows = packed_ref[...].astype(F32)[:8].astype(BF16)
    for g in range(PLANE):
        a_ref[g, :, HALF:] = rows


def turn(z_at, a_parts, spread_b, packed):
    return pl.pallas_call(
        turn_kernel,
        out_shape=[shape((PLANE, 8, HALF + D))] + [shape((PLANE, 8, WIDE))] * NZ,
        in_specs=[SMEM] + [VMEM] * (NZ + 2),
        out_specs=[VMEM] * (1 + NZ),
        compiler_params=ROOM,
        name="turn",
    )(z_at, *a_parts, spread_b, packed)


def route_kernel(z_ref, before_ref, a_ref, b0, b1, b2, b3, out_ref):
    z = z_ref[0]
    for k, b_ref in enumerate((b0, b1, b2, b3)):
        plane = lax.rem(z + NZ - k, NZ) * NX
        for xy in range(PLANE):
            q = before_ref[plane + (xy // NX) * 16 + xy % NX]
            out_ref[q, :, :WIDE] = a_ref[xy, :, k * WIDE : (k + 1) * WIDE]
            out_ref[q, :, WIDE:] = b_ref[xy]


def route(z_at, match_before, spread_a, b_parts):
    return pl.pallas_call(
        route_kernel,
        out_shape=shape((N_PEER, 8, 2 * WIDE)),
        in_specs=[SMEM] * 2 + [VMEM] * (1 + NZ),
        out_specs=VMEM,
        compiler_params=ROOM,
        name="route",
    )(z_at, match_before, spread_a, *b_parts)


def on_device(hidden_in, out_grad, gain, w_down, w_up, matching):
    tokens, held_grad = hidden_in[0], out_grad[0]
    down_rows, up_rows = w_down[0], w_up[0]
    peer = lax.axis_index("peer")
    z = (peer // NX) % NZ
    place = (peer // 16) * NX + peer % NX

    z_at = z.reshape(1)
    a_out = [lax.dynamic_slice_in_dim(tokens, ((z + k) % NZ) * WIDE, WIDE, 1) for k in range(NZ)]
    a_parts = [along(part.reshape(PLANE, 8, WIDE), 1, k) for k, part in enumerate(a_out)]
    spread_b = in_plane(tokens[:, HALF:].reshape(PLANE, 8, HALF))

    rows = lambda array: lax.dynamic_slice_in_dim(array, place * 4, 4, 0)
    match_wide = jnp.pad(matching.astype(F32), ((0, 0), (0, D - N_PEER)))
    packed = along(pack(jnp.concatenate([rows(up_rows), rows(down_rows)], axis=0), gain, match_wide), 1)
    match_before = packed[11, :N_PEER].astype(jnp.int32)

    a_turned, *b_out = turn(z_at, a_parts, spread_b, packed)
    b_parts = [along(part, 1, k) for k, part in enumerate(b_out)]
    spread_a = in_plane(a_turned)
    both = spread_a.reshape(ROWS, HALF + D)
    act_grad = act_grad_of(held_grad, both)

    landed = in_cube(route(z_at, match_before, spread_a, b_parts))
    act_out, part = adapter(landed, both, packed, held_grad, act_grad)

    part = in_plane(part)
    plane_sum = jnp.sum(part.astype(F32), axis=0).reshape(NZ, OWN, 2 * LATENT)
    total = 0.0
    for k in range(NZ):
        chunk = lax.dynamic_index_in_dim(plane_sum, (z + k) % NZ, 0, keepdims=False)
        total = total + along(chunk, -1, k)
    total = total.T.reshape(PLANE, 2, 4, OWN)
    grad_up = total[:, 0].reshape(LATENT, OWN)
    grad_down = total[:, 1].reshape(LATENT, OWN)
    own = lambda array: lax.dynamic_slice_in_dim(array, peer * OWN, OWN, 1)
    grad_gain = jnp.sum(own(down_rows).astype(F32) * grad_down, axis=0, keepdims=True) / own(gain)
    return act_out.reshape(1, ROWS, D), grad_down[None], grad_up[None], grad_gain


def solution(mesh):
    placed = (
        P("section", "peer", None),
        P("section", "peer", None),
        P("section", None),
        P("section", None, None),
        P("section", None, None),
        P("section", None),
    )
    return jax.shard_map(
        on_device,
        mesh=mesh,
        in_specs=placed,
        out_specs=(
            P("section", "peer", None),
            P("section", None, "peer"),
            P("section", None, "peer"),
            P("section", "peer"),
        ),
        check_vma=False,
    )
```

time: 966 us -> 201 us (0.21)
  the two profiles are of different devices: /device:TPU:128 before, /device:TPU:1 now
where the time goes in v3:
time: 201 us; the launch traced here: 198 us
  starting transfers between devices  104 us (52%)
  waiting for transfers between devices  78.8 us (39%)
  local copies, waits for them, and re-layouts  7.57 us (4%)
  Pallas kernels  5.3 us (3%)
    ppermute x13, starting transfers between devices, along(): return lax.ppermute(value, ('section', 'peer'), pairs)  73.1 us
    all_to_all x1, waiting for transfers between devices, in_cube(): lax.all_to_all(value, 'peer', split_axis=0, concat_axis=0, tiled=True)  32.8 us
    ppermute x13, waiting for transfers between devices, along(): return lax.ppermute(value, ('section', 'peer'), pairs)  28.4 us
    all_to_all x3, starting transfers between devices, in_plane(): lax.all_to_all(value, 'peer', split_axis=0, concat_axis=0, tiled=True, ax...  18 us
    all_to_all x3, waiting for transfers between devices, in_plane(): lax.all_to_all(value, 'peer', split_axis=0, concat_axis=0, tiled=True, ax...  17.5 us
    all_to_all x1, starting transfers between devices, in_cube(): lax.all_to_all(value, 'peer', split_axis=0, concat_axis=0, tiled=True)  12.4 us
  transfers between devices with their start and end apart: 17, of which 10 were waited for; matrix products, arithmetic and copies ran while one was open for 1% of the time, Pallas kernels for 0%

profile of v3, /device:TPU:1, one launch (start us, length us, event | category | flops | bytes accessed | tf_op | source)
XLA Modules:
  0.0 197.8 jit_solution(14139539904388808763)
XLA Ops:
  0.8 1.3 dynamic-slice_bitcast_fusion
  2.1 10.2 %collective-permute-start.1 = (bf16[16,8,640]{2,1,0:T(8,128)(2,1)S(1)}, bf16[16,8,640]{2,1,0:T(8,128)(2,1)S(1)}, u32[]{:S(2)}, u32[]{:S(2)}) collective-permute-start(bf16[16,8,640]{2,1,0:T(8,128)(2,1)S(1)} %get-tuple-element.21), channel_id=1, source_target_pairs={{0,64},{1,65},{2,66},{3,67},{4,68},{5,69},{6,70},{7,71},{8,72},{9,... | collective-permute-start | bytes 491528 | tf_op jit(solution)/shard_map/ppermute | solution.py:35
  12.3 3.3 %collective-permute-start.2 = (bf16[16,8,640]{2,1,0:T(8,128)(2,1)S(1)}, bf16[16,8,640]{2,1,0:T(8,128)(2,1)S(1)}, u32[]{:S(2)}, u32[]{:S(2)}) collective-permute-start(bf16[16,8,640]{2,1,0:T(8,128)(2,1)S(1)} %get-tuple-element.20), channel_id=1, source_target_pairs={{0,68},{1,69},{2,70},{3,71},{4,72},{5,73},{6,74},{7,75},{8,76},{9,... | collective-permute-start | bytes 491528 | tf_op jit(solution)/shard_map/ppermute | solution.py:35
  15.6 9.4 %collective-permute-start.3 = (bf16[16,8,640]{2,1,0:T(8,128)(2,1)S(1)}, bf16[16,8,640]{2,1,0:T(8,128)(2,1)S(1)}, u32[]{:S(2)}, u32[]{:S(2)}) collective-permute-start(bf16[16,8,640]{2,1,0:T(8,128)(2,1)S(1)} %get-tuple-element.19), channel_id=1, source_target_pairs={{0,72},{1,73},{2,74},{3,75},{4,76},{5,77},{6,78},{7,79},{8,64},{9,... | collective-permute-start | bytes 491528 | tf_op jit(solution)/shard_map/ppermute | solution.py:35
  24.9 3.3 %collective-permute-start.4 = (bf16[16,8,640]{2,1,0:T(8,128)(2,1)S(1)}, bf16[16,8,640]{2,1,0:T(8,128)(2,1)S(1)}, u32[]{:S(2)}, u32[]{:S(2)}) collective-permute-start(bf16[16,8,640]{2,1,0:T(8,128)(2,1)S(1)} %get-tuple-element.18), channel_id=1, source_target_pairs={{0,76},{1,77},{2,78},{3,79},{4,64},{5,65},{6,66},{7,67},{8,68},{9,... | collective-permute-start | bytes 491528 | tf_op jit(solution)/shard_map/ppermute | solution.py:35
  29.1 6.8 %all-to-all-start = ((bf16[16,8,2560]{2,1,0:T(8,128)(2,1)}), bf16[16,8,2560]{2,1,0:T(8,128)(2,1)S(1)}, u32[]{:S(2)}, u32[]{:S(2)}) async-start(bf16[16,8,2560]{2,1,0:T(8,128)(2,1)} %slice_bitcast_fusion), calls=%async_computation | async-start | bytes 1310720 | tf_op jit(solution)/shard_map/all_to_all | solution.py:39
  35.9 1.0 dynamic-slice_bitcast_fusion.8
  37.1 3.0 %collective-permute-start = (bf16[16,5120]{1,0:T(8,128)(2,1)S(1)}, bf16[16,5120]{1,0:T(8,128)(2,1)S(1)}, u32[]{:S(2)}, u32[]{:S(2)}) collective-permute-start(bf16[16,5120]{1,0:T(8,128)(2,1)S(1)} %pack.1), channel_id=1, source_target_pairs={{0,64},{1,65},{2,66},{3,67},{4,68},{5,69},{6,70},{7,71},{8,72},{9,... | collective-permute-start | bytes 491528 | tf_op jit(solution)/shard_map/ppermute | solution.py:35
  40.6 5.9 %collective-permute-done.4.a3 = bf16[16,8,640]{2,1,0:T(8,128)(2,1)S(1)} collective-permute-done((bf16[16,8,640]{2,1,0:T(8,128)(2,1)S(1)}, bf16[16,8,640]{2,1,0:T(8,128)(2,1)S(1)}, u32[]{:S(2)}, u32[]{:S(2)}) %collective-permute-start.4) | collective-permute-done | bytes 163872 | tf_op jit(solution)/shard_map/ppermute | solution.py:35
  46.6 4.2 %collective-permute-done.packed_ref = bf16[16,5120]{1,0:T(8,128)(2,1)S(1)} collective-permute-done((bf16[16,5120]{1,0:T(8,128)(2,1)S(1)}, bf16[16,5120]{1,0:T(8,128)(2,1)S(1)}, u32[]{:S(2)}, u32[]{:S(2)}) %collective-permute-start) | collective-permute-done | bytes 163872 | tf_op jit(solution)/shard_map/ppermute | solution.py:35
  50.9 1.3 copy-done.2
  52.2 7.5 %all-to-all-start.1 = ((bf16[16,8,7680]{2,1,0:T(8,128)(2,1)}), bf16[16,8,7680]{2,1,0:T(8,128)(2,1)S(1)}, u32[]{:S(2)}, u32[]{:S(2)}) async-start(bf16[16,8,7680]{2,1,0:T(8,128)(2,1)} %copy-done.2), calls=%async_computation.1 | async-start | bytes 3932160 | tf_op jit(solution)/shard_map/all_to_all | solution.py:39
  59.8 10.3 %collective-permute-start.5 = (bf16[16,8,640]{2,1,0:T(8,128)(2,1)S(1)}, bf16[16,8,640]{2,1,0:T(8,128)(2,1)S(1)}, u32[]{:S(2)}, u32[]{:S(2)}) collective-permute-start(bf16[16,8,640]{2,1,0:T(8,128)(2,1)S(1)} %get-tuple-element.12), channel_id=1, source_target_pairs={{0,64},{1,65},{2,66},{3,67},{4,68},{5,69},{6,70},{7,71},{8,72},{9,... | collective-permute-start | bytes 491528 | tf_op jit(solution)/shard_map/ppermute | solution.py:35
  70.0 4.7 %collective-permute-start.6 = (bf16[16,8,640]{2,1,0:T(8,128)(2,1)S(1)}, bf16[16,8,640]{2,1,0:T(8,128)(2,1)S(1)}, u32[]{:S(2)}, u32[]{:S(2)}) collective-permute-start(bf16[16,8,640]{2,1,0:T(8,128)(2,1)S(1)} %get-tuple-element.13), channel_id=1, source_target_pairs={{0,68},{1,69},{2,70},{3,71},{4,72},{5,73},{6,74},{7,75},{8,76},{9,... | collective-permute-start | bytes 491528 | tf_op jit(solution)/shard_map/ppermute | solution.py:35
  74.7 5.6 %collective-permute-start.7 = (bf16[16,8,640]{2,1,0:T(8,128)(2,1)S(1)}, bf16[16,8,640]{2,1,0:T(8,128)(2,1)S(1)}, u32[]{:S(2)}, u32[]{:S(2)}) collective-permute-start(bf16[16,8,640]{2,1,0:T(8,128)(2,1)S(1)} %get-tuple-element.14), channel_id=1, source_target_pairs={{0,72},{1,73},{2,74},{3,75},{4,76},{5,77},{6,78},{7,79},{8,64},{9,... | collective-permute-start | bytes 491528 | tf_op jit(solution)/shard_map/ppermute | solution.py:35
  80.3 6.8 %collective-permute-start.8 = (bf16[16,8,640]{2,1,0:T(8,128)(2,1)S(1)}, bf16[16,8,640]{2,1,0:T(8,128)(2,1)S(1)}, u32[]{:S(2)}, u32[]{:S(2)}) collective-permute-start(bf16[16,8,640]{2,1,0:T(8,128)(2,1)S(1)} %get-tuple-element.15), channel_id=1, source_target_pairs={{0,76},{1,77},{2,78},{3,79},{4,64},{5,65},{6,66},{7,67},{8,68},{9,... | collective-permute-start | bytes 491528 | tf_op jit(solution)/shard_map/ppermute | solution.py:35
  87.2 9.0 %collective-permute-done.7.b2 = bf16[16,8,640]{2,1,0:T(8,128)(2,1)S(1)} collective-permute-done((bf16[16,8,640]{2,1,0:T(8,128)(2,1)S(1)}, bf16[16,8,640]{2,1,0:T(8,128)(2,1)S(1)}, u32[]{:S(2)}, u32[]{:S(2)}) %collective-permute-start.7) | collective-permute-done | bytes 163872 | tf_op jit(solution)/shard_map/ppermute | solution.py:35
  96.2 5.0 %collective-permute-done.8.b3 = bf16[16,8,640]{2,1,0:T(8,128)(2,1)S(1)} collective-permute-done((bf16[16,8,640]{2,1,0:T(8,128)(2,1)S(1)}, bf16[16,8,640]{2,1,0:T(8,128)(2,1)S(1)}, u32[]{:S(2)}, u32[]{:S(2)}) %collective-permute-start.8) | collective-permute-done | bytes 163872 | tf_op jit(solution)/shard_map/ppermute | solution.py:35
  101.9 1.0 copy-done.1
  103.0 12.4 %all-to-all-start.2 = ((bf16[64,8,1280]{2,1,0:T(8,128)(2,1)}), bf16[64,8,1280]{2,1,0:T(8,128)(2,1)}, u32[]{:S(2)}, u32[]{:S(2)}) async-start(bf16[64,8,1280]{2,1,0:T(8,128)(2,1)} %copy-done.1), calls=%async_computation.2 | async-start | bytes 2621440 | tf_op jit(solution)/shard_map/all_to_all | solution.py:43
  115.9 32.8 %all-to-all-done.2.landed_ref = bf16[64,8,1280]{2,1,0:T(8,128)(2,1)} async-done(((bf16[64,8,1280]{2,1,0:T(8,128)(2,1)}), bf16[64,8,1280]{2,1,0:T(8,128)(2,1)}, u32[]{:S(2)}, u32[]{:S(2)}) %all-to-all-start.2) | async-done | bytes 1310752 | tf_op jit(solution)/shard_map/all_to_all | solution.py:43
  148.8 3.9 %adapter.1 = (bf16[16,8,5120]{2,1,0:T(8,128)(2,1)}, bf16[16,320,128]{2,1,0:T(8,128)(2,1)S(1)}) custom-call(bf16[64,8,1280]{2,1,0:T(8,128)(2,1)} %all-to-all-done.2.landed_ref, bf16[128,7680]{1,0:T(8,128)(2,1)S(1)} %bitcast.43, bf16[16,5120]{1,0:T(8,128)(2,1)S(1)} %collective-permute-done.packed_ref, bf16[128,5120]{1,0:T(8,128)(2,1)S(1)} %bitcast.45, ...), custom_call_target="tpu_custom_call" | custom-call | tf_op jit(solution)/shard_map/adapter/pallas_call | solution.py:138
  152.6 1.1 copy-done.3
  153.7 3.7 %all-to-all-start.3 = ((bf16[16,320,128]{2,1,0:T(8,128)(2,1)}), bf16[16,320,128]{2,1,0:T(8,128)(2,1)S(1)}, u32[]{:S(2)}, u32[]{:S(2)}) async-start(bf16[16,320,128]{2,1,0:T(8,128)(2,1)} %copy-done.3), calls=%async_computation.3 | async-start | bytes 2621440 | tf_op jit(solution)/shard_map/all_to_all | solution.py:39
  157.4 17.5 %all-to-all-done.3 = bf16[16,320,128]{2,1,0:T(8,128)(2,1)S(1)} async-done(((bf16[16,320,128]{2,1,0:T(8,128)(2,1)}), bf16[16,320,128]{2,1,0:T(8,128)(2,1)S(1)}, u32[]{:S(2)}, u32[]{:S(2)}) %all-to-all-start.3) | async-done | bytes 1310752 | tf_op jit(solution)/shard_map/all_to_all | solution.py:39
  175.1 5.5 %collective-permute-start.10 = (f32[80,128]{1,0:T(8,128)S(1)}, f32[80,128]{1,0:T(8,128)S(1)}, u32[]{:S(2)}, u32[]{:S(2)}) collective-permute-start(f32[80,128]{1,0:T(8,128)S(1)} %get-tuple-element.22), channel_id=1, source_target_pairs={{0,452},{1,453},{2,454},{3,455},{4,456},{5,457},{6,458},{7,459},{8... | collective-permute-start | bytes 122888 | tf_op jit(solution)/shard_map/ppermute | solution.py:35
  180.6 3.0 %collective-permute-start.11 = (f32[80,128]{1,0:T(8,128)S(1)}, f32[80,128]{1,0:T(8,128)S(1)}, u32[]{:S(2)}, u32[]{:S(2)}) collective-permute-start(f32[80,128]{1,0:T(8,128)S(1)} %get-tuple-element.24), channel_id=1, source_target_pairs={{0,456},{1,457},{2,458},{3,459},{4,460},{5,461},{6,462},{7,463},{8... | collective-permute-start | bytes 122888 | tf_op jit(solution)/shard_map/ppermute | solution.py:35
  183.6 2.9 %collective-permute-start.12 = (f32[80,128]{1,0:T(8,128)S(1)}, f32[80,128]{1,0:T(8,128)S(1)}, u32[]{:S(2)}, u32[]{:S(2)}) collective-permute-start(f32[80,128]{1,0:T(8,128)S(1)} %get-tuple-element.23), channel_id=1, source_target_pairs={{0,460},{1,461},{2,462},{3,463},{4,448},{5,449},{6,450},{7,451},{8... | collective-permute-start | bytes 122888 | tf_op jit(solution)/shard_map/ppermute | solution.py:35
  186.6 5.2 %collective-permute-start.9 = (f32[80,128]{1,0:T(8,128)S(1)}, f32[80,128]{1,0:T(8,128)S(1)}, u32[]{:S(2)}, u32[]{:S(2)}) collective-permute-start(f32[80,128]{1,0:T(8,128)S(1)} %get-tuple-element.25), channel_id=1, source_target_pairs={{0,448},{1,449},{2,450},{3,451},{4,452},{5,453},{6,454},{7,455},{8... | collective-permute-start | bytes 122888 | tf_op jit(solution)/shard_map/ppermute | solution.py:35
  192.6 1.2 collective-permute-done.11
  193.8 1.4 collective-permute-done.12
  195.2 1.3 collective-permute-done.9
  (35 shorter events, 5.3 us)
Async XLA Ops:
  0.6 27.6 %copy-start.5 = (bf16[1,128,5120]{2,1,0:T(8,128)(2,1)S(1)}, bf16[1,128,5120]{2,1,0:T(8,128)(2,1)}, u32[]{:S(2)}) copy-start(bf16[1,128,5120]{2,1,0:T(8,128)(2,1)} %param.6) | copy-start | bytes 3932164
  2.1 38.1 %collective-permute-start.1 = (bf16[16,8,640]{2,1,0:T(8,128)(2,1)S(1)}, bf16[16,8,640]{2,1,0:T(8,128)(2,1)S(1)}, u32[]{:S(2)}, u32[]{:S(2)}) collective-permute-start(bf16[16,8,640]{2,1,0:T(8,128)(2,1)S(1)} %get-tuple-element.21), channel_id=1, source_target_pairs={{0,64},{1,65},{2,66},{3,67},{4,68},{5,69},{6,70},{7,71},{8,72},{9,... | collective-permute-start | bytes 491528 | tf_op jit(solution)/shard_map/ppermute | solution.py:35
  12.3 27.9 %collective-permute-start.2 = (bf16[16,8,640]{2,1,0:T(8,128)(2,1)S(1)}, bf16[16,8,640]{2,1,0:T(8,128)(2,1)S(1)}, u32[]{:S(2)}, u32[]{:S(2)}) collective-permute-start(bf16[16,8,640]{2,1,0:T(8,128)(2,1)S(1)} %get-tuple-element.20), channel_id=1, source_target_pairs={{0,68},{1,69},{2,70},{3,71},{4,72},{5,73},{6,74},{7,75},{8,76},{9,... | collective-permute-start | bytes 491528 | tf_op jit(solution)/shard_map/ppermute | solution.py:35
  15.6 25.1 %collective-permute-start.3 = (bf16[16,8,640]{2,1,0:T(8,128)(2,1)S(1)}, bf16[16,8,640]{2,1,0:T(8,128)(2,1)S(1)}, u32[]{:S(2)}, u32[]{:S(2)}) collective-permute-start(bf16[16,8,640]{2,1,0:T(8,128)(2,1)S(1)} %get-tuple-element.19), channel_id=1, source_target_pairs={{0,72},{1,73},{2,74},{3,75},{4,76},{5,77},{6,78},{7,79},{8,64},{9,... | collective-permute-start | bytes 491528 | tf_op jit(solution)/shard_map/ppermute | solution.py:35
  24.9 21.6 %collective-permute-start.4 = (bf16[16,8,640]{2,1,0:T(8,128)(2,1)S(1)}, bf16[16,8,640]{2,1,0:T(8,128)(2,1)S(1)}, u32[]{:S(2)}, u32[]{:S(2)}) collective-permute-start(bf16[16,8,640]{2,1,0:T(8,128)(2,1)S(1)} %get-tuple-element.18), channel_id=1, source_target_pairs={{0,76},{1,77},{2,78},{3,79},{4,64},{5,65},{6,66},{7,67},{8,68},{9,... | collective-permute-start | bytes 491528 | tf_op jit(solution)/shard_map/ppermute | solution.py:35
  28.2 7.7 %copy-start.6 = (s32[1,64]{1,0:T(1,128)S(1)}, s32[1,64]{1,0:T(1,128)}, u32[]{:S(2)}) copy-start(s32[1,64]{1,0:T(1,128)} %param.11) | copy-start | bytes 772
  28.2 8.8 %copy-start.4 = (f32[1,5120]{1,0:T(1,128)S(1)}, f32[1,5120]{1,0:T(1,128)}, u32[]{:S(2)}) copy-start(f32[1,5120]{1,0:T(1,128)} %gain_ref.1) | copy-start | bytes 61444
  29.1 21.6 %all-to-all-start = ((bf16[16,8,2560]{2,1,0:T(8,128)(2,1)}), bf16[16,8,2560]{2,1,0:T(8,128)(2,1)S(1)}, u32[]{:S(2)}, u32[]{:S(2)}) async-start(bf16[16,8,2560]{2,1,0:T(8,128)(2,1)} %slice_bitcast_fusion), calls=%async_computation | async-start | bytes 1310720 | tf_op jit(solution)/shard_map/all_to_all | solution.py:39
  37.1 13.6 %collective-permute-start = (bf16[16,5120]{1,0:T(8,128)(2,1)S(1)}, bf16[16,5120]{1,0:T(8,128)(2,1)S(1)}, u32[]{:S(2)}, u32[]{:S(2)}) collective-permute-start(bf16[16,5120]{1,0:T(8,128)(2,1)S(1)} %pack.1), channel_id=1, source_target_pairs={{0,64},{1,65},{2,66},{3,67},{4,68},{5,69},{6,70},{7,71},{8,72},{9,... | collective-permute-start | bytes 491528 | tf_op jit(solution)/shard_map/ppermute | solution.py:35
  50.9 1.3 copy-start.2
  52.2 49.0 %all-to-all-start.1 = ((bf16[16,8,7680]{2,1,0:T(8,128)(2,1)}), bf16[16,8,7680]{2,1,0:T(8,128)(2,1)S(1)}, u32[]{:S(2)}, u32[]{:S(2)}) async-start(bf16[16,8,7680]{2,1,0:T(8,128)(2,1)} %copy-done.2), calls=%async_computation.1 | async-start | bytes 3932160 | tf_op jit(solution)/shard_map/all_to_all | solution.py:39
  59.8 27.4 %collective-permute-start.5 = (bf16[16,8,640]{2,1,0:T(8,128)(2,1)S(1)}, bf16[16,8,640]{2,1,0:T(8,128)(2,1)S(1)}, u32[]{:S(2)}, u32[]{:S(2)}) collective-permute-start(bf16[16,8,640]{2,1,0:T(8,128)(2,1)S(1)} %get-tuple-element.12), channel_id=1, source_target_pairs={{0,64},{1,65},{2,66},{3,67},{4,68},{5,69},{6,70},{7,71},{8,72},{9,... | collective-permute-start | bytes 491528 | tf_op jit(solution)/shard_map/ppermute | solution.py:35
  70.0 17.2 %collective-permute-start.6 = (bf16[16,8,640]{2,1,0:T(8,128)(2,1)S(1)}, bf16[16,8,640]{2,1,0:T(8,128)(2,1)S(1)}, u32[]{:S(2)}, u32[]{:S(2)}) collective-permute-start(bf16[16,8,640]{2,1,0:T(8,128)(2,1)S(1)} %get-tuple-element.13), channel_id=1, source_target_pairs={{0,68},{1,69},{2,70},{3,71},{4,72},{5,73},{6,74},{7,75},{8,76},{9,... | collective-permute-start | bytes 491528 | tf_op jit(solution)/shard_map/ppermute | solution.py:35
  74.7 21.5 %collective-permute-start.7 = (bf16[16,8,640]{2,1,0:T(8,128)(2,1)S(1)}, bf16[16,8,640]{2,1,0:T(8,128)(2,1)S(1)}, u32[]{:S(2)}, u32[]{:S(2)}) collective-permute-start(bf16[16,8,640]{2,1,0:T(8,128)(2,1)S(1)} %get-tuple-element.14), channel_id=1, source_target_pairs={{0,72},{1,73},{2,74},{3,75},{4,76},{5,77},{6,78},{7,79},{8,64},{9,... | collective-permute-start | bytes 491528 | tf_op jit(solution)/shard_map/ppermute | solution.py:35
  80.3 20.9 %collective-permute-start.8 = (bf16[16,8,640]{2,1,0:T(8,128)(2,1)S(1)}, bf16[16,8,640]{2,1,0:T(8,128)(2,1)S(1)}, u32[]{:S(2)}, u32[]{:S(2)}) collective-permute-start(bf16[16,8,640]{2,1,0:T(8,128)(2,1)S(1)} %get-tuple-element.15), channel_id=1, source_target_pairs={{0,76},{1,77},{2,78},{3,79},{4,64},{5,65},{6,66},{7,67},{8,68},{9,... | collective-permute-start | bytes 491528 | tf_op jit(solution)/shard_map/ppermute | solution.py:35
  101.9 1.1 copy-start.1
  103.0 12.5 %copy-start = (bf16[1,128,5120]{2,1,0:T(8,128)(2,1)S(1)}, bf16[1,128,5120]{2,1,0:T(8,128)(2,1)}, u32[]{:S(2)}) copy-start(bf16[1,128,5120]{2,1,0:T(8,128)(2,1)} %param.7) | copy-start | bytes 3932164
  103.0 45.8 %all-to-all-start.2 = ((bf16[64,8,1280]{2,1,0:T(8,128)(2,1)}), bf16[64,8,1280]{2,1,0:T(8,128)(2,1)}, u32[]{:S(2)}, u32[]{:S(2)}) async-start(bf16[64,8,1280]{2,1,0:T(8,128)(2,1)} %copy-done.1), calls=%async_computation.2 | async-start | bytes 2621440 | tf_op jit(solution)/shard_map/all_to_all | solution.py:43
  152.6 1.1 copy-start.3
  153.7 21.2 %all-to-all-start.3 = ((bf16[16,320,128]{2,1,0:T(8,128)(2,1)}), bf16[16,320,128]{2,1,0:T(8,128)(2,1)S(1)}, u32[]{:S(2)}, u32[]{:S(2)}) async-start(bf16[16,320,128]{2,1,0:T(8,128)(2,1)} %copy-done.3), calls=%async_computation.3 | async-start | bytes 2621440 | tf_op jit(solution)/shard_map/all_to_all | solution.py:39
  175.1 17.5 %collective-permute-start.10 = (f32[80,128]{1,0:T(8,128)S(1)}, f32[80,128]{1,0:T(8,128)S(1)}, u32[]{:S(2)}, u32[]{:S(2)}) collective-permute-start(f32[80,128]{1,0:T(8,128)S(1)} %get-tuple-element.22), channel_id=1, source_target_pairs={{0,452},{1,453},{2,454},{3,455},{4,456},{5,457},{6,458},{7,459},{8... | collective-permute-start | bytes 122888 | tf_op jit(solution)/shard_map/ppermute | solution.py:35
  180.6 13.1 %collective-permute-start.11 = (f32[80,128]{1,0:T(8,128)S(1)}, f32[80,128]{1,0:T(8,128)S(1)}, u32[]{:S(2)}, u32[]{:S(2)}) collective-permute-start(f32[80,128]{1,0:T(8,128)S(1)} %get-tuple-element.24), channel_id=1, source_target_pairs={{0,456},{1,457},{2,458},{3,459},{4,460},{5,461},{6,462},{7,463},{8... | collective-permute-start | bytes 122888 | tf_op jit(solution)/shard_map/ppermute | solution.py:35
  183.6 11.6 %collective-permute-start.12 = (f32[80,128]{1,0:T(8,128)S(1)}, f32[80,128]{1,0:T(8,128)S(1)}, u32[]{:S(2)}, u32[]{:S(2)}) collective-permute-start(f32[80,128]{1,0:T(8,128)S(1)} %get-tuple-element.23), channel_id=1, source_target_pairs={{0,460},{1,461},{2,462},{3,463},{4,448},{5,449},{6,450},{7,451},{8... | collective-permute-start | bytes 122888 | tf_op jit(solution)/shard_map/ppermute | solution.py:35
  186.6 9.9 %collective-permute-start.9 = (f32[80,128]{1,0:T(8,128)S(1)}, f32[80,128]{1,0:T(8,128)S(1)}, u32[]{:S(2)}, u32[]{:S(2)}) collective-permute-start(f32[80,128]{1,0:T(8,128)S(1)} %get-tuple-element.25), channel_id=1, source_target_pairs={{0,448},{1,449},{2,450},{3,451},{4,452},{5,453},{6,454},{7,455},{8... | collective-permute-start | bytes 122888 | tf_op jit(solution)/shard_map/ppermute | solution.py:35

commit v4 on v3

--- a/solution.py
+++ b/solution.py
@@ -13,7 +13,9 @@
 LATENT = 64
 ROWS = 128
 WIDE = 640
-HALF = D // 2
+SPAN = D // NZ
+HALF = 2 * SPAN
+LEAD = 10**11
 OWN = D // N_PEER
 PLANES = [[y * 16 + z * 4 + x for y in range(NY) for x in range(NX)] for z in range(NZ)]
 BF16, F32 = jnp.bfloat16, jnp.float32
@@ -88,37 +90,37 @@
     )(held_grad, both)
 
 
-def adapter_kernel(landed_ref, both_ref, packed_ref, grad_ref, act_grad_ref, out_ref, part_ref, normed_ref):
-    def tokens(z, at):
-        pieces = [landed_ref[y * 16 + z * 4 + x, :, at : at + WIDE].astype(F32) for y in range(NY) for x in range(NX)]
-        return jnp.concatenate(pieces, axis=0)
-
-    def weights(cols):
-        return both_ref[:, HALF + cols.start : HALF + cols.stop]
-
-    chunks = [(z, h * WIDE, slice(h * HALF + z * WIDE, h * HALF + (z + 1) * WIDE)) for h in range(2) for z in range(NZ)]
+def landed_rows(landed_ref, z, at):
+    pieces = [landed_ref[y * 16 + z * 4 + x, :, at : at + WIDE].astype(F32) for y in range(NY) for x in range(NX)]
+    return jnp.concatenate(pieces, axis=0)
+
+
+CHUNKS = [(z, at, slice(z * SPAN + at, z * SPAN + at + WIDE)) for z in range(NZ) for at in range(0, SPAN, WIDE)]
+
+
+def weights(both_ref, cols):
+    return both_ref[:, HALF + cols.start : HALF + cols.stop]
+
+
+def adapter_kernel(landed_ref, both_ref, packed_ref, grad_ref, act_grad_ref, active_ref, part_ref, normed_ref):
     squares = jnp.zeros((ROWS, 1), F32)
-    for z, at, cols in chunks:
-        t = tokens(z, at)
+    for z, at, cols in CHUNKS:
+        t = landed_rows(landed_ref, z, at)
         squares += jnp.sum(t * t, axis=1, keepdims=True)
     inv_rms = lax.rsqrt(squares / D + 1e-05)
     product = jnp.zeros((ROWS, 2 * LATENT), F32)
-    for z, at, cols in chunks:
+    for z, at, cols in CHUNKS:
         gain = jnp.sum(packed_ref[:, cols].astype(F32)[8:11], axis=0, keepdims=True)
-        n = (tokens(z, at) * inv_rms * gain).astype(BF16)
+        n = (landed_rows(landed_ref, z, at) * inv_rms * gain).astype(BF16)
         normed_ref[:, cols] = n
-        product += lax.dot_general(n, weights(cols), LAST, preferred_element_type=F32)
+        product += lax.dot_general(n, weights(both_ref, cols), LAST, preferred_element_type=F32)
     lane = lax.broadcasted_iota(jnp.int32, (ROWS, 2 * LATENT), 1)
     is_up = lax.rem(lane, 8) < 4
     preact = jnp.where(is_up, 0.0, product)
     q = sigmoid(preact)
     active = pltpu.roll(preact * q, 2 * LATENT - 4, 1)
     active = jnp.where(is_up, active, 0.0).astype(BF16)
-    for z, at, cols in chunks:
-        up = jnp.dot(active, weights(cols), preferred_element_type=F32)
-        t = (tokens(z, at) + up)
-        for g in range(PLANE):
-            out_ref[g, :, cols] = t[g * 8 : (g + 1) * 8].astype(BF16)
+    active_ref[...] = active
     act_grad = pltpu.roll(act_grad_ref[...], 4, 1)
     pre_grad = jnp.where(is_up, 0.0, act_grad * q * (1.0 + preact * (1.0 - q)))
     down = pre_grad.T.astype(BF16)
@@ -137,7 +139,7 @@
 def adapter(landed, both, packed, held_grad, act_grad):
     return pl.pallas_call(
         adapter_kernel,
-        out_shape=(shape((PLANE, 8, D)), shape((PLANE, NZ * OWN, 2 * LATENT))),
+        out_shape=(shape((ROWS, 2 * LATENT)), shape((PLANE, NZ * OWN, 2 * LATENT))),
         in_specs=[VMEM] * 5,
         out_specs=[VMEM] * 2,
         scratch_shapes=[pltpu.VMEM((ROWS, D), BF16)],
@@ -146,47 +148,114 @@
     )(landed, both, packed, held_grad, act_grad)
 
 
-def turn_kernel(z_ref, a0, a1, a2, a3, spread_ref, packed_ref, a_ref, b0, b1, b2, b3):
-    z = z_ref[0]
-    for k, (part, out) in enumerate(zip((a0, a1, a2, a3), (b0, b1, b2, b3))):
-        a_ref[:, :, k * WIDE : (k + 1) * WIDE] = part[...]
-        at = pl.multiple_of(lax.rem(z + k, NZ) * WIDE, 128)
-        out[...] = spread_ref[:, :, pl.ds(at, WIDE)]
+def finish_kernel(landed_ref, both_ref, active_ref, out_ref):
+    for z, at, cols in CHUNKS:
+        up = jnp.dot(active_ref[...], weights(both_ref, cols), preferred_element_type=F32)
+        t = landed_rows(landed_ref, z, at) + up
+        for g in range(PLANE):
+            out_ref[g, :, cols] = t[g * 8 : (g + 1) * 8].astype(BF16)
+
+
+def finish(landed, both, active):
+    return pl.pallas_call(
+        finish_kernel,
+        out_shape=shape((PLANE, 8, D)),
+        in_specs=[VMEM] * 3,
+        out_specs=VMEM,
+        compiler_params=ROOM,
+        name="finish",
+    )(landed, both, active)
+
+
+def beside_kernel(a0, a1, packed_ref, out_ref):
+    out_ref[:, :, :SPAN] = a0[...]
+    out_ref[:, :, SPAN:HALF] = a1[...]
     rows = packed_ref[...].astype(F32)[:8].astype(BF16)
     for g in range(PLANE):
-        a_ref[g, :, HALF:] = rows
-
-
-def turn(z_at, a_parts, spread_b, packed):
-    return pl.pallas_call(
-        turn_kernel,
-        out_shape=[shape((PLANE, 8, HALF + D))] + [shape((PLANE, 8, WIDE))] * NZ,
-        in_specs=[SMEM] + [VMEM] * (NZ + 2),
-        out_specs=[VMEM] * (1 + NZ),
-        compiler_params=ROOM,
-        name="turn",
-    )(z_at, *a_parts, spread_b, packed)
-
-
-def route_kernel(z_ref, before_ref, a_ref, b0, b1, b2, b3, out_ref):
+        out_ref[g, :, HALF:] = rows
+
+
+def beside(a_parts, packed):
+    return pl.pallas_call(
+        beside_kernel,
+        out_shape=shape((PLANE, 8, HALF + D)),
+        in_specs=[VMEM] * 3,
+        out_specs=VMEM,
+        compiler_params=ROOM,
+        name="beside",
+    )(*a_parts, packed)
+
+
+def seen_kernel(*refs):
+    refs[-1][...] = sum(ref[0, :, :128].astype(F32) for ref in refs[:-1])
+
+
+def seen(*values):
+    return pl.pallas_call(
+        seen_kernel,
+        out_shape=shape((8, 128), F32),
+        in_specs=[VMEM] * len(values),
+        out_specs=VMEM,
+        compiler_params=ROOM,
+        cost_estimate=pl.CostEstimate(flops=LEAD, bytes_accessed=0, transcendentals=0),
+        name="seen",
+    )(*values)
+
+
+def halves_kernel(spread_ref, after_ref, b0, b1):
+    b0[...] = spread_ref[:, :, :SPAN]
+    b1[...] = spread_ref[:, :, SPAN:]
+
+
+def halves(spread_b, after):
+    return pl.pallas_call(
+        halves_kernel,
+        out_shape=[shape((PLANE, 8, SPAN))] * 2,
+        in_specs=[VMEM] * 2,
+        out_specs=[VMEM] * 2,
+        compiler_params=ROOM,
+        name="halves",
+    )(spread_b, after)
+
+
+def route_kernel(z_ref, before_ref, a_ref, b0, b1, after_ref, out_ref):
     z = z_ref[0]
-    for k, b_ref in enumerate((b0, b1, b2, b3)):
+    for k in range(NZ):
         plane = lax.rem(z + NZ - k, NZ) * NX
         for xy in range(PLANE):
-            q = before_ref[plane + (xy // NX) * 16 + xy % NX]
-            out_ref[q, :, :WIDE] = a_ref[xy, :, k * WIDE : (k + 1) * WIDE]
-            out_ref[q, :, WIDE:] = b_ref[xy]
-
-
-def route(z_at, match_before, spread_a, b_parts):
+            piece = a_ref[xy, :, k * SPAN : (k + 1) * SPAN] if k < 2 else (b0, b1)[k - 2][xy]
+            out_ref[before_ref[plane + (xy // NX) * 16 + xy % NX]] = piece
+
+
+def route(z_at, match_before, spread_a, b_parts, after):
     return pl.pallas_call(
         route_kernel,
-        out_shape=shape((N_PEER, 8, 2 * WIDE)),
-        in_specs=[SMEM] * 2 + [VMEM] * (1 + NZ),
+        out_shape=shape((N_PEER, 8, SPAN)),
+        in_specs=[SMEM] * 2 + [VMEM] * 4,
         out_specs=VMEM,
         compiler_params=ROOM,
         name="route",
-    )(z_at, match_before, spread_a, *b_parts)
+    )(z_at, match_before, spread_a, *b_parts, after)
+
+
+def sums_kernel(p0, p1, p2, p3, down_rows_ref, gain_ref, down_ref, up_ref, grad_gain_ref):
+    total = (p0[...] + p1[...] + p2[...] + p3[...]).T
+    for g in range(PLANE):
+        up_ref[g * 4 : (g + 1) * 4, :] = total[g * 8 : g * 8 + 4]
+        down_ref[g * 4 : (g + 1) * 4, :] = total[g * 8 + 4 : (g + 1) * 8]
+    weighted = down_rows_ref[...].astype(F32) * down_ref[...]
+    grad_gain_ref[...] = jnp.sum(weighted, axis=0, keepdims=True) / gain_ref[...]
+
+
+def sums(parts, own_down, own_gain):
+    return pl.pallas_call(
+        sums_kernel,
+        out_shape=(shape((LATENT, OWN), F32), shape((LATENT, OWN), F32), shape((1, OWN), F32)),
+        in_specs=[VMEM] * (NZ + 2),
+        out_specs=[VMEM] * 3,
+        compiler_params=ROOM,
+        name="sums",
+    )(*parts, own_down, own_gain)
 
 
 def on_device(hidden_in, out_grad, gain, w_down, w_up, matching):
@@ -197,35 +266,32 @@
     place = (peer // 16) * NX + peer % NX
 
     z_at = z.reshape(1)
-    a_out = [lax.dynamic_slice_in_dim(tokens, ((z + k) % NZ) * WIDE, WIDE, 1) for k in range(NZ)]
-    a_parts = [along(part.reshape(PLANE, 8, WIDE), 1, k) for k, part in enumerate(a_out)]
-    spread_b = in_plane(tokens[:, HALF:].reshape(PLANE, 8, HALF))
+    out = [lax.dynamic_slice_in_dim(tokens, ((z + k) % NZ) * SPAN, SPAN, 1).reshape(PLANE, 8, SPAN) for k in range(NZ)]
+    a_parts = [along(out[k], 1, k) for k in (0, 1)]
+    spread_b = in_plane(jnp.concatenate(out[2:], axis=2))
 
     rows = lambda array: lax.dynamic_slice_in_dim(array, place * 4, 4, 0)
     match_wide = jnp.pad(matching.astype(F32), ((0, 0), (0, D - N_PEER)))
     packed = along(pack(jnp.concatenate([rows(up_rows), rows(down_rows)], axis=0), gain, match_wide), 1)
     match_before = packed[11, :N_PEER].astype(jnp.int32)
 
-    a_turned, *b_out = turn(z_at, a_parts, spread_b, packed)
-    b_parts = [along(part, 1, k) for k, part in enumerate(b_out)]
-    spread_a = in_plane(a_turned)
+    b_parts = [along(part, 1, k) for k, part in zip((2, 3), halves(spread_b, seen(a_parts[0])))]
+    spread_a = in_plane(beside(a_parts, packed))
     both = spread_a.reshape(ROWS, HALF + D)
     act_grad = act_grad_of(held_grad, both)
 
-    landed = in_cube(route(z_at, match_before, spread_a, b_parts))
-    act_out, part = adapter(landed, both, packed, held_grad, act_grad)
+    landed = in_cube(route(z_at, match_before, spread_a, b_parts, seen(*b_parts)))
+    active, part = adapter(landed, both, packed, held_grad, act_grad)
+    act_out = finish(landed, both, active)
 
     part = in_plane(part)
     plane_sum = jnp.sum(part.astype(F32), axis=0).reshape(NZ, OWN, 2 * LATENT)
-    total = 0.0
+    parts = []
     for k in range(NZ):
         chunk = lax.dynamic_index_in_dim(plane_sum, (z + k) % NZ, 0, keepdims=False)
-        total = total + along(chunk, -1, k)
-    total = total.T.reshape(PLANE, 2, 4, OWN)
-    grad_up = total[:, 0].reshape(LATENT, OWN)
-    grad_down = total[:, 1].reshape(LATENT, OWN)
+        parts.append(along(chunk, -1, k))
     own = lambda array: lax.dynamic_slice_in_dim(array, peer * OWN, OWN, 1)
-    grad_gain = jnp.sum(own(down_rows).astype(F32) * grad_down, axis=0, keepdims=True) / own(gain)
+    grad_down, grad_up, grad_gain = sums(parts, own(down_rows), own(gain))
     return act_out.reshape(1, ROWS, D), grad_down[None], grad_up[None], grad_gain
 
 

time: 201 us -> 188 us (0.935)
  starting transfers between devices: 104 us -> 74 us
  waiting for transfers between devices: 78.8 us -> 91.2 us
  local copies, waits for them, and re-layouts: 7.57 us -> 10.7 us
    ppermute x13 -> x9, starting transfers between devices: 73.1 us -> 49.2 us  [along(): return lax.ppermute(value, ('section', 'peer'), pairs)]
    all_to_all x3, waiting for transfers between devices: 17.5 us -> 36 us  [in_plane(): lax.all_to_all(value, 'peer', split_axis=0, concat_axis=0, tiled=True, ax...]
    all_to_all x1, starting transfers between devices: 12.4 us -> 6.39 us  [in_cube(): lax.all_to_all(value, 'peer', split_axis=0, concat_axis=0, tiled=True)]
    ppermute x13 -> x9, waiting for transfers between devices: 28.4 us -> 24.2 us  [along(): return lax.ppermute(value, ('section', 'peer'), pairs)]
    unnamed x14 -> x12, local copies, waits for them, and re-layouts: 3.44 us -> 6.74 us
    pallas_call x3 -> x8, Pallas kernels: 4.7 us -> 5.93 us  [the longest x1 1.96 us: adapter(): pl.pallas_call(adapter_kernel, out_shape=(shape((ROWS, 2 * LATENT)), shap...]
  transfers between devices with their start and end apart: 17 -> 13, of which waited for: 10 -> 11; matrix products, arithmetic and copies ran while one was open for 1% -> 2% of each run, Pallas kernels for 0% -> 2%
where the time goes in v4:
time: 188 us; the launch traced here: 187 us
  waiting for transfers between devices  91.2 us (49%)
  starting transfers between devices  74 us (39%)
  local copies, waits for them, and re-layouts  10.7 us (6%)
  Pallas kernels  6.52 us (3%)
  other arithmetic  3.09 us (2%)
    ppermute x9, starting transfers between devices, along(): return lax.ppermute(value, ('section', 'peer'), pairs)  49.2 us
    all_to_all x3, waiting for transfers between devices, in_plane(): lax.all_to_all(value, 'peer', split_axis=0, concat_axis=0, tiled=True, ax...  36 us
    all_to_all x1, waiting for transfers between devices, in_cube(): lax.all_to_all(value, 'peer', split_axis=0, concat_axis=0, tiled=True)  31 us
    ppermute x9, waiting for transfers between devices, along(): return lax.ppermute(value, ('section', 'peer'), pairs)  24.2 us
    all_to_all x3, starting transfers between devices, in_plane(): lax.all_to_all(value, 'peer', split_axis=0, concat_axis=0, tiled=True, ax...  18.4 us
    unnamed x12, local copies, waits for them, and re-layouts  6.74 us
    all_to_all x1, starting transfers between devices, in_cube(): lax.all_to_all(value, 'peer', split_axis=0, concat_axis=0, tiled=True)  6.39 us
  transfers between devices with their start and end apart: 13, of which 11 were waited for; matrix products, arithmetic and copies ran while one was open for 2% of the time, Pallas kernels for 2%

profile of v4, /device:TPU:1, one launch (start us, length us, event | category | flops | bytes accessed | tf_op | source)
XLA Modules:
  0.0 186.6 jit_solution(15731747860922175185)
XLA Ops:
  1.3 1.0 dynamic-slice_bitcast_fusion.8
  3.2 10.2 %collective-permute-start = (bf16[16,5120]{1,0:T(8,128)(2,1)S(1)}, bf16[16,5120]{1,0:T(8,128)(2,1)S(1)}, u32[]{:S(2)}, u32[]{:S(2)}) collective-permute-start(bf16[16,5120]{1,0:T(8,128)(2,1)S(1)} %pack.1), channel_id=1, source_target_pairs={{0,64},{1,65},{2,66},{3,67},{4,68},{5,69},{6,70},{7,71},{8,72},{9,... | collective-permute-start | bytes 491528 | tf_op jit(solution)/shard_map/ppermute | solution.py:37
  13.5 1.4 dynamic-slice_bitcast_fusion.1
  14.9 1.9 %collective-permute-start.1 = (bf16[16,8,1280]{2,1,0:T(8,128)(2,1)S(1)}, bf16[16,8,1280]{2,1,0:T(8,128)(2,1)S(1)}, u32[]{:S(2)}, u32[]{:S(2)}) collective-permute-start(bf16[16,8,1280]{2,1,0:T(8,128)(2,1)S(1)} %get-tuple-element.20), channel_id=1, source_target_pairs={{0,64},{1,65},{2,66},{3,67},{4,68},{5,69},{6,70},{7,71},{8,72},{9,... | collective-permute-start | bytes 983048 | tf_op jit(solution)/shard_map/ppermute | solution.py:37
  16.8 9.7 %collective-permute-start.2 = (bf16[16,8,1280]{2,1,0:T(8,128)(2,1)S(1)}, bf16[16,8,1280]{2,1,0:T(8,128)(2,1)S(1)}, u32[]{:S(2)}, u32[]{:S(2)}) collective-permute-start(bf16[16,8,1280]{2,1,0:T(8,128)(2,1)S(1)} %get-tuple-element.19), channel_id=1, source_target_pairs={{0,68},{1,69},{2,70},{3,71},{4,72},{5,73},{6,74},{7,75},{8,76},{9,... | collective-permute-start | bytes 983048 | tf_op jit(solution)/shard_map/ppermute | solution.py:37
  27.4 6.8 %all-to-all-start.1 = ((bf16[16,8,2560]{2,1,0:T(8,128)(2,1)}), bf16[16,8,2560]{2,1,0:T(8,128)(2,1)S(1)}, u32[]{:S(2)}, u32[]{:S(2)}) async-start(bf16[16,8,2560]{2,1,0:T(8,128)(2,1)} %pad_maximum_fusion), calls=%async_computation.1 | async-start | bytes 1310720 | tf_op jit(solution)/shard_map/all_to_all | solution.py:41
  34.8 9.0 %all-to-all-done.1.spread_ref = bf16[16,8,2560]{2,1,0:T(8,128)(2,1)S(1)} async-done(((bf16[16,8,2560]{2,1,0:T(8,128)(2,1)}), bf16[16,8,2560]{2,1,0:T(8,128)(2,1)S(1)}, u32[]{:S(2)}, u32[]{:S(2)}) %all-to-all-start.1) | async-done | bytes 655392 | tf_op jit(solution)/shard_map/all_to_all | solution.py:41
  44.7 7.1 %collective-permute-start.3 = (bf16[16,8,1280]{2,1,0:T(8,128)(2,1)}, bf16[16,8,1280]{2,1,0:T(8,128)(2,1)S(1)}, u32[]{:S(2)}, u32[]{:S(2)}) collective-permute-start(bf16[16,8,1280]{2,1,0:T(8,128)(2,1)} %get-tuple-element.11), channel_id=1, source_target_pairs={{0,72},{1,73},{2,74},{3,75},{4,76},{5,77},{6,78},{7,79},{8,64},{9,... | collective-permute-start | bytes 983048 | tf_op jit(solution)/shard_map/ppermute | solution.py:37
  51.8 4.4 %collective-permute-start.4 = (bf16[16,8,1280]{2,1,0:T(8,128)(2,1)}, bf16[16,8,1280]{2,1,0:T(8,128)(2,1)S(1)}, u32[]{:S(2)}, u32[]{:S(2)}) collective-permute-start(bf16[16,8,1280]{2,1,0:T(8,128)(2,1)} %get-tuple-element.12), channel_id=1, source_target_pairs={{0,76},{1,77},{2,78},{3,79},{4,64},{5,65},{6,66},{7,67},{8,68},{9,... | collective-permute-start | bytes 983048 | tf_op jit(solution)/shard_map/ppermute | solution.py:37
  56.2 6.3 %collective-permute-done.2.a1 = bf16[16,8,1280]{2,1,0:T(8,128)(2,1)S(1)} collective-permute-done((bf16[16,8,1280]{2,1,0:T(8,128)(2,1)S(1)}, bf16[16,8,1280]{2,1,0:T(8,128)(2,1)S(1)}, u32[]{:S(2)}, u32[]{:S(2)}) %collective-permute-start.2) | collective-permute-done | bytes 327712 | tf_op jit(solution)/shard_map/ppermute | solution.py:37
  62.6 1.3 copy-done
  63.9 7.3 %all-to-all-start = ((bf16[16,8,7680]{2,1,0:T(8,128)(2,1)}), bf16[16,8,7680]{2,1,0:T(8,128)(2,1)S(1)}, u32[]{:S(2)}, u32[]{:S(2)}) async-start(bf16[16,8,7680]{2,1,0:T(8,128)(2,1)} %copy-done), calls=%async_computation | async-start | bytes 3932160 | tf_op jit(solution)/shard_map/all_to_all | solution.py:41
  71.2 6.9 %collective-permute-done.3.refs_0_.b0 = bf16[16,8,1280]{2,1,0:T(8,128)(2,1)S(1)} collective-permute-done((bf16[16,8,1280]{2,1,0:T(8,128)(2,1)}, bf16[16,8,1280]{2,1,0:T(8,128)(2,1)S(1)}, u32[]{:S(2)}, u32[]{:S(2)}) %collective-permute-start.3) | collective-permute-done | bytes 327712 | tf_op jit(solution)/shard_map/ppermute | solution.py:37
  78.1 7.5 %collective-permute-done.4.refs_1_.b1 = bf16[16,8,1280]{2,1,0:T(8,128)(2,1)S(1)} collective-permute-done((bf16[16,8,1280]{2,1,0:T(8,128)(2,1)}, bf16[16,8,1280]{2,1,0:T(8,128)(2,1)S(1)}, u32[]{:S(2)}, u32[]{:S(2)}) %collective-permute-start.4) | collective-permute-done | bytes 327712 | tf_op jit(solution)/shard_map/ppermute | solution.py:37
  85.7 10.5 %all-to-all-done.a_ref = bf16[16,8,7680]{2,1,0:T(8,128)(2,1)S(1)} async-done(((bf16[16,8,7680]{2,1,0:T(8,128)(2,1)}), bf16[16,8,7680]{2,1,0:T(8,128)(2,1)S(1)}, u32[]{:S(2)}, u32[]{:S(2)}) %all-to-all-start) | async-done | bytes 1966112 | tf_op jit(solution)/shard_map/all_to_all | solution.py:41
  96.9 1.0 copy-done.3
  97.9 6.4 %all-to-all-start.2 = ((bf16[64,8,1280]{2,1,0:T(8,128)(2,1)}), bf16[64,8,1280]{2,1,0:T(8,128)(2,1)S(1)}, u32[]{:S(2)}, u32[]{:S(2)}) async-start(bf16[64,8,1280]{2,1,0:T(8,128)(2,1)} %copy-done.3), calls=%async_computation.2 | async-start | bytes 2621440 | tf_op jit(solution)/shard_map/all_to_all | solution.py:45
  104.3 1.3 copy-done.1
  106.1 31.0 %all-to-all-done.2.landed_ref = bf16[64,8,1280]{2,1,0:T(8,128)(2,1)S(1)} async-done(((bf16[64,8,1280]{2,1,0:T(8,128)(2,1)}), bf16[64,8,1280]{2,1,0:T(8,128)(2,1)S(1)}, u32[]{:S(2)}, u32[]{:S(2)}) %all-to-all-start.2) | async-done | bytes 1310752 | tf_op jit(solution)/shard_map/all_to_all | solution.py:45
  137.2 1.3 copy-done.2
  138.5 2.0 %adapter.1 = (bf16[128,128]{1,0:T(8,128)(2,1)S(1)}, bf16[16,320,128]{2,1,0:T(8,128)(2,1)S(1)}) custom-call(bf16[64,8,1280]{2,1,0:T(8,128)(2,1)S(1)} %all-to-all-done.2.landed_ref, bf16[128,7680]{1,0:T(8,128)(2,1)S(1)} %bitcast.35, bf16[16,5120]{1,0:T(8,128)(2,1)S(1)} %collective-permute-done.packed_ref, bf16[128,5120]{1,0:T(8,128)(2,1)S(1)} %bitcast.38, ...), custom_call_target="tpu_custom_call" | custom-call | tf_op jit(solution)/shard_map/adapter/pallas_call | solution.py:140
  140.4 1.0 copy-done.4
  141.5 4.4 %all-to-all-start.3 = ((bf16[16,320,128]{2,1,0:T(8,128)(2,1)}), bf16[16,320,128]{2,1,0:T(8,128)(2,1)}, u32[]{:S(2)}, u32[]{:S(2)}) async-start(bf16[16,320,128]{2,1,0:T(8,128)(2,1)} %copy-done.4), calls=%async_computation.3 | async-start | bytes 2621440 | tf_op jit(solution)/shard_map/all_to_all | solution.py:41
  146.8 16.5 %all-to-all-done.3 = bf16[16,320,128]{2,1,0:T(8,128)(2,1)} async-done(((bf16[16,320,128]{2,1,0:T(8,128)(2,1)}), bf16[16,320,128]{2,1,0:T(8,128)(2,1)}, u32[]{:S(2)}, u32[]{:S(2)}) %all-to-all-start.3) | async-done | bytes 1310752 | tf_op jit(solution)/shard_map/all_to_all | solution.py:41
  163.3 1.5 convert_reduce_fusion
  164.8 6.2 %collective-permute-start.5 = (f32[80,128]{1,0:T(8,128)S(1)}, f32[80,128]{1,0:T(8,128)S(1)}, u32[]{:S(2)}, u32[]{:S(2)}) collective-permute-start(f32[80,128]{1,0:T(8,128)S(1)} %get-tuple-element.25), channel_id=1, source_target_pairs={{0,448},{1,449},{2,450},{3,451},{4,452},{5,453},{6,454},{7,455},{8... | collective-permute-start | bytes 122888 | tf_op jit(solution)/shard_map/ppermute | solution.py:37
  171.0 1.9 %collective-permute-start.6 = (f32[80,128]{1,0:T(8,128)S(1)}, f32[80,128]{1,0:T(8,128)S(1)}, u32[]{:S(2)}, u32[]{:S(2)}) collective-permute-start(f32[80,128]{1,0:T(8,128)S(1)} %get-tuple-element.24), channel_id=1, source_target_pairs={{0,452},{1,453},{2,454},{3,455},{4,456},{5,457},{6,458},{7,459},{8... | collective-permute-start | bytes 122888 | tf_op jit(solution)/shard_map/ppermute | solution.py:37
  172.9 2.3 %collective-permute-start.7 = (f32[80,128]{1,0:T(8,128)S(1)}, f32[80,128]{1,0:T(8,128)S(1)}, u32[]{:S(2)}, u32[]{:S(2)}) collective-permute-start(f32[80,128]{1,0:T(8,128)S(1)} %get-tuple-element.23), channel_id=1, source_target_pairs={{0,456},{1,457},{2,458},{3,459},{4,460},{5,461},{6,462},{7,463},{8... | collective-permute-start | bytes 122888 | tf_op jit(solution)/shard_map/ppermute | solution.py:37
  175.3 5.5 %collective-permute-start.8 = (f32[80,128]{1,0:T(8,128)S(1)}, f32[80,128]{1,0:T(8,128)S(1)}, u32[]{:S(2)}, u32[]{:S(2)}) collective-permute-start(f32[80,128]{1,0:T(8,128)S(1)} %get-tuple-element.22), channel_id=1, source_target_pairs={{0,460},{1,461},{2,462},{3,463},{4,448},{5,449},{6,450},{7,451},{8... | collective-permute-start | bytes 122888 | tf_op jit(solution)/shard_map/ppermute | solution.py:37
  181.6 1.5 finish.1
  183.4 1.4 collective-permute-done.7.p2
  184.8 1.0 collective-permute-done.8.p3
  (27 shorter events, 8.0 us)
Async XLA Ops:
  2.4 0.7 copy-start.5
  3.2 53.0 %collective-permute-start = (bf16[16,5120]{1,0:T(8,128)(2,1)S(1)}, bf16[16,5120]{1,0:T(8,128)(2,1)S(1)}, u32[]{:S(2)}, u32[]{:S(2)}) collective-permute-start(bf16[16,5120]{1,0:T(8,128)(2,1)S(1)} %pack.1), channel_id=1, source_target_pairs={{0,64},{1,65},{2,66},{3,67},{4,68},{5,69},{6,70},{7,71},{8,72},{9,... | collective-permute-start | bytes 491528 | tf_op jit(solution)/shard_map/ppermute | solution.py:37
  14.9 19.9 %collective-permute-start.1 = (bf16[16,8,1280]{2,1,0:T(8,128)(2,1)S(1)}, bf16[16,8,1280]{2,1,0:T(8,128)(2,1)S(1)}, u32[]{:S(2)}, u32[]{:S(2)}) collective-permute-start(bf16[16,8,1280]{2,1,0:T(8,128)(2,1)S(1)} %get-tuple-element.20), channel_id=1, source_target_pairs={{0,64},{1,65},{2,66},{3,67},{4,68},{5,69},{6,70},{7,71},{8,72},{9,... | collective-permute-start | bytes 983048 | tf_op jit(solution)/shard_map/ppermute | solution.py:37
  16.8 45.7 %collective-permute-start.2 = (bf16[16,8,1280]{2,1,0:T(8,128)(2,1)S(1)}, bf16[16,8,1280]{2,1,0:T(8,128)(2,1)S(1)}, u32[]{:S(2)}, u32[]{:S(2)}) collective-permute-start(bf16[16,8,1280]{2,1,0:T(8,128)(2,1)S(1)} %get-tuple-element.19), channel_id=1, source_target_pairs={{0,68},{1,69},{2,70},{3,71},{4,72},{5,73},{6,74},{7,75},{8,76},{9,... | collective-permute-start | bytes 983048 | tf_op jit(solution)/shard_map/ppermute | solution.py:37
  27.4 16.5 %all-to-all-start.1 = ((bf16[16,8,2560]{2,1,0:T(8,128)(2,1)}), bf16[16,8,2560]{2,1,0:T(8,128)(2,1)S(1)}, u32[]{:S(2)}, u32[]{:S(2)}) async-start(bf16[16,8,2560]{2,1,0:T(8,128)(2,1)} %pad_maximum_fusion), calls=%async_computation.1 | async-start | bytes 1310720 | tf_op jit(solution)/shard_map/all_to_all | solution.py:41
  44.7 33.4 %collective-permute-start.3 = (bf16[16,8,1280]{2,1,0:T(8,128)(2,1)}, bf16[16,8,1280]{2,1,0:T(8,128)(2,1)S(1)}, u32[]{:S(2)}, u32[]{:S(2)}) collective-permute-start(bf16[16,8,1280]{2,1,0:T(8,128)(2,1)} %get-tuple-element.11), channel_id=1, source_target_pairs={{0,72},{1,73},{2,74},{3,75},{4,76},{5,77},{6,78},{7,79},{8,64},{9,... | collective-permute-start | bytes 983048 | tf_op jit(solution)/shard_map/ppermute | solution.py:37
  51.8 33.9 %collective-permute-start.4 = (bf16[16,8,1280]{2,1,0:T(8,128)(2,1)}, bf16[16,8,1280]{2,1,0:T(8,128)(2,1)S(1)}, u32[]{:S(2)}, u32[]{:S(2)}) collective-permute-start(bf16[16,8,1280]{2,1,0:T(8,128)(2,1)} %get-tuple-element.12), channel_id=1, source_target_pairs={{0,76},{1,77},{2,78},{3,79},{4,64},{5,65},{6,66},{7,67},{8,68},{9,... | collective-permute-start | bytes 983048 | tf_op jit(solution)/shard_map/ppermute | solution.py:37
  62.6 1.3 copy-start
  63.9 32.3 %all-to-all-start = ((bf16[16,8,7680]{2,1,0:T(8,128)(2,1)}), bf16[16,8,7680]{2,1,0:T(8,128)(2,1)S(1)}, u32[]{:S(2)}, u32[]{:S(2)}) async-start(bf16[16,8,7680]{2,1,0:T(8,128)(2,1)} %copy-done), calls=%async_computation | async-start | bytes 3932160 | tf_op jit(solution)/shard_map/all_to_all | solution.py:41
  96.9 1.1 copy-start.3
  97.9 39.2 %all-to-all-start.2 = ((bf16[64,8,1280]{2,1,0:T(8,128)(2,1)}), bf16[64,8,1280]{2,1,0:T(8,128)(2,1)S(1)}, u32[]{:S(2)}, u32[]{:S(2)}) async-start(bf16[64,8,1280]{2,1,0:T(8,128)(2,1)} %copy-done.3), calls=%async_computation.2 | async-start | bytes 2621440 | tf_op jit(solution)/shard_map/all_to_all | solution.py:45
  104.3 1.3 copy-start.1
  137.1 1.3 copy-start.2
  140.4 1.1 copy-start.4
  141.5 21.8 %all-to-all-start.3 = ((bf16[16,320,128]{2,1,0:T(8,128)(2,1)}), bf16[16,320,128]{2,1,0:T(8,128)(2,1)}, u32[]{:S(2)}, u32[]{:S(2)}) async-start(bf16[16,320,128]{2,1,0:T(8,128)(2,1)} %copy-done.4), calls=%async_computation.3 | async-start | bytes 2621440 | tf_op jit(solution)/shard_map/all_to_all | solution.py:41
  164.8 18.3 %collective-permute-start.5 = (f32[80,128]{1,0:T(8,128)S(1)}, f32[80,128]{1,0:T(8,128)S(1)}, u32[]{:S(2)}, u32[]{:S(2)}) collective-permute-start(f32[80,128]{1,0:T(8,128)S(1)} %get-tuple-element.25), channel_id=1, source_target_pairs={{0,448},{1,449},{2,450},{3,451},{4,452},{5,453},{6,454},{7,455},{8... | collective-permute-start | bytes 122888 | tf_op jit(solution)/shard_map/ppermute | solution.py:37
  171.0 12.4 %collective-permute-start.6 = (f32[80,128]{1,0:T(8,128)S(1)}, f32[80,128]{1,0:T(8,128)S(1)}, u32[]{:S(2)}, u32[]{:S(2)}) collective-permute-start(f32[80,128]{1,0:T(8,128)S(1)} %get-tuple-element.24), channel_id=1, source_target_pairs={{0,452},{1,453},{2,454},{3,455},{4,456},{5,457},{6,458},{7,459},{8... | collective-permute-start | bytes 122888 | tf_op jit(solution)/shard_map/ppermute | solution.py:37
  172.9 11.9 %collective-permute-start.7 = (f32[80,128]{1,0:T(8,128)S(1)}, f32[80,128]{1,0:T(8,128)S(1)}, u32[]{:S(2)}, u32[]{:S(2)}) collective-permute-start(f32[80,128]{1,0:T(8,128)S(1)} %get-tuple-element.23), channel_id=1, source_target_pairs={{0,456},{1,457},{2,458},{3,459},{4,460},{5,461},{6,462},{7,463},{8... | collective-permute-start | bytes 122888 | tf_op jit(solution)/shard_map/ppermute | solution.py:37
  175.3 10.6 %collective-permute-start.8 = (f32[80,128]{1,0:T(8,128)S(1)}, f32[80,128]{1,0:T(8,128)S(1)}, u32[]{:S(2)}, u32[]{:S(2)}) collective-permute-start(f32[80,128]{1,0:T(8,128)S(1)} %get-tuple-element.22), channel_id=1, source_target_pairs={{0,460},{1,461},{2,462},{3,463},{4,448},{5,449},{6,450},{7,451},{8... | collective-permute-start | bytes 122888 | tf_op jit(solution)/shard_map/ppermute | solution.py:37

commit v5 on v4

--- a/solution.py
+++ b/solution.py
@@ -16,8 +16,10 @@
 SPAN = D // NZ
 HALF = 2 * SPAN
 LEAD = 10**11
+PACKED = D + 256
 OWN = D // N_PEER
 PLANES = [[y * 16 + z * 4 + x for y in range(NY) for x in range(NX)] for z in range(NZ)]
+LINES = [[y * 16 + z * 4 + x for z in range(NZ)] for y in range(NY) for x in range(NX)]
 BF16, F32 = jnp.bfloat16, jnp.float32
 SMEM = pl.BlockSpec(memory_space=pltpu.SMEM)
 VMEM = pl.BlockSpec(memory_space=pltpu.VMEM)
@@ -53,41 +55,33 @@
     return 1.0 / (1.0 + jnp.exp(-value))
 
 
-def pack_kernel(rows_ref, gain_ref, match_ref, out_ref):
-    gain = gain_ref[...]
-    high = gain.astype(BF16).astype(F32)
-    middle = (gain - high).astype(BF16).astype(F32)
-    row = lax.broadcasted_iota(jnp.int32, (8, D), 0)
-    rest = jnp.zeros((8, D), F32)
-    for at, value in enumerate((high, middle, gain - high - middle, match_ref[...])):
-        rest = jnp.where(row == at, value, rest)
-    out_ref[...] = jnp.concatenate([rows_ref[...].astype(F32), rest], axis=0).astype(BF16)
-
-
-def pack(rows, gain_row, match_row):
+def pack_kernel(place_ref, rows_ref, gain_ref, match_ref, out_ref):
+    at = lax.broadcasted_iota(jnp.int32, (8, 128), 0)
+    terms = jnp.zeros((8, 128), F32)
+    for r in range(8):
+        unit = place_ref[0] * 8 + r
+        tile = gain_ref[pl.ds(jnp.minimum(unit // 3, D // 128 - 1), 1), :]
+        high = tile.astype(BF16).astype(F32)
+        middle = (tile - high).astype(BF16).astype(F32)
+        which = lax.rem(unit, 3)
+        term = jnp.where(which == 0, high, jnp.where(which == 1, middle, tile - high - middle))
+        terms = jnp.where(at == r, term, terms)
+    out_ref[:, :D] = rows_ref[...]
+    out_ref[:, D : D + 128] = terms.astype(BF16)
+    out_ref[:, D + 128 :] = jnp.zeros((8, 128), BF16)
+    match_row = match_ref[...].astype(F32)
+    out_ref[:, D + 128 : D + 128 + N_PEER] = jnp.broadcast_to(match_row, (8, N_PEER)).astype(BF16)
+
+
+def pack(place, rows, gain_tiles, match_row):
     return pl.pallas_call(
         pack_kernel,
-        out_shape=shape((16, D)),
-        in_specs=[VMEM] * 3,
+        out_shape=shape((8, PACKED)),
+        in_specs=[SMEM] + [VMEM] * 3,
         out_specs=VMEM,
         compiler_params=ROOM,
         name="pack",
-    )(rows, gain_row, match_row)
-
-
-def act_grad_kernel(grad_ref, both_ref, out_ref):
-    out_ref[...] = lax.dot_general(grad_ref[...], both_ref[:, HALF:], LAST, preferred_element_type=F32)
-
-
-def act_grad_of(held_grad, both):
-    return pl.pallas_call(
-        act_grad_kernel,
-        out_shape=shape((ROWS, 2 * LATENT), F32),
-        in_specs=[VMEM] * 2,
-        out_specs=VMEM,
-        compiler_params=ROOM,
-        name="act_grad",
-    )(held_grad, both)
+    )(place, rows, gain_tiles, match_row)
 
 
 def landed_rows(landed_ref, z, at):
@@ -102,7 +96,8 @@
     return both_ref[:, HALF + cols.start : HALF + cols.stop]
 
 
-def adapter_kernel(landed_ref, both_ref, packed_ref, grad_ref, act_grad_ref, active_ref, part_ref, normed_ref):
+def adapter_kernel(landed_ref, both_ref, grad_ref, active_ref, part_ref, normed_ref):
+    terms = both_ref[:, HALF + D : HALF + D + 128].astype(F32)
     squares = jnp.zeros((ROWS, 1), F32)
     for z, at, cols in CHUNKS:
         t = landed_rows(landed_ref, z, at)
@@ -110,7 +105,9 @@
     inv_rms = lax.rsqrt(squares / D + 1e-05)
     product = jnp.zeros((ROWS, 2 * LATENT), F32)
     for z, at, cols in CHUNKS:
-        gain = jnp.sum(packed_ref[:, cols].astype(F32)[8:11], axis=0, keepdims=True)
+        tiles = range(cols.start // 128, cols.stop // 128)
+        gain = [jnp.sum(terms[3 * t : 3 * t + 3], axis=0, keepdims=True) for t in tiles]
+        gain = jnp.concatenate(gain, axis=1)
         n = (landed_rows(landed_ref, z, at) * inv_rms * gain).astype(BF16)
         normed_ref[:, cols] = n
         product += lax.dot_general(n, weights(both_ref, cols), LAST, preferred_element_type=F32)
@@ -121,7 +118,10 @@
     active = pltpu.roll(preact * q, 2 * LATENT - 4, 1)
     active = jnp.where(is_up, active, 0.0).astype(BF16)
     active_ref[...] = active
-    act_grad = pltpu.roll(act_grad_ref[...], 4, 1)
+    act_grad = jnp.zeros((ROWS, 2 * LATENT), F32)
+    for z, at, cols in CHUNKS:
+        act_grad += lax.dot_general(grad_ref[:, cols], weights(both_ref, cols), LAST, preferred_element_type=F32)
+    act_grad = pltpu.roll(act_grad, 4, 1)
     pre_grad = jnp.where(is_up, 0.0, act_grad * q * (1.0 + preact * (1.0 - q)))
     down = pre_grad.T.astype(BF16)
     up = active.astype(F32).T.astype(BF16)
@@ -136,19 +136,20 @@
             part_ref[y * NX + x, z * OWN : (z + 1) * OWN, :] = part[i * OWN : (i + 1) * OWN]
 
 
-def adapter(landed, both, packed, held_grad, act_grad):
+def adapter(landed, both, held_grad):
     return pl.pallas_call(
         adapter_kernel,
         out_shape=(shape((ROWS, 2 * LATENT)), shape((PLANE, NZ * OWN, 2 * LATENT))),
-        in_specs=[VMEM] * 5,
+        in_specs=[VMEM] * 3,
         out_specs=[VMEM] * 2,
         scratch_shapes=[pltpu.VMEM((ROWS, D), BF16)],
         compiler_params=ROOM,
         name="adapter",
-    )(landed, both, packed, held_grad, act_grad)
-
-
-def finish_kernel(landed_ref, both_ref, active_ref, out_ref):
+    )(landed, both, held_grad)
+
+
+def finish_kernel(landed_ref, both_ref, active_ref, out_ref, zero_ref):
+    zero_ref[...] = jnp.zeros(zero_ref.shape, F32)
     for z, at, cols in CHUNKS:
         up = jnp.dot(active_ref[...], weights(both_ref, cols), preferred_element_type=F32)
         t = landed_rows(landed_ref, z, at) + up
@@ -159,9 +160,9 @@
 def finish(landed, both, active):
     return pl.pallas_call(
         finish_kernel,
-        out_shape=shape((PLANE, 8, D)),
+        out_shape=(shape((PLANE, 8, D)), shape((8, 2 * LATENT), F32)),
         in_specs=[VMEM] * 3,
-        out_specs=VMEM,
+        out_specs=[VMEM] * 2,
         compiler_params=ROOM,
         name="finish",
     )(landed, both, active)
@@ -170,15 +171,14 @@
 def beside_kernel(a0, a1, packed_ref, out_ref):
     out_ref[:, :, :SPAN] = a0[...]
     out_ref[:, :, SPAN:HALF] = a1[...]
-    rows = packed_ref[...].astype(F32)[:8].astype(BF16)
     for g in range(PLANE):
-        out_ref[g, :, HALF:] = rows
+        out_ref[g, :, HALF:] = packed_ref[...]
 
 
 def beside(a_parts, packed):
     return pl.pallas_call(
         beside_kernel,
-        out_shape=shape((PLANE, 8, HALF + D)),
+        out_shape=shape((PLANE, 8, HALF + PACKED)),
         in_specs=[VMEM] * 3,
         out_specs=VMEM,
         compiler_params=ROOM,
@@ -187,7 +187,7 @@
 
 
 def seen_kernel(*refs):
-    refs[-1][...] = sum(ref[0, :, :128].astype(F32) for ref in refs[:-1])
+    refs[-1][...] = sum(ref[(0,) * (len(ref.shape) - 2) + (slice(0, 8), slice(0, 128))].astype(F32) for ref in refs[:-1])
 
 
 def seen(*values):
@@ -238,8 +238,8 @@
     )(z_at, match_before, spread_a, *b_parts, after)
 
 
-def sums_kernel(p0, p1, p2, p3, down_rows_ref, gain_ref, down_ref, up_ref, grad_gain_ref):
-    total = (p0[...] + p1[...] + p2[...] + p3[...]).T
+def sums_kernel(p0, down_rows_ref, gain_ref, down_ref, up_ref, grad_gain_ref):
+    total = p0[...].T
     for g in range(PLANE):
         up_ref[g * 4 : (g + 1) * 4, :] = total[g * 8 : g * 8 + 4]
         down_ref[g * 4 : (g + 1) * 4, :] = total[g * 8 + 4 : (g + 1) * 8]
@@ -251,7 +251,7 @@
     return pl.pallas_call(
         sums_kernel,
         out_shape=(shape((LATENT, OWN), F32), shape((LATENT, OWN), F32), shape((1, OWN), F32)),
-        in_specs=[VMEM] * (NZ + 2),
+        in_specs=[VMEM] * 3,
         out_specs=[VMEM] * 3,
         compiler_params=ROOM,
         name="sums",
@@ -271,25 +271,22 @@
     spread_b = in_plane(jnp.concatenate(out[2:], axis=2))
 
     rows = lambda array: lax.dynamic_slice_in_dim(array, place * 4, 4, 0)
-    match_wide = jnp.pad(matching.astype(F32), ((0, 0), (0, D - N_PEER)))
-    packed = along(pack(jnp.concatenate([rows(up_rows), rows(down_rows)], axis=0), gain, match_wide), 1)
-    match_before = packed[11, :N_PEER].astype(jnp.int32)
-
-    b_parts = [along(part, 1, k) for k, part in zip((2, 3), halves(spread_b, seen(a_parts[0])))]
+    both_rows = jnp.concatenate([rows(up_rows), rows(down_rows)], axis=0)
+    packed = along(pack(place.reshape(1), both_rows, gain.reshape(D // 128, 128), matching), 1)
+    match_before = packed[0, D + 128 : D + 128 + N_PEER].astype(jnp.int32)
+
+    b_parts = [along(part, 1, k) for k, part in zip((2, 3), halves(spread_b, seen(a_parts[0], packed)))]
     spread_a = in_plane(beside(a_parts, packed))
-    both = spread_a.reshape(ROWS, HALF + D)
-    act_grad = act_grad_of(held_grad, both)
+    both = spread_a.reshape(ROWS, HALF + PACKED)
 
     landed = in_cube(route(z_at, match_before, spread_a, b_parts, seen(*b_parts)))
-    active, part = adapter(landed, both, packed, held_grad, act_grad)
-    act_out = finish(landed, both, active)
+    active, part = adapter(landed, both, held_grad)
+    act_out, zero = finish(landed, both, active)
 
     part = in_plane(part)
     plane_sum = jnp.sum(part.astype(F32), axis=0).reshape(NZ, OWN, 2 * LATENT)
-    parts = []
-    for k in range(NZ):
-        chunk = lax.dynamic_index_in_dim(plane_sum, (z + k) % NZ, 0, keepdims=False)
-        parts.append(along(chunk, -1, k))
+    lines = lax.all_to_all(plane_sum, "peer", split_axis=0, concat_axis=0, tiled=True, axis_index_groups=LINES)
+    parts = [along(jnp.sum(lines, axis=0) + zero[:1], -1)]
     own = lambda array: lax.dynamic_slice_in_dim(array, peer * OWN, OWN, 1)
     grad_down, grad_up, grad_gain = sums(parts, own(down_rows), own(gain))
     return act_out.reshape(1, ROWS, D), grad_down[None], grad_up[None], grad_gain

time: 188 us -> 180 us (0.957)
  blocking collectives: 0 us -> 56.2 us
  waiting for transfers between devices: 91.2 us -> 43.5 us
  starting transfers between devices: 74 us -> 64.6 us
  local copies, waits for them, and re-layouts: 10.7 us -> 5.99 us
    all_to_all x0 -> x2, blocking collectives: none -> 56.2 us  [the longest x1 37.7 us: in_cube(): lax.all_to_all(value, 'peer', split_axis=0, concat_axis=0, tiled=True)]
    all_to_all x1, waiting for transfers between devices: 31 us -> 2.47 us  [on_device(): lax.all_to_all(plane_sum, 'peer', split_axis=0, concat_axis=0, tiled=True...]
    all_to_all x3 -> x2, waiting for transfers between devices: 36 us -> 9.38 us  [in_plane(): lax.all_to_all(value, 'peer', split_axis=0, concat_axis=0, tiled=True, ax...]
    ppermute x9 -> x6, waiting for transfers between devices: 24.2 us -> 31.6 us  [along(): return lax.ppermute(value, ('section', 'peer'), pairs)]
    ppermute x9 -> x6, starting transfers between devices: 49.2 us -> 43.3 us  [along(): return lax.ppermute(value, ('section', 'peer'), pairs)]
    unnamed x12 -> x8, local copies, waits for them, and re-layouts: 6.74 us -> 1.32 us
    all_to_all x3 -> x2, starting transfers between devices: 18.4 us -> 16.1 us  [in_plane(): lax.all_to_all(value, 'peer', split_axis=0, concat_axis=0, tiled=True, ax...]
  transfers between devices with their start and end apart: 13 -> 9, of which waited for: 11 -> 7; matrix products, arithmetic and copies ran while one was open for 2% -> 2% of each run, Pallas kernels for 2% -> 1%
where the time goes in v5:
time: 180 us; the launch traced here: 179 us
  starting transfers between devices  64.6 us (36%)
  blocking collectives  56.2 us (31%)
  waiting for transfers between devices  43.5 us (24%)
  local copies, waits for them, and re-layouts  5.99 us (3%)
  Pallas kernels  5.56 us (3%)
  other arithmetic  1.81 us (1%)
    ppermute x6, starting transfers between devices, along(): return lax.ppermute(value, ('section', 'peer'), pairs)  43.3 us
    all_to_all x1, blocking collectives, in_cube(): lax.all_to_all(value, 'peer', split_axis=0, concat_axis=0, tiled=True)  37.7 us
    ppermute x6, waiting for transfers between devices, along(): return lax.ppermute(value, ('section', 'peer'), pairs)  31.6 us
    all_to_all x1, blocking collectives, in_plane(): lax.all_to_all(value, 'peer', split_axis=0, concat_axis=0, tiled=True, ax...  18.5 us
    all_to_all x2, starting transfers between devices, in_plane(): lax.all_to_all(value, 'peer', split_axis=0, concat_axis=0, tiled=True, ax...  16.1 us
    all_to_all x2, waiting for transfers between devices, in_plane(): lax.all_to_all(value, 'peer', split_axis=0, concat_axis=0, tiled=True, ax...  9.38 us
    all_to_all x1, starting transfers between devices, on_device(): lax.all_to_all(plane_sum, 'peer', split_axis=0, concat_axis=0, tiled=True...  5.27 us
  transfers between devices with their start and end apart: 9, of which 7 were waited for; matrix products, arithmetic and copies ran while one was open for 2% of the time, Pallas kernels for 1%

profile of v5, /device:TPU:1, one launch (start us, length us, event | category | flops | bytes accessed | tf_op | source)
XLA Modules:
  0.0 178.6 jit_solution(4188774662434713112)
XLA Ops:
  0.7 0.0 copy-start.2
  0.8 2.1 %dynamic-slice_bitcast_fusion.1 = (bf16[16,8,1280]{2,1,0:T(8,128)(2,1)S(1)}, bf16[16,8,1280]{2,1,0:T(8,128)(2,1)}, bf16[16,8,1280]{2,1,0:T(8,128)(2,1)S(1)}, bf16[16,8,1280]{2,1,0:T(8,128)(2,1)S(1)}) fusion(bf16[1,128,5120]{2,1,0:T(8,128)(2,1)} %param.6, s32[]{:T(128)S(6)} %select_n.64, s32[]{:T(128)S(6)} %select_n.62, s32[]{:T(128)S(6)} %select_n.60, ...), kind=kLoop, calls=%fused_computation.3 | loop fusion | bytes 2621456 | tf_op jit(solution)/shard_map/reshape | solution.py:269
  2.9 10.2 %collective-permute-start.1 = (bf16[16,8,1280]{2,1,0:T(8,128)(2,1)S(1)}, bf16[16,8,1280]{2,1,0:T(8,128)(2,1)S(1)}, u32[]{:S(2)}, u32[]{:S(2)}) collective-permute-start(bf16[16,8,1280]{2,1,0:T(8,128)(2,1)S(1)} %get-tuple-element.24), channel_id=1, source_target_pairs={{0,64},{1,65},{2,66},{3,67},{4,68},{5,69},{6,70},{7,71},{8,72},{9,... | collective-permute-start | bytes 983048 | tf_op jit(solution)/shard_map/ppermute | solution.py:39
  13.1 1.0 dynamic-slice_bitcast_fusion.4
  14.1 0.1 pack.1
  14.2 1.9 %collective-permute-start = (bf16[8,5376]{1,0:T(8,128)(2,1)S(1)}, bf16[8,5376]{1,0:T(8,128)(2,1)S(1)}, u32[]{:S(2)}, u32[]{:S(2)}) collective-permute-start(bf16[8,5376]{1,0:T(8,128)(2,1)S(1)} %pack.1), channel_id=1, source_target_pairs={{0,64},{1,65},{2,66},{3,67},{4,68},{5,69},{6,70},{7,71},{8,72},{9,... | collective-permute-start | bytes 258056 | tf_op jit(solution)/shard_map/ppermute | solution.py:39
  16.2 0.9 pad_maximum_fusion
  17.0 6.8 %all-to-all-start.1 = ((bf16[16,8,2560]{2,1,0:T(8,128)(2,1)}), bf16[16,8,2560]{2,1,0:T(8,128)(2,1)S(1)}, u32[]{:S(2)}, u32[]{:S(2)}) async-start(bf16[16,8,2560]{2,1,0:T(8,128)(2,1)} %pad_maximum_fusion), calls=%async_computation.1 | async-start | bytes 1310720 | tf_op jit(solution)/shard_map/all_to_all | solution.py:43
  23.8 9.9 %collective-permute-start.2 = (bf16[16,8,1280]{2,1,0:T(8,128)(2,1)}, bf16[16,8,1280]{2,1,0:T(8,128)(2,1)S(1)}, u32[]{:S(2)}, u32[]{:S(2)}) collective-permute-start(bf16[16,8,1280]{2,1,0:T(8,128)(2,1)} %get-tuple-element.23), channel_id=1, source_target_pairs={{0,68},{1,69},{2,70},{3,71},{4,72},{5,73},{6,74},{7,75},{8,76},{9,... | collective-permute-start | bytes 983048 | tf_op jit(solution)/shard_map/ppermute | solution.py:39
  33.8 2.0 %all-to-all-done.1.spread_ref = bf16[16,8,2560]{2,1,0:T(8,128)(2,1)S(1)} async-done(((bf16[16,8,2560]{2,1,0:T(8,128)(2,1)}), bf16[16,8,2560]{2,1,0:T(8,128)(2,1)S(1)}, u32[]{:S(2)}, u32[]{:S(2)}) %all-to-all-start.1) | async-done | bytes 655392 | tf_op jit(solution)/shard_map/all_to_all | solution.py:43
  35.8 11.5 %collective-permute-start.3 = (bf16[16,8,1280]{2,1,0:T(8,128)(2,1)S(1)}, bf16[16,8,1280]{2,1,0:T(8,128)(2,1)S(1)}, u32[]{:S(2)}, u32[]{:S(2)}) collective-permute-start(bf16[16,8,1280]{2,1,0:T(8,128)(2,1)S(1)} %get-tuple-element.13), channel_id=1, source_target_pairs={{0,72},{1,73},{2,74},{3,75},{4,76},{5,77},{6,78},{7,79},{8,64},{9,... | collective-permute-start | bytes 983048 | tf_op jit(solution)/shard_map/ppermute | solution.py:39
  47.4 2.4 %collective-permute-start.4 = (bf16[16,8,1280]{2,1,0:T(8,128)(2,1)S(1)}, bf16[16,8,1280]{2,1,0:T(8,128)(2,1)S(1)}, u32[]{:S(2)}, u32[]{:S(2)}) collective-permute-start(bf16[16,8,1280]{2,1,0:T(8,128)(2,1)S(1)} %get-tuple-element.14), channel_id=1, source_target_pairs={{0,76},{1,77},{2,78},{3,79},{4,64},{5,65},{6,66},{7,67},{8,68},{9,... | collective-permute-start | bytes 983048 | tf_op jit(solution)/shard_map/ppermute | solution.py:39
  49.7 9.4 %collective-permute-done.2.a1 = bf16[16,8,1280]{2,1,0:T(8,128)(2,1)S(1)} collective-permute-done((bf16[16,8,1280]{2,1,0:T(8,128)(2,1)}, bf16[16,8,1280]{2,1,0:T(8,128)(2,1)S(1)}, u32[]{:S(2)}, u32[]{:S(2)}) %collective-permute-start.2) | collective-permute-done | bytes 327712 | tf_op jit(solution)/shard_map/ppermute | solution.py:39
  59.2 0.1 beside.1
  59.3 1.3 copy-done
  60.6 9.3 %all-to-all-start = ((bf16[16,8,7936]{2,1,0:T(8,128)(2,1)}), bf16[16,8,7936]{2,1,0:T(8,128)(2,1)S(1)}, u32[]{:S(2)}, u32[]{:S(2)}) async-start(bf16[16,8,7936]{2,1,0:T(8,128)(2,1)} %copy-done), calls=%async_computation | async-start | bytes 4063232 | tf_op jit(solution)/shard_map/all_to_all | solution.py:43
  69.9 4.3 %collective-permute-done.3.refs_0_.b0 = bf16[16,8,1280]{2,1,0:T(8,128)(2,1)S(1)} collective-permute-done((bf16[16,8,1280]{2,1,0:T(8,128)(2,1)S(1)}, bf16[16,8,1280]{2,1,0:T(8,128)(2,1)S(1)}, u32[]{:S(2)}, u32[]{:S(2)}) %collective-permute-start.3) | collective-permute-done | bytes 327712 | tf_op jit(solution)/shard_map/ppermute | solution.py:39
  74.3 8.0 %collective-permute-done.4.refs_1_.b1 = bf16[16,8,1280]{2,1,0:T(8,128)(2,1)S(1)} collective-permute-done((bf16[16,8,1280]{2,1,0:T(8,128)(2,1)S(1)}, bf16[16,8,1280]{2,1,0:T(8,128)(2,1)S(1)}, u32[]{:S(2)}, u32[]{:S(2)}) %collective-permute-start.4) | collective-permute-done | bytes 327712 | tf_op jit(solution)/shard_map/ppermute | solution.py:39
  82.2 7.4 %all-to-all-done.a_ref = bf16[16,8,7936]{2,1,0:T(8,128)(2,1)S(1)} async-done(((bf16[16,8,7936]{2,1,0:T(8,128)(2,1)}), bf16[16,8,7936]{2,1,0:T(8,128)(2,1)S(1)}, u32[]{:S(2)}, u32[]{:S(2)}) %all-to-all-start) | async-done | bytes 2031648 | tf_op jit(solution)/shard_map/all_to_all | solution.py:43
  89.6 0.7 route.1
  90.3 37.7 %all_to_all.25.landed_ref = bf16[64,8,1280]{2,1,0:T(8,128)(2,1)S(1)} all-to-all(bf16[64,8,1280]{2,1,0:T(8,128)(2,1)S(1)} %route.1), channel_id=1, replica_groups=mesh['section'=8,'peer'=64] {'peer'}, dimensions={0} | all-to-all | bytes 2621440 | tf_op jit(solution)/shard_map/all_to_all | solution.py:47
  128.0 2.3 %adapter.1 = (bf16[128,128]{1,0:T(8,128)(2,1)S(1)}, bf16[16,320,128]{2,1,0:T(8,128)(2,1)S(1)}) custom-call(bf16[64,8,1280]{2,1,0:T(8,128)(2,1)S(1)} %all_to_all.25.landed_ref, bf16[128,7936]{1,0:T(8,128)(2,1)S(1)} %bitcast.30, bf16[128,5120]{1,0:T(8,128)(2,1)S(1)} %bitcast.32), custom_call_target="tpu_custom_call" | custom-call | tf_op jit(solution)/shard_map/adapter/pallas_call | solution.py:140
  130.3 18.5 %all_to_all.26 = bf16[16,320,128]{2,1,0:T(8,128)(2,1)S(1)} all-to-all(bf16[16,320,128]{2,1,0:T(8,128)(2,1)S(1)} %get-tuple-element.17), channel_id=1, replica_groups={{0,1,2,3,16,17,18,19,32,33,34,35,48,49,50,51},{4,5,6,7,20,21,22,23,36,3..., dimensions={0} | all-to-all | bytes 2621440 | tf_op jit(solution)/shard_map/all_to_all | solution.py:43
  148.9 0.9 convert_reduce_fusion
  149.7 5.3 %all-to-all-start.4 = ((f32[4,80,128]{2,1,0:T(8,128)}), f32[4,80,128]{2,1,0:T(8,128)S(1)}, u32[]{:S(2)}, u32[]{:S(2)}) async-start(f32[4,80,128]{2,1,0:T(8,128)} %bitcast.34), calls=%async_computation.4 | async-start | bytes 327680 | tf_op jit(solution)/shard_map/all_to_all | solution.py:288
  155.0 0.8 dynamic-slice_bitcast_fusion.6.down_rows_ref
  155.8 1.6 finish.1
  157.4 2.5 %all-to-all-done.4 = f32[4,80,128]{2,1,0:T(8,128)S(1)} async-done(((f32[4,80,128]{2,1,0:T(8,128)}), f32[4,80,128]{2,1,0:T(8,128)S(1)}, u32[]{:S(2)}, u32[]{:S(2)}) %all-to-all-start.4) | async-done | bytes 163872 | tf_op jit(solution)/shard_map/all_to_all | solution.py:288
  159.9 7.3 %collective-permute-start.5 = (f32[80,128]{1,0:T(8,128)S(1)}, f32[80,128]{1,0:T(8,128)S(1)}, u32[]{:S(2)}, u32[]{:S(2)}) collective-permute-start(f32[80,128]{1,0:T(8,128)S(1)} %broadcast_add_fusion), channel_id=1, source_target_pairs={{0,448},{1,449},{2,450},{3,451},{4,452},{5,453},{6,454},{7,455},{8... | collective-permute-start | bytes 122888 | tf_op jit(solution)/shard_map/ppermute | solution.py:39
  167.2 0.8 constant_dynamic-slice_fusion.gain_ref
  168.0 9.9 %collective-permute-done.5.p0 = f32[80,128]{1,0:T(8,128)S(1)} collective-permute-done((f32[80,128]{1,0:T(8,128)S(1)}, f32[80,128]{1,0:T(8,128)S(1)}, u32[]{:S(2)}, u32[]{:S(2)}) %collective-permute-start.5) | collective-permute-done | bytes 40992 | tf_op jit(solution)/shard_map/ppermute | solution.py:39
  177.9 0.7 sums.1
  (16 shorter events, 0.1 us)
Async XLA Ops:
  0.7 13.4 %copy-start.2 = (f32[1,5120]{1,0:T(1,128)S(1)}, f32[1,5120]{1,0:T(1,128)}, u32[]{:S(2)}) copy-start(f32[1,5120]{1,0:T(1,128)} %param.8) | copy-start | bytes 61444
  0.8 13.4 %copy-start.3 = (s32[1,64]{1,0:T(1,128)S(1)}, s32[1,64]{1,0:T(1,128)}, u32[]{:S(2)}) copy-start(s32[1,64]{1,0:T(1,128)} %match_ref.1) | copy-start | bytes 772
  2.9 30.9 %collective-permute-start.1 = (bf16[16,8,1280]{2,1,0:T(8,128)(2,1)S(1)}, bf16[16,8,1280]{2,1,0:T(8,128)(2,1)S(1)}, u32[]{:S(2)}, u32[]{:S(2)}) collective-permute-start(bf16[16,8,1280]{2,1,0:T(8,128)(2,1)S(1)} %get-tuple-element.24), channel_id=1, source_target_pairs={{0,64},{1,65},{2,66},{3,67},{4,68},{5,69},{6,70},{7,71},{8,72},{9,... | collective-permute-start | bytes 983048 | tf_op jit(solution)/shard_map/ppermute | solution.py:39
  14.2 19.5 %collective-permute-start = (bf16[8,5376]{1,0:T(8,128)(2,1)S(1)}, bf16[8,5376]{1,0:T(8,128)(2,1)S(1)}, u32[]{:S(2)}, u32[]{:S(2)}) collective-permute-start(bf16[8,5376]{1,0:T(8,128)(2,1)S(1)} %pack.1), channel_id=1, source_target_pairs={{0,64},{1,65},{2,66},{3,67},{4,68},{5,69},{6,70},{7,71},{8,72},{9,... | collective-permute-start | bytes 258056 | tf_op jit(solution)/shard_map/ppermute | solution.py:39
  17.0 18.7 %all-to-all-start.1 = ((bf16[16,8,2560]{2,1,0:T(8,128)(2,1)}), bf16[16,8,2560]{2,1,0:T(8,128)(2,1)S(1)}, u32[]{:S(2)}, u32[]{:S(2)}) async-start(bf16[16,8,2560]{2,1,0:T(8,128)(2,1)} %pad_maximum_fusion), calls=%async_computation.1 | async-start | bytes 1310720 | tf_op jit(solution)/shard_map/all_to_all | solution.py:43
  23.8 35.4 %collective-permute-start.2 = (bf16[16,8,1280]{2,1,0:T(8,128)(2,1)}, bf16[16,8,1280]{2,1,0:T(8,128)(2,1)S(1)}, u32[]{:S(2)}, u32[]{:S(2)}) collective-permute-start(bf16[16,8,1280]{2,1,0:T(8,128)(2,1)} %get-tuple-element.23), channel_id=1, source_target_pairs={{0,68},{1,69},{2,70},{3,71},{4,72},{5,73},{6,74},{7,75},{8,76},{9,... | collective-permute-start | bytes 983048 | tf_op jit(solution)/shard_map/ppermute | solution.py:39
  35.8 38.5 %collective-permute-start.3 = (bf16[16,8,1280]{2,1,0:T(8,128)(2,1)S(1)}, bf16[16,8,1280]{2,1,0:T(8,128)(2,1)S(1)}, u32[]{:S(2)}, u32[]{:S(2)}) collective-permute-start(bf16[16,8,1280]{2,1,0:T(8,128)(2,1)S(1)} %get-tuple-element.13), channel_id=1, source_target_pairs={{0,72},{1,73},{2,74},{3,75},{4,76},{5,77},{6,78},{7,79},{8,64},{9,... | collective-permute-start | bytes 983048 | tf_op jit(solution)/shard_map/ppermute | solution.py:39
  47.4 34.9 %collective-permute-start.4 = (bf16[16,8,1280]{2,1,0:T(8,128)(2,1)S(1)}, bf16[16,8,1280]{2,1,0:T(8,128)(2,1)S(1)}, u32[]{:S(2)}, u32[]{:S(2)}) collective-permute-start(bf16[16,8,1280]{2,1,0:T(8,128)(2,1)S(1)} %get-tuple-element.14), channel_id=1, source_target_pairs={{0,76},{1,77},{2,78},{3,79},{4,64},{5,65},{6,66},{7,67},{8,68},{9,... | collective-permute-start | bytes 983048 | tf_op jit(solution)/shard_map/ppermute | solution.py:39
  59.3 1.3 copy-start
  60.6 29.0 %all-to-all-start = ((bf16[16,8,7936]{2,1,0:T(8,128)(2,1)}), bf16[16,8,7936]{2,1,0:T(8,128)(2,1)S(1)}, u32[]{:S(2)}, u32[]{:S(2)}) async-start(bf16[16,8,7936]{2,1,0:T(8,128)(2,1)} %copy-done), calls=%async_computation | async-start | bytes 4063232 | tf_op jit(solution)/shard_map/all_to_all | solution.py:43
  90.3 37.7 %copy-start.1 = (bf16[1,128,5120]{2,1,0:T(8,128)(2,1)S(1)}, bf16[1,128,5120]{2,1,0:T(8,128)(2,1)}, u32[]{:S(2)}) copy-start(bf16[1,128,5120]{2,1,0:T(8,128)(2,1)} %param.7) | copy-start | bytes 3932164
  149.7 10.1 %all-to-all-start.4 = ((f32[4,80,128]{2,1,0:T(8,128)}), f32[4,80,128]{2,1,0:T(8,128)S(1)}, u32[]{:S(2)}, u32[]{:S(2)}) async-start(f32[4,80,128]{2,1,0:T(8,128)} %bitcast.34), calls=%async_computation.4 | async-start | bytes 327680 | tf_op jit(solution)/shard_map/all_to_all | solution.py:288
  159.9 18.0 %collective-permute-start.5 = (f32[80,128]{1,0:T(8,128)S(1)}, f32[80,128]{1,0:T(8,128)S(1)}, u32[]{:S(2)}, u32[]{:S(2)}) collective-permute-start(f32[80,128]{1,0:T(8,128)S(1)} %broadcast_add_fusion), channel_id=1, source_target_pairs={{0,448},{1,449},{2,450},{3,451},{4,452},{5,453},{6,454},{7,455},{8... | collective-permute-start | bytes 122888 | tf_op jit(solution)/shard_map/ppermute | solution.py:39

commit v6 on v5

--- a/solution.py
+++ b/solution.py
@@ -17,6 +17,7 @@
 HALF = 2 * SPAN
 LEAD = 10**11
 PACKED = D + 256
+FIRST, SECOND = (3, 0), (1, 2)
 OWN = D // N_PEER
 PLANES = [[y * 16 + z * 4 + x for y in range(NY) for x in range(NX)] for z in range(NZ)]
 LINES = [[y * 16 + z * 4 + x for z in range(NZ)] for y in range(NY) for x in range(NX)]
@@ -220,10 +221,10 @@
 
 def route_kernel(z_ref, before_ref, a_ref, b0, b1, after_ref, out_ref):
     z = z_ref[0]
-    for k in range(NZ):
+    for i, k in enumerate(FIRST + SECOND):
         plane = lax.rem(z + NZ - k, NZ) * NX
         for xy in range(PLANE):
-            piece = a_ref[xy, :, k * SPAN : (k + 1) * SPAN] if k < 2 else (b0, b1)[k - 2][xy]
+            piece = a_ref[xy, :, i * SPAN : (i + 1) * SPAN] if i < 2 else (b0, b1)[i - 2][xy]
             out_ref[before_ref[plane + (xy // NX) * 16 + xy % NX]] = piece
 
 
@@ -266,8 +267,8 @@
     place = (peer // 16) * NX + peer % NX
 
     z_at = z.reshape(1)
-    out = [lax.dynamic_slice_in_dim(tokens, ((z + k) % NZ) * SPAN, SPAN, 1).reshape(PLANE, 8, SPAN) for k in range(NZ)]
-    a_parts = [along(out[k], 1, k) for k in (0, 1)]
+    out = [lax.dynamic_slice_in_dim(tokens, ((z + k) % NZ) * SPAN, SPAN, 1).reshape(PLANE, 8, SPAN) for k in FIRST + SECOND]
+    a_parts = [along(out[i], 1, k) for i, k in enumerate(FIRST)]
     spread_b = in_plane(jnp.concatenate(out[2:], axis=2))
 
     rows = lambda array: lax.dynamic_slice_in_dim(array, place * 4, 4, 0)
@@ -275,7 +276,7 @@
     packed = along(pack(place.reshape(1), both_rows, gain.reshape(D // 128, 128), matching), 1)
     match_before = packed[0, D + 128 : D + 128 + N_PEER].astype(jnp.int32)
 
-    b_parts = [along(part, 1, k) for k, part in zip((2, 3), halves(spread_b, seen(a_parts[0], packed)))]
+    b_parts = [along(part, 1, k) for k, part in zip(SECOND, halves(spread_b, seen(a_parts[0], packed)))]
     spread_a = in_plane(beside(a_parts, packed))
     both = spread_a.reshape(ROWS, HALF + PACKED)
 

time: 180 us -> 178 us (0.989)
  starting transfers between devices: 64.6 us -> 55.9 us
  blocking collectives: 56.2 us -> 64.5 us
    all_to_all x1, blocking collectives: 37.7 us -> 45.2 us  [in_cube(): lax.all_to_all(value, 'peer', split_axis=0, concat_axis=0, tiled=True)]
    all_to_all x2, waiting for transfers between devices: 9.38 us -> 2.34 us  [in_plane(): lax.all_to_all(value, 'peer', split_axis=0, concat_axis=0, tiled=True, ax...]
    ppermute x6, waiting for transfers between devices: 31.6 us -> 37.8 us  [along(): return lax.ppermute(value, ('section', 'peer'), pairs)]
    all_to_all x2, starting transfers between devices: 16.1 us -> 10.5 us  [in_plane(): lax.all_to_all(value, 'peer', split_axis=0, concat_axis=0, tiled=True, ax...]
    ppermute x6, starting transfers between devices: 43.3 us -> 40.5 us  [along(): return lax.ppermute(value, ('section', 'peer'), pairs)]
  transfers between devices with their start and end apart: 9 -> 9, of which waited for: 7 -> 6; matrix products, arithmetic and copies ran while one was open for 2% -> 2% of each run, Pallas kernels for 1% -> 1%
where the time goes in v6:
time: 178 us; the launch traced here: 177 us
  blocking collectives  64.5 us (36%)
  starting transfers between devices  55.9 us (31%)
  waiting for transfers between devices  42.6 us (24%)
  local copies, waits for them, and re-layouts  5.99 us (3%)
  Pallas kernels  5.56 us (3%)
  other arithmetic  1.81 us (1%)
    all_to_all x1, blocking collectives, in_cube(): lax.all_to_all(value, 'peer', split_axis=0, concat_axis=0, tiled=True)  45.2 us
    ppermute x6, starting transfers between devices, along(): return lax.ppermute(value, ('section', 'peer'), pairs)  40.5 us
    ppermute x6, waiting for transfers between devices, along(): return lax.ppermute(value, ('section', 'peer'), pairs)  37.8 us
    all_to_all x1, blocking collectives, in_plane(): lax.all_to_all(value, 'peer', split_axis=0, concat_axis=0, tiled=True, ax...  19.2 us
    all_to_all x2, starting transfers between devices, in_plane(): lax.all_to_all(value, 'peer', split_axis=0, concat_axis=0, tiled=True, ax...  10.5 us
    all_to_all x1, starting transfers between devices, on_device(): lax.all_to_all(plane_sum, 'peer', split_axis=0, concat_axis=0, tiled=True...  4.99 us
  transfers between devices with their start and end apart: 9, of which 6 were waited for; matrix products, arithmetic and copies ran while one was open for 2% of the time, Pallas kernels for 1%

profile of v6, /device:TPU:1, one launch (start us, length us, event | category | flops | bytes accessed | tf_op | source)
XLA Modules:
  0.0 177.3 jit_solution(5949147863344914332)
XLA Ops:
  0.7 0.0 copy-start.2
  0.8 2.1 %dynamic-slice_bitcast_fusion.1 = (bf16[16,8,1280]{2,1,0:T(8,128)(2,1)S(1)}, bf16[16,8,1280]{2,1,0:T(8,128)(2,1)}, bf16[16,8,1280]{2,1,0:T(8,128)(2,1)S(1)}, bf16[16,8,1280]{2,1,0:T(8,128)(2,1)S(1)}) fusion(bf16[1,128,5120]{2,1,0:T(8,128)(2,1)} %param.6, s32[]{:T(128)S(6)} %select_n.64, s32[]{:T(128)S(6)} %select_n.62, s32[]{:T(128)S(6)} %select_n.60, ...), kind=kLoop, calls=%fused_computation.3 | loop fusion | bytes 2621456 | tf_op jit(solution)/shard_map/reshape | solution.py:270
  2.9 14.3 %collective-permute-start.1 = (bf16[16,8,1280]{2,1,0:T(8,128)(2,1)S(1)}, bf16[16,8,1280]{2,1,0:T(8,128)(2,1)S(1)}, u32[]{:S(2)}, u32[]{:S(2)}) collective-permute-start(bf16[16,8,1280]{2,1,0:T(8,128)(2,1)S(1)} %get-tuple-element.24), channel_id=1, source_target_pairs={{0,76},{1,77},{2,78},{3,79},{4,64},{5,65},{6,66},{7,67},{8,68},{9,... | collective-permute-start | bytes 983048 | tf_op jit(solution)/shard_map/ppermute | solution.py:40
  17.2 1.0 dynamic-slice_bitcast_fusion.4
  18.2 0.1 pack.1
  18.3 1.9 %collective-permute-start = (bf16[8,5376]{1,0:T(8,128)(2,1)S(1)}, bf16[8,5376]{1,0:T(8,128)(2,1)S(1)}, u32[]{:S(2)}, u32[]{:S(2)}) collective-permute-start(bf16[8,5376]{1,0:T(8,128)(2,1)S(1)} %pack.1), channel_id=1, source_target_pairs={{0,64},{1,65},{2,66},{3,67},{4,68},{5,69},{6,70},{7,71},{8,72},{9,... | collective-permute-start | bytes 258056 | tf_op jit(solution)/shard_map/ppermute | solution.py:40
  20.2 0.9 pad_maximum_fusion
  21.1 6.8 %all-to-all-start.1 = ((bf16[16,8,2560]{2,1,0:T(8,128)(2,1)}), bf16[16,8,2560]{2,1,0:T(8,128)(2,1)S(1)}, u32[]{:S(2)}, u32[]{:S(2)}) async-start(bf16[16,8,2560]{2,1,0:T(8,128)(2,1)} %pad_maximum_fusion), calls=%async_computation.1 | async-start | bytes 1310720 | tf_op jit(solution)/shard_map/all_to_all | solution.py:44
  27.9 6.8 %collective-permute-start.2 = (bf16[16,8,1280]{2,1,0:T(8,128)(2,1)}, bf16[16,8,1280]{2,1,0:T(8,128)(2,1)S(1)}, u32[]{:S(2)}, u32[]{:S(2)}) collective-permute-start(bf16[16,8,1280]{2,1,0:T(8,128)(2,1)} %get-tuple-element.23), channel_id=1, source_target_pairs={{0,64},{1,65},{2,66},{3,67},{4,68},{5,69},{6,70},{7,71},{8,72},{9,... | collective-permute-start | bytes 983048 | tf_op jit(solution)/shard_map/ppermute | solution.py:40
  34.6 3.0 %collective-permute-done.packed_ref.refs_1_ = bf16[8,5376]{1,0:T(8,128)(2,1)S(1)} collective-permute-done((bf16[8,5376]{1,0:T(8,128)(2,1)S(1)}, bf16[8,5376]{1,0:T(8,128)(2,1)S(1)}, u32[]{:S(2)}, u32[]{:S(2)}) %collective-permute-start) | collective-permute-done | bytes 86048 | tf_op jit(solution)/shard_map/ppermute | solution.py:40
  37.6 2.3 %all-to-all-done.1.spread_ref = bf16[16,8,2560]{2,1,0:T(8,128)(2,1)S(1)} async-done(((bf16[16,8,2560]{2,1,0:T(8,128)(2,1)}), bf16[16,8,2560]{2,1,0:T(8,128)(2,1)S(1)}, u32[]{:S(2)}, u32[]{:S(2)}) %all-to-all-start.1) | async-done | bytes 655392 | tf_op jit(solution)/shard_map/all_to_all | solution.py:44
  40.0 7.7 %collective-permute-start.3 = (bf16[16,8,1280]{2,1,0:T(8,128)(2,1)S(1)}, bf16[16,8,1280]{2,1,0:T(8,128)(2,1)S(1)}, u32[]{:S(2)}, u32[]{:S(2)}) collective-permute-start(bf16[16,8,1280]{2,1,0:T(8,128)(2,1)S(1)} %get-tuple-element.13), channel_id=1, source_target_pairs={{0,68},{1,69},{2,70},{3,71},{4,72},{5,73},{6,74},{7,75},{8,76},{9,... | collective-permute-start | bytes 983048 | tf_op jit(solution)/shard_map/ppermute | solution.py:40
  47.7 2.8 %collective-permute-start.4 = (bf16[16,8,1280]{2,1,0:T(8,128)(2,1)S(1)}, bf16[16,8,1280]{2,1,0:T(8,128)(2,1)S(1)}, u32[]{:S(2)}, u32[]{:S(2)}) collective-permute-start(bf16[16,8,1280]{2,1,0:T(8,128)(2,1)S(1)} %get-tuple-element.14), channel_id=1, source_target_pairs={{0,72},{1,73},{2,74},{3,75},{4,76},{5,77},{6,78},{7,79},{8,64},{9,... | collective-permute-start | bytes 983048 | tf_op jit(solution)/shard_map/ppermute | solution.py:40
  50.6 0.1 beside.1
  50.8 1.3 copy-done
  52.1 3.7 %all-to-all-start = ((bf16[16,8,7936]{2,1,0:T(8,128)(2,1)}), bf16[16,8,7936]{2,1,0:T(8,128)(2,1)S(1)}, u32[]{:S(2)}, u32[]{:S(2)}) async-start(bf16[16,8,7936]{2,1,0:T(8,128)(2,1)} %copy-done), calls=%async_computation | async-start | bytes 4063232 | tf_op jit(solution)/shard_map/all_to_all | solution.py:44
  55.8 16.6 %collective-permute-done.3.refs_0_.b0 = bf16[16,8,1280]{2,1,0:T(8,128)(2,1)S(1)} collective-permute-done((bf16[16,8,1280]{2,1,0:T(8,128)(2,1)S(1)}, bf16[16,8,1280]{2,1,0:T(8,128)(2,1)S(1)}, u32[]{:S(2)}, u32[]{:S(2)}) %collective-permute-start.3) | collective-permute-done | bytes 327712 | tf_op jit(solution)/shard_map/ppermute | solution.py:40
  72.4 10.4 %collective-permute-done.4.refs_1_.b1 = bf16[16,8,1280]{2,1,0:T(8,128)(2,1)S(1)} collective-permute-done((bf16[16,8,1280]{2,1,0:T(8,128)(2,1)S(1)}, bf16[16,8,1280]{2,1,0:T(8,128)(2,1)S(1)}, u32[]{:S(2)}, u32[]{:S(2)}) %collective-permute-start.4) | collective-permute-done | bytes 327712 | tf_op jit(solution)/shard_map/ppermute | solution.py:40
  82.8 0.7 route.1
  83.5 0.0 copy-start.1
  83.5 45.2 %all_to_all.25.landed_ref = bf16[64,8,1280]{2,1,0:T(8,128)(2,1)S(1)} all-to-all(bf16[64,8,1280]{2,1,0:T(8,128)(2,1)S(1)} %route.1), channel_id=1, replica_groups=mesh['section'=8,'peer'=64] {'peer'}, dimensions={0} | all-to-all | bytes 2621440 | tf_op jit(solution)/shard_map/all_to_all | solution.py:48
  128.7 2.3 %adapter.1 = (bf16[128,128]{1,0:T(8,128)(2,1)S(1)}, bf16[16,320,128]{2,1,0:T(8,128)(2,1)S(1)}) custom-call(bf16[64,8,1280]{2,1,0:T(8,128)(2,1)S(1)} %all_to_all.25.landed_ref, bf16[128,7936]{1,0:T(8,128)(2,1)S(1)} %bitcast.30, bf16[128,5120]{1,0:T(8,128)(2,1)S(1)} %bitcast.32), custom_call_target="tpu_custom_call" | custom-call | tf_op jit(solution)/shard_map/adapter/pallas_call | solution.py:141
  131.1 19.2 %all_to_all.26 = bf16[16,320,128]{2,1,0:T(8,128)(2,1)S(1)} all-to-all(bf16[16,320,128]{2,1,0:T(8,128)(2,1)S(1)} %get-tuple-element.17), channel_id=1, replica_groups={{0,1,2,3,16,17,18,19,32,33,34,35,48,49,50,51},{4,5,6,7,20,21,22,23,36,3..., dimensions={0} | all-to-all | bytes 2621440 | tf_op jit(solution)/shard_map/all_to_all | solution.py:44
  150.3 0.9 convert_reduce_fusion
  151.2 5.0 %all-to-all-start.4 = ((f32[4,80,128]{2,1,0:T(8,128)}), f32[4,80,128]{2,1,0:T(8,128)S(1)}, u32[]{:S(2)}, u32[]{:S(2)}) async-start(f32[4,80,128]{2,1,0:T(8,128)} %bitcast.34), calls=%async_computation.4 | async-start | bytes 327680 | tf_op jit(solution)/shard_map/all_to_all | solution.py:289
  156.2 0.8 dynamic-slice_bitcast_fusion.6.down_rows_ref
  157.0 1.6 finish.1
  158.6 2.5 %all-to-all-done.4 = f32[4,80,128]{2,1,0:T(8,128)S(1)} async-done(((f32[4,80,128]{2,1,0:T(8,128)}), f32[4,80,128]{2,1,0:T(8,128)S(1)}, u32[]{:S(2)}, u32[]{:S(2)}) %all-to-all-start.4) | async-done | bytes 163872 | tf_op jit(solution)/shard_map/all_to_all | solution.py:289
  161.1 6.9 %collective-permute-start.5 = (f32[80,128]{1,0:T(8,128)S(1)}, f32[80,128]{1,0:T(8,128)S(1)}, u32[]{:S(2)}, u32[]{:S(2)}) collective-permute-start(f32[80,128]{1,0:T(8,128)S(1)} %broadcast_add_fusion), channel_id=1, source_target_pairs={{0,448},{1,449},{2,450},{3,451},{4,452},{5,453},{6,454},{7,455},{8... | collective-permute-start | bytes 122888 | tf_op jit(solution)/shard_map/ppermute | solution.py:40
  168.0 0.8 constant_dynamic-slice_fusion.gain_ref
  168.8 7.8 %collective-permute-done.5.p0 = f32[80,128]{1,0:T(8,128)S(1)} collective-permute-done((f32[80,128]{1,0:T(8,128)S(1)}, f32[80,128]{1,0:T(8,128)S(1)}, u32[]{:S(2)}, u32[]{:S(2)}) %collective-permute-start.5) | collective-permute-done | bytes 40992 | tf_op jit(solution)/shard_map/ppermute | solution.py:40
  176.6 0.7 sums.1
  (16 shorter events, 0.1 us)
Async XLA Ops:
  0.7 17.4 %copy-start.2 = (f32[1,5120]{1,0:T(1,128)S(1)}, f32[1,5120]{1,0:T(1,128)}, u32[]{:S(2)}) copy-start(f32[1,5120]{1,0:T(1,128)} %param.8) | copy-start | bytes 61444
  0.8 17.4 %copy-start.3 = (s32[1,64]{1,0:T(1,128)S(1)}, s32[1,64]{1,0:T(1,128)}, u32[]{:S(2)}) copy-start(s32[1,64]{1,0:T(1,128)} %match_ref.1) | copy-start | bytes 772
  2.9 34.8 %collective-permute-start.1 = (bf16[16,8,1280]{2,1,0:T(8,128)(2,1)S(1)}, bf16[16,8,1280]{2,1,0:T(8,128)(2,1)S(1)}, u32[]{:S(2)}, u32[]{:S(2)}) collective-permute-start(bf16[16,8,1280]{2,1,0:T(8,128)(2,1)S(1)} %get-tuple-element.24), channel_id=1, source_target_pairs={{0,76},{1,77},{2,78},{3,79},{4,64},{5,65},{6,66},{7,67},{8,68},{9,... | collective-permute-start | bytes 983048 | tf_op jit(solution)/shard_map/ppermute | solution.py:40
  18.3 19.3 %collective-permute-start = (bf16[8,5376]{1,0:T(8,128)(2,1)S(1)}, bf16[8,5376]{1,0:T(8,128)(2,1)S(1)}, u32[]{:S(2)}, u32[]{:S(2)}) collective-permute-start(bf16[8,5376]{1,0:T(8,128)(2,1)S(1)} %pack.1), channel_id=1, source_target_pairs={{0,64},{1,65},{2,66},{3,67},{4,68},{5,69},{6,70},{7,71},{8,72},{9,... | collective-permute-start | bytes 258056 | tf_op jit(solution)/shard_map/ppermute | solution.py:40
  21.1 18.9 %all-to-all-start.1 = ((bf16[16,8,2560]{2,1,0:T(8,128)(2,1)}), bf16[16,8,2560]{2,1,0:T(8,128)(2,1)S(1)}, u32[]{:S(2)}, u32[]{:S(2)}) async-start(bf16[16,8,2560]{2,1,0:T(8,128)(2,1)} %pad_maximum_fusion), calls=%async_computation.1 | async-start | bytes 1310720 | tf_op jit(solution)/shard_map/all_to_all | solution.py:44
  27.9 22.8 %collective-permute-start.2 = (bf16[16,8,1280]{2,1,0:T(8,128)(2,1)}, bf16[16,8,1280]{2,1,0:T(8,128)(2,1)S(1)}, u32[]{:S(2)}, u32[]{:S(2)}) collective-permute-start(bf16[16,8,1280]{2,1,0:T(8,128)(2,1)} %get-tuple-element.23), channel_id=1, source_target_pairs={{0,64},{1,65},{2,66},{3,67},{4,68},{5,69},{6,70},{7,71},{8,72},{9,... | collective-permute-start | bytes 983048 | tf_op jit(solution)/shard_map/ppermute | solution.py:40
  40.0 32.4 %collective-permute-start.3 = (bf16[16,8,1280]{2,1,0:T(8,128)(2,1)S(1)}, bf16[16,8,1280]{2,1,0:T(8,128)(2,1)S(1)}, u32[]{:S(2)}, u32[]{:S(2)}) collective-permute-start(bf16[16,8,1280]{2,1,0:T(8,128)(2,1)S(1)} %get-tuple-element.13), channel_id=1, source_target_pairs={{0,68},{1,69},{2,70},{3,71},{4,72},{5,73},{6,74},{7,75},{8,76},{9,... | collective-permute-start | bytes 983048 | tf_op jit(solution)/shard_map/ppermute | solution.py:40
  47.7 35.1 %collective-permute-start.4 = (bf16[16,8,1280]{2,1,0:T(8,128)(2,1)S(1)}, bf16[16,8,1280]{2,1,0:T(8,128)(2,1)S(1)}, u32[]{:S(2)}, u32[]{:S(2)}) collective-permute-start(bf16[16,8,1280]{2,1,0:T(8,128)(2,1)S(1)} %get-tuple-element.14), channel_id=1, source_target_pairs={{0,72},{1,73},{2,74},{3,75},{4,76},{5,77},{6,78},{7,79},{8,64},{9,... | collective-permute-start | bytes 983048 | tf_op jit(solution)/shard_map/ppermute | solution.py:40
  50.8 1.3 copy-start
  52.1 30.7 %all-to-all-start = ((bf16[16,8,7936]{2,1,0:T(8,128)(2,1)}), bf16[16,8,7936]{2,1,0:T(8,128)(2,1)S(1)}, u32[]{:S(2)}, u32[]{:S(2)}) async-start(bf16[16,8,7936]{2,1,0:T(8,128)(2,1)} %copy-done), calls=%async_computation | async-start | bytes 4063232 | tf_op jit(solution)/shard_map/all_to_all | solution.py:44
  83.5 45.3 %copy-start.1 = (bf16[1,128,5120]{2,1,0:T(8,128)(2,1)S(1)}, bf16[1,128,5120]{2,1,0:T(8,128)(2,1)}, u32[]{:S(2)}) copy-start(bf16[1,128,5120]{2,1,0:T(8,128)(2,1)} %param.7) | copy-start | bytes 3932164
  151.2 9.8 %all-to-all-start.4 = ((f32[4,80,128]{2,1,0:T(8,128)}), f32[4,80,128]{2,1,0:T(8,128)S(1)}, u32[]{:S(2)}, u32[]{:S(2)}) async-start(f32[4,80,128]{2,1,0:T(8,128)} %bitcast.34), calls=%async_computation.4 | async-start | bytes 327680 | tf_op jit(solution)/shard_map/all_to_all | solution.py:289
  161.1 15.5 %collective-permute-start.5 = (f32[80,128]{1,0:T(8,128)S(1)}, f32[80,128]{1,0:T(8,128)S(1)}, u32[]{:S(2)}, u32[]{:S(2)}) collective-permute-start(f32[80,128]{1,0:T(8,128)S(1)} %broadcast_add_fusion), channel_id=1, source_target_pairs={{0,448},{1,449},{2,450},{3,451},{4,452},{5,453},{6,454},{7,455},{8... | collective-permute-start | bytes 122888 | tf_op jit(solution)/shard_map/ppermute | solution.py:40
